TPU v7x, 32 devices: a whole 2x2x4 slice. The times are simulated.
32 devices in a mesh: dp: 16 (over z, y, x), blk: 2 (over core).
Axes of the slice: x: 2, y: 2, z: 4, core: 2. Of those that a mesh axis runs over, the one named last changes fastest.
Arguments:
- patches: bfloat16 [24576, 768], P(('dp', 'blk')), may hold values from -6 to 6
- visible: int32 [24576], P(('dp', 'blk')), may hold values 0 or 1
- padding: int32 [24576], P(('dp', 'blk')), may hold values from 0 to 1, as said below
- field_ids: int32 [24576], P(('dp', 'blk')), may hold values from 0 to 1, as said below
- enc_gain_a: bfloat16 [768], replicated, may hold values from 0.25 to 1.75
- enc_shift_a: bfloat16 [768], replicated, may hold values from -1.5 to 1.5
- enc_qkv: bfloat16 [768, 2304], replicated, may hold values from -0.21875 to 0.21875
- enc_out: bfloat16 [768, 768], replicated, may hold values from -0.875 to 0.875
- enc_out_bias: bfloat16 [768], replicated, may hold values from -1.5 to 1.5
- enc_gain_b: bfloat16 [768], replicated, may hold values from 0.25 to 1.75
- enc_shift_b: bfloat16 [768], replicated, may hold values from -1.5 to 1.5
- enc_up: bfloat16 [768, 3072], replicated, may hold values from -0.21875 to 0.21875
- enc_up_bias: bfloat16 [3072], replicated, may hold values from -1.5 to 1.5
- enc_down: bfloat16 [3072, 768], replicated, may hold values from -0.109375 to 0.109375
- enc_down_bias: bfloat16 [768], replicated, may hold values from -1.5 to 1.5
- embed_map: bfloat16 [768, 512], replicated, may hold values from -0.21875 to 0.21875
- embed_bias: bfloat16 [512], replicated, may hold values from -1.5 to 1.5
- mask_token: bfloat16 [512], replicated, may hold values from -4 to 4
- dec_gain_a: bfloat16 [512], replicated, may hold values from 0.25 to 1.75
- dec_shift_a: bfloat16 [512], replicated, may hold values from -1.5 to 1.5
- dec_qkv: bfloat16 [512, 1536], replicated, may hold values from -0.25 to 0.25
- dec_out: bfloat16 [512, 512], replicated, may hold values from -1.5 to 1.5
- dec_out_bias: bfloat16 [512], replicated, may hold values from -1.5 to 1.5
- dec_gain_b: bfloat16 [512], replicated, may hold values from 0.25 to 1.75
- dec_shift_b: bfloat16 [512], replicated, may hold values from -1.5 to 1.5
- dec_up: bfloat16 [512, 2048], replicated, may hold values from -0.25 to 0.25
- dec_up_bias: bfloat16 [2048], replicated, may hold values from -1.5 to 1.5
- dec_down: bfloat16 [2048, 512], replicated, may hold values from -0.125 to 0.125
- dec_down_bias: bfloat16 [512], replicated, may hold values from -1.5 to 1.5
- cotangent: bfloat16 [24576, 512], P(('dp', 'blk')), may hold values from -6 to 6
Outputs:
- decoded: bfloat16 [24576, 512], P(('dp', 'blk'))
- patches_grad: bfloat16 [24576, 768], P(('dp', 'blk'))
- grad_enc_gain_a: float32 [768], replicated
- grad_enc_shift_a: float32 [768], replicated
- grad_enc_qkv: float32 [768, 2304], replicated
- grad_enc_out: float32 [768, 768], replicated
- grad_enc_out_bias: float32 [768], replicated
- grad_enc_gain_b: float32 [768], replicated
- grad_enc_shift_b: float32 [768], replicated
- grad_enc_up: float32 [768, 3072], replicated
- grad_enc_up_bias: float32 [3072], replicated
- grad_enc_down: float32 [3072, 768], replicated
- grad_enc_down_bias: float32 [768], replicated
- grad_embed_map: float32 [768, 512], replicated
- grad_embed_bias: float32 [512], replicated
- grad_mask_token: float32 [512], replicated
- grad_dec_gain_a: float32 [512], replicated
- grad_dec_shift_a: float32 [512], replicated
- grad_dec_qkv: float32 [512, 1536], replicated
- grad_dec_out: float32 [512, 512], replicated
- grad_dec_out_bias: float32 [512], replicated
- grad_dec_gain_b: float32 [512], replicated
- grad_dec_shift_b: float32 [512], replicated
- grad_dec_up: float32 [512, 2048], replicated
- grad_dec_up_bias: float32 [2048], replicated
- grad_dec_down: float32 [2048, 512], replicated
- grad_dec_down_bias: float32 [512], replicated
Inputs may be any that keep to these rules, and one draw needn't show every extreme that they name: In each group of 1536 consecutive rows the padding rows, if any, form a trailing run of at most 383 rows; some group has exactly that many. `field_ids`: in each group of 1536 consecutive rows field 0 is a leading run shorter than half the group and field 1 is all the rest.
All inputs are finite; a program needn't handle non-finite values. No bound on the sum of `visible` on one device may be relied on, other than what follows from the above.
Results may differ from a plain program's by a relative error of at most 0.019.
Values may be sent and summed in bfloat16 or wider, within the bound.
No kernel may reach another device: no remote copies, remote signals or barrier semaphores. Data moves between devices by JAX's collectives and lax.ppermute only.
A program may use at most 320 MiB of HBM per device.

v0:
```python
import math

import jax
import jax.numpy as jnp
from jax import lax
from jax.experimental import pallas as pl
from jax.experimental.pallas import tpu as pltpu
from jax.sharding import PartitionSpec as P

HE = 12
HD = 16
TILE = 256
VMEM_LIMIT = 60 * 1024 * 1024
DEC_BITS = (1, 2, 0, 3)
ENC_BITS = ((2, 1, 0, 3), (1, 2, 0, 3), (0, 1, 2, 3))
STEPS = "dcadbdacbdacdbacbdadcabcbacbcacbacb"
SHORT = 512
WEIGHT_LIMIT = 40 * 1024 * 1024
SMALL_LIMIT = 24 * 1024 * 1024
FLOPS_PER_MICRO, BYTES_PER_MICRO = 1.15e9, 3.6e6


epsilon = 1e-06


def matmul(left_side, right_side):
    return jnp.dot(left_side, right_side, preferred_element_type=jnp.float32)


def matmul_tn(left_side, right_side):
    return lax.dot_general(
        left_side, right_side, (((0,), (0,)), ((), ())), preferred_element_type=jnp.float32
    )


def matmul_nt(left_side, right_side):
    return lax.dot_general(
        left_side, right_side, (((1,), (1,)), ((), ())), preferred_element_type=jnp.float32
    )


def bits_of(count):
    return count.bit_length() - 1


def across(value, axis, bit):
    count = lax.axis_size(axis)
    return lax.ppermute(value, axis, [(i, i ^ (1 << bit)) for i in range(count)])


def cost(micros):
    return pl.CostEstimate(
        flops=int(micros * FLOPS_PER_MICRO), bytes_accessed=int(micros * BYTES_PER_MICRO), transcendentals=0
    )


TOKEN = jax.ShapeDtypeStruct((8, 128), jnp.float32)


class Order:
    def __init__(self):
        self.token, self.smalls = None, 0

    def run(self, kernel, name, scalars, in_specs, operands, out_specs, out_shape, scratch=(), micros=1.0, steps=1, limit=VMEM_LIMIT):
        count = len(in_specs)
        if self.token is not None:
            in_specs = [*in_specs, pl.BlockSpec(memory_space=pl.ANY)]
            operands = [*operands, self.token]
        more = len(in_specs) - count

        outs = len(out_specs)

        def body(meta, *refs):
            rest = refs[count + more :]
            kernel(meta, *refs[:count], *rest[:outs], *rest[outs + 1 :])

        out_specs = [*out_specs, pl.BlockSpec(memory_space=pl.ANY)]
        results = pl.pallas_call(
            body,
            out_shape=[*out_shape, TOKEN],
            grid_spec=pltpu.PrefetchScalarGridSpec(
                num_scalar_prefetch=1, grid=(steps,), in_specs=in_specs, out_specs=out_specs, scratch_shapes=list(scratch)
            ),
            compiler_params=pltpu.CompilerParams(vmem_limit_bytes=limit),
            cost_estimate=cost(micros),
            name=name,
        )(scalars, *operands)
        self.token = results[-1]
        return results[:-1]

    def run_small(self, kernel, name, operands, out_shape, scalars=None, out_specs=None, scratch=()):
        micros = 40.0 if self.smalls < 8 else 4.0
        self.smalls += 1
        count, outs = len(operands), len(out_shape)
        in_specs = [pl.BlockSpec(memory_space=pltpu.VMEM)] * count
        first = []
        if scalars is not None:
            in_specs, first = [pl.BlockSpec(memory_space=pltpu.SMEM), *in_specs], [scalars]
        if self.token is not None:
            in_specs = [*in_specs, pl.BlockSpec(memory_space=pl.ANY)]
            operands = [*operands, self.token]
        used = count + len(first)

        def body(*refs):
            rest = refs[len(in_specs) :]
            kernel(*refs[:used], *rest[:outs], *rest[outs + 1 :])

        out_specs = out_specs or [pl.BlockSpec(memory_space=pltpu.VMEM)] * outs
        results = pl.pallas_call(
            body,
            out_shape=[*out_shape, TOKEN],
            in_specs=in_specs,
            out_specs=[*out_specs, pl.BlockSpec(memory_space=pl.ANY)],
            scratch_shapes=list(scratch),
            compiler_params=pltpu.CompilerParams(vmem_limit_bytes=SMALL_LIMIT),
            cost_estimate=cost(micros),
            name=name,
        )(*first, *operands)
        self.token = results[-1]
        return results[:-1]


class Entry:
    def __init__(self, kind, lhs, rhs, r, n, width, shape, counted):
        self.kind, self.lhs, self.rhs, self.r, self.n = kind, lhs, rhs, r, n
        self.width, self.shape, self.counted = width, shape, counted


class Bundle:
    def __init__(self, order, bits, spots, tiles, entries, short=()):
        self.order, self.run, self.entries = order, order.run, entries
        self.shards = min(16, lax.axis_size("dp"))
        self.bits = [bit for bit in bits if bit < bits_of(self.shards)]
        self.spots, self.tiles = spots, tiles
        self.width = max(entry.width for entry in entries)
        self.firsts, self.bases, first, base = [], [], 0, 0
        for entry in entries:
            self.firsts.append(first)
            self.bases.append(base)
            first += entry.n
            base += entry.n * entry.r
        self.short, self.short_base = list(short), base
        self.steps, self.rows = first, base + (16 if self.short else 0)

    def block(self, index_map):
        return pl.BlockSpec((1, self.rows, self.width), index_map)

    def shaped(self, count):
        return jax.ShapeDtypeStruct((count, self.rows, self.width), jnp.bfloat16)

    def size(self, count):
        return 2 * count * self.rows * self.width

    def spot_of(self, index):
        spot = jnp.int32(0)
        for at, bit in enumerate(self.bits):
            spot = spot | ((lax.shift_right_logical(index, bit) & 1) << (len(self.bits) - 1 - at))
        return spot

    def weigh(self):
        entries, shards, width = self.entries, self.shards, self.width
        token_rows = entries[0].lhs.shape[0]
        tallest = max(shards * entry.r for entry in entries)

        def unit_work(entry, offset, unit, refs, kept_ref, sent_ref, scratch, meta):
            r, n, height, span = entry.r, entry.n, shards * entry.r, entry.width
            turned, total, lhs_tile, rhs_tile, sems = scratch
            spot, half, live = meta[0], meta[1], meta[2]
            count = TILE if entry.counted else token_rows

            def block(ref):
                return ref[0] if entry.counted else ref[...]

            def put(out_ref, value):
                value = value.astype(BF16)
                if entry.kind == "wide":
                    at = pl.ds(pl.multiple_of(offset + unit * r, 16), r)
                    for shard in range(shards):
                        target = self.spot_of(lax.bitwise_xor(jnp.int32(shard), spot))
                        out_ref[target, at, :span] = value[shard * r : (shard + 1) * r]
                        if span < width:
                            out_ref[target, at, span:] = jnp.zeros((r, width - span), BF16)
                else:
                    each, tall = shards // n, n * r
                    for inner in range(each):
                        target = self.spot_of(lax.bitwise_xor(unit * each + inner, spot))
                        out_ref[target, offset : offset + tall, :span] = value[inner * tall : (inner + 1) * tall]

            def turn():
                turned[:height, :count] = block(refs[0]).T

            if entry.kind == "wide":
                pl.when(unit == 0)(turn)
            else:
                turn()

            def product(rhs_ref):
                return matmul(turned[:height, :count], block(rhs_ref))

            def add_rest(flip):
                lhs_at = 0 if entry.kind == "wide" else unit * height
                rhs_at = (half ^ flip) * span if entry.kind == "tall" else ((half ^ flip) * n + unit) * span

                def add(tile, carry):
                    copies = [
                        pltpu.make_async_copy(
                            source.at[tile, :, pl.ds(pl.multiple_of(jnp.int32(at), LANES), size)], target.at[:, :size], sems.at[index]
                        )
                        for index, (source, target, at, size) in enumerate(
                            ((refs[3], lhs_tile, lhs_at, height), (refs[4], rhs_tile, rhs_at, span))
                        )
                    ]
                    for copy in copies:
                        copy.start()
                    for copy in copies:
                        copy.wait()
                    total[:height, :span] += matmul_tn(lhs_tile[:, :height], rhs_tile[:, :span])
                    return carry

                lax.fori_loop(1, live, add, 0)

            for flip, rhs_ref, out_ref in ((1, refs[1], sent_ref), (0, refs[2], kept_ref)):
                if not entry.counted:
                    put(out_ref, product(rhs_ref))
                    continue

                @pl.when(live == 1)
                def _(rhs_ref=rhs_ref, out_ref=out_ref):
                    put(out_ref, product(rhs_ref))

                @pl.when(live > 1)
                def _(flip=flip, rhs_ref=rhs_ref, out_ref=out_ref):
                    total[:height, :span] = product(rhs_ref)
                    add_rest(flip)
                    put(out_ref, total[:height, :span])

        starts, in_specs, operands = [], [], []
        for first, entry in zip(self.firsts, entries):
            n, height, span = entry.n, shards * entry.r, entry.width
            starts.append(len(operands))

            def unit_of(step, first=first, n=n):
                return jnp.clip(step - first, 0, n - 1)

            def spec(size, column, depth, entry=entry):
                mode = pl.Buffered(depth)
                if entry.counted:
                    return pl.BlockSpec((1, TILE, size), lambda step, meta: (0, 0, column(step, meta)), pipeline_mode=mode)
                return pl.BlockSpec((token_rows, size), lambda step, meta: (0, column(step, meta)), pipeline_mode=mode)

            if entry.kind == "wide":
                in_specs.append(spec(height, lambda step, meta: 0, 1))
                for flip in (1, 0):
                    in_specs.append(
                        spec(span, lambda step, meta, n=n, unit_of=unit_of, flip=flip: (meta[1] ^ flip) * n + unit_of(step), 2)
                    )
            else:
                in_specs.append(spec(height, lambda step, meta, unit_of=unit_of: unit_of(step), 2))
                for flip in (1, 0):
                    in_specs.append(spec(span, lambda step, meta, flip=flip: meta[1] ^ flip, 1))
            lhs, rhs = entry.lhs, entry.rhs
            if entry.counted:
                lhs, rhs = (value.reshape(-1, TILE, value.shape[1]) for value in (lhs, rhs))
                in_specs += [pl.BlockSpec(memory_space=pl.ANY)] * 2
                operands += [lhs, rhs, rhs, lhs, rhs]
            else:
                operands += [lhs, rhs, rhs]
        starts.append(len(operands))
        main = len(operands)
        for value in self.short:
            in_specs.append(whole(value.shape))
            operands.append(value)

        def add_short(refs, half, spot, sent_ref, kept_ref, row_s):
            row_s[...] = jnp.zeros_like(row_s)
            offset = 0
            for ref in refs:
                size = ref.shape[1]
                row_s[:, offset : offset + size] = ref[...]
                offset += size
            base, lane, row = self.short_base, iota((16, width), 1), iota((16, width), 0)
            for flip, out_ref in ((1, sent_ref), (0, kept_ref)):
                for shard in range(shards):
                    at = ((half ^ flip) * shards + shard) * SHORT
                    first_row = row_s[:, pl.ds(pl.multiple_of(at, LANES), width)]
                    next_row = row_s[:, pl.ds(pl.multiple_of(at + width, LANES), width)]
                    value = jnp.where(row == 0, first_row, jnp.where((row == 1) & (lane < SHORT - width), next_row, 0.0))
                    target = self.spot_of(lax.bitwise_xor(jnp.int32(shard), spot))
                    out_ref[target, base : base + 16, :] = value.astype(BF16)

        def kernel(meta, *refs):
            sent_ref, kept_ref, *scratch = refs[len(operands) :]
            step = pl.program_id(0)
            if self.short:
                row_s = scratch.pop()
                pl.when(step == 0)(lambda: add_short(refs[main : len(operands)], meta[1], meta[0], sent_ref, kept_ref, row_s))
            for index, entry in enumerate(entries):
                first = self.firsts[index]

                @pl.when((step >= first) & (step < first + entry.n))
                def _(index=index, entry=entry, first=first):
                    ins = refs[starts[index] : starts[index + 1]]
                    unit_work(entry, self.bases[index], step - first, ins, kept_ref, sent_ref, scratch, meta)

        shape = (shards, self.rows, width)
        sent, kept = self.run(
            kernel,
            "weight_grads",
            jnp.concatenate([self.spots, self.tiles[:1]]),
            in_specs,
            operands,
            [pl.BlockSpec(shape, lambda step, meta: (0, 0, 0))] * 2,
            [self.shaped(shards)] * 2,
            [
                pltpu.VMEM((tallest, token_rows), BF16),
                pltpu.VMEM((tallest, width), F32),
                pltpu.VMEM((TILE, tallest), BF16),
                pltpu.VMEM((TILE, width), BF16),
                pltpu.SemaphoreType.DMA((2,)),
            ]
            + [pltpu.VMEM((1, (2 * shards + 2) * SHORT), F32)] * bool(self.short),
            micros=40.0,
            steps=self.steps,
            limit=WEIGHT_LIMIT,
        )
        self.terms = (kept, across(sent, "blk", 0))
        self.due, self.stage = list(self.bits), 0

    def step(self):
        bits = len(self.bits)
        for last, step in ((bits, self.halve), (bits + 1, self.own), (2 * bits, self.join), (2 * bits + 1, self.finish)):
            if self.stage < last:
                self.stage += 1
                step()
                return
        self.placed = self.place()

    def halve(self):
        bit = self.due.pop(0)
        first, second = self.terms
        count = first.shape[0] // 2

        def kernel(a_ref, b_ref, sent_ref, stay_ref):
            for base, target in ((count, sent_ref), (0, stay_ref)):

                def add(index, carry, base=base, target=target):
                    target[index] = (a_ref[base + index].astype(F32) + b_ref[base + index].astype(F32)).astype(BF16)
                    return carry

                lax.fori_loop(0, count, add, 0)

        sent, stay = self.order.run_small(
            kernel, "halve", [first, second], [self.shaped(count)] * 2
        )
        self.terms = (stay, across(sent, "dp", bit))

    def own(self):
        def kernel(a_ref, b_ref, out_ref):
            out_ref[...] = (a_ref[...].astype(F32) + b_ref[...].astype(F32)).astype(BF16)

        def add(a, b):
            return self.order.run_small(kernel, "own", [a, b], [self.shaped(1)])[0]

        total = add(*self.terms)
        for bit in range(bits_of(self.shards), bits_of(lax.axis_size("dp"))):
            total = add(total, across(total, "dp", bit))
        self.due = list(reversed(self.bits))
        self.spread(total)

    def spread(self, held):
        bit = self.due.pop(0)
        self.held = (held, across(held, "dp", bit))

    def join(self):
        count = self.held[0].shape[0]

        def kernel(a_ref, b_ref, out_ref):
            out_ref[:count] = a_ref[...]
            out_ref[count:] = b_ref[...]

        (held,) = self.order.run_small(
            kernel, "join", list(self.held), [self.shaped(2 * count)]
        )
        self.spread(held)

    def finish(self):
        self.other = [across(held, "blk", 0) for held in self.held]

    def place(self):
        entries, shards, bits, slots = self.entries, self.shards, self.bits, 4
        half_count = shards // 2
        heights = [entry.r if entry.kind == "wide" else entry.n * entry.r for entry in entries]
        more = bool(self.short)
        count = len(entries) + more

        def kernel(meta, *refs):
            sources = refs[:4]
            outs, stages, sems = refs[4 : 4 + count], refs[4 + count : 4 + 2 * count], refs[-1]
            side = meta[1]

            def copies(slot, row_block):
                pairs = [
                    (stage.at[slot], out_ref.at[pl.ds(pl.multiple_of(row_block * height, 8), height), :])
                    for stage, out_ref, height in zip(stages, outs, heights)
                ]
                if more:
                    pairs += [(stages[-1].at[slot, which], outs[-1].at[which * shards + row_block]) for which in range(2)]
                return [pltpu.make_async_copy(*pair, sems.at[index, slot]) for index, pair in enumerate(pairs)]

            for upper in range(2):
                mine, other = sources[upper], sources[2 + upper]

                def one(index, carry, upper=upper, mine=mine, other=other):
                    step = upper * half_count + index
                    slot = lax.rem(step, slots)

                    @pl.when(step >= slots)
                    def _():
                        for copy in copies(slot, 0):
                            copy.wait()

                    for entry, offset, stage in zip(entries, self.bases, stages):
                        span = entry.width
                        for which, source in ((side, mine), (1 - side, other)):
                            for unit in range(entry.n):
                                row = offset + unit * entry.r
                                value = source[index, row : row + entry.r, :span].astype(F32)
                                if entry.kind == "wide":
                                    at = pl.ds(pl.multiple_of((which * entry.n + unit) * span, LANES), span)
                                    stage[slot, :, at] = value
                                else:
                                    at = pl.ds(pl.multiple_of(which * span, LANES), span)
                                    stage[slot, unit * entry.r : (unit + 1) * entry.r, at] = value
                    if more:
                        for which, source in ((side, mine), (1 - side, other)):
                            value = source[index, self.short_base : self.short_base + 16, :].astype(F32)
                            for at in range(SHORT // LANES):
                                row, lane = divmod(at * LANES, self.width)
                                stages[-1][slot, which, at : at + 1, :] = value[row : row + 1, lane : lane + LANES]
                    shard = jnp.int32(0)
                    for at, bit in enumerate(bits):
                        shard = shard | ((lax.shift_right_logical(step, len(bits) - 1 - at) & 1) << bit)
                    for copy in copies(slot, lax.bitwise_xor(shard, meta[0])):
                        copy.start()
                    return carry

                lax.fori_loop(0, half_count, one, 0)
            for step in range(max(shards - slots, 0), shards):
                for copy in copies(step % slots, 0):
                    copy.wait()

        return self.order.run_small(
            kernel,
            "place_shards",
            [self.held[0], self.held[1], *self.other],
            [jax.ShapeDtypeStruct(entry.shape, jnp.float32) for entry in entries]
            + [jax.ShapeDtypeStruct((2 * shards, 8, LANES), jnp.float32)] * more,
            scalars=self.spots,
            out_specs=[pl.BlockSpec(memory_space=pl.ANY)] * count,
            scratch=[pltpu.VMEM((slots, height, entry.shape[1]), F32) for height, entry in zip(heights, entries)]
            + [pltpu.VMEM((slots, 2, 8, LANES), F32)] * more
            + [pltpu.SemaphoreType.DMA((count + more, slots))],
        )


LOG2E = math.log2(math.e)
NEVER = -1e30
LANES = 128
BF16, F32 = jnp.bfloat16, jnp.float32


def colsum(value):
    return jnp.sum(value.astype(F32), axis=0, keepdims=True)


def normed_rows(stream):
    centred = stream - jnp.mean(stream, axis=-1, keepdims=True)
    inverse = lax.rsqrt(jnp.mean(centred * centred, axis=-1, keepdims=True) + epsilon)
    return centred * inverse, inverse


def norm_back(grad, unit, inverse, gain):
    grad = grad * gain
    inner = jnp.mean(grad * unit, axis=-1, keepdims=True)
    return inverse * (grad - jnp.mean(grad, axis=-1, keepdims=True) - unit * inner)


def gelu_pair(u):
    bell = jnp.exp2(u * u * (-0.5 * LOG2E))
    t = 1.0 / (1.0 + (0.3275911 * math.sqrt(0.5)) * jnp.abs(u))
    poly = ((((1.061405429 * t - 1.453152027) * t + 1.421413741) * t - 0.284496736) * t + 0.254829592) * t
    tail = 0.5 * poly * bell
    phi = jnp.where(u < 0, tail, 1.0 - tail)
    return u * phi, phi + u * bell * (1.0 / math.sqrt(2.0 * math.pi))


def iota(shape, axis):
    return lax.broadcasted_iota(jnp.int32, shape, axis)


def fill_groups(target, source):
    for group in range(target.shape[0]):
        target[group] = source[:, group * LANES : (group + 1) * LANES].astype(target.dtype)


def attend_forward(keys, head, q_s, k_s, v_s, mask_ref, o_s, probs=None, inverse_s=None, totals=None):
    groups, rows, _ = q_s.shape
    inside = LANES // head
    lanes = iota((rows, LANES), 1)
    which = lax.div(lanes, jnp.int32(head))
    if totals is not None:
        totals[...] = jnp.zeros_like(totals)

    def one_group(group, carry):
        queries = q_s[group]
        key_rows = k_s[group, :keys, :]
        values = v_s[group, :keys, :]
        blended = jnp.zeros((rows, LANES), F32)
        inverses = jnp.zeros((rows, LANES), F32)
        for h in range(inside):
            own = which == h
            query = jnp.where(own, queries, 0.0).astype(BF16)
            scores = matmul_nt(query, key_rows) + mask_ref[:, :keys]
            top = jnp.max(scores, axis=1, keepdims=True)
            prob = jnp.exp2(scores - top).astype(BF16)
            if probs is not None:
                probs[group * inside + h, :, :keys] = prob
            both = matmul(prob, values)
            inverse = 1.0 / both[:, LANES:]
            blended = jnp.where(own, both[:, :LANES] * inverse, blended)
            if inverse_s is not None:
                inverses = jnp.where(own, inverse, inverses)
            if totals is not None:
                at = lanes == group * inside + h
                totals[...] = jnp.where(at, top + jnp.log2(both[:, LANES:]), totals[...])
        o_s[group] = blended
        if inverse_s is not None:
            inverse_s[group] = inverses
        return carry

    lax.fori_loop(0, groups, one_group, 0)


def attend_backward(keys, head, q_s, k_s, v_s, o_s, ob_s, dq_s, dk_s, dv_s, probs=None, mask_ref=None, totals=None):
    groups, rows, _ = q_s.shape
    inside = LANES // head
    lanes = iota((rows, LANES), 1)
    which = lax.div(lanes, jnp.int32(head))

    def one_group(group, carry):
        queries, grads = q_s[group], ob_s[group]
        key_rows = k_s[group, :keys, :]
        values = v_s[group, :keys, :LANES]
        product = grads * o_s[group]
        queries_t = queries.T.astype(BF16)
        grads_t = grads.T.astype(BF16)
        query_grad = jnp.zeros((rows, LANES), F32)
        for h in range(inside):
            own = which == h
            at = slice(h * head, (h + 1) * head)
            inner = jnp.sum(jnp.where(own, product, 0.0), axis=1, keepdims=True)
            if probs is not None:
                prob = probs[group * inside + h, :, :keys]
            else:
                query = jnp.where(own, queries, 0.0).astype(BF16)
                total = jnp.sum(jnp.where(lanes == group * inside + h, totals, 0.0), axis=1, keepdims=True)
                prob = jnp.exp2(matmul_nt(query, key_rows) + (mask_ref[:, :keys] - total)).astype(BF16)
            grad_probs = matmul_nt(jnp.where(own, grads, 0.0).astype(BF16), values)
            score_grad = (prob.astype(F32) * (grad_probs - inner)).astype(BF16)
            query_grad = jnp.where(own, matmul(score_grad, key_rows), query_grad)
            dk_s[group, at, :keys] += matmul(queries_t[at], score_grad)
            dv_s[group, at, :keys] += matmul(grads_t[at], prob)
        dq_s[group] = query_grad
        return carry

    lax.fori_loop(0, groups, one_group, 0)


def whole(shape):
    rank = len(shape)
    return pl.BlockSpec(shape, lambda step, meta: (0,) * rank, pipeline_mode=pl.Buffered(1))


def out_whole(shape):
    rank = len(shape)
    return pl.BlockSpec(shape, lambda step, meta: (0,) * rank)


def row_tile(width):
    return pl.BlockSpec((TILE, width), lambda step, meta: (step, 0))


def live_tile(width):
    return pl.BlockSpec((TILE, width), lambda step, meta: (jnp.minimum(step, meta[0] - 1), 0))


def call(order, kernel, name, meta, in_specs, operands, out_specs, out_shape, scratch, micros, steps):
    return order.run(kernel, name, meta, in_specs, operands, out_specs, out_shape, scratch, micros=micros, steps=steps)


def shaped(rows, width, dtype):
    return jax.ShapeDtypeStruct((rows, width), dtype)


MARKS = 16


def enc_in(order, meta, patches, raw, far_raw, params, qkv, heads):
    rows, width = patches.shape
    factor = (width // heads) ** (-0.5) * LOG2E

    def marks_of(seen, padded, label):
        seen, kept, label = seen[...].astype(F32), 1.0 - padded[...].astype(F32), label[...].astype(F32) + 1.0
        row, result = iota((MARKS, rows), 0), jnp.zeros((MARKS, rows), F32)
        for index, value in enumerate((seen * kept * label, label, seen, kept * label)):
            result = jnp.where(row == index, value, result)
        return result

    def kernel(meta, patches_ref, *refs):
        raw_refs, far_refs, (params_ref, qkv_ref) = refs[:3], refs[3:6], refs[6:8]
        sel_ref, code_ref, far_code_ref, label_ref, marks_ref, far_marks_ref, columns_ref, s_ref, n_ref, q_ref, kv_ref, place_s = refs[8:]
        step = pl.program_id(0)

        @pl.when(step == 0)
        def _():
            below = (iota((rows, rows), 0) <= iota((rows, rows), 1)).astype(F32).astype(BF16)
            for index, (source, target) in enumerate(((raw_refs, marks_ref), (far_refs, far_marks_ref))):
                marks = marks_of(*source)
                target[...] = marks
                place = matmul(marks.astype(BF16), below)[2:3, :]
                place_s[index : index + 1, :] = jnp.where(marks[2:3, :] > 0, place - 1.0, -1.0)
            columns_ref[...] = marks_ref[...].T

        @pl.when(step < jnp.maximum(meta[0], meta[1]))
        def _():
            target = (step * TILE + iota((TILE, rows), 0)).astype(F32)
            sel = jnp.where(target == place_s[0:1, :], 1.0, 0.0).astype(BF16)
            far_sel = jnp.where(target == place_s[1:2, :], 1.0, 0.0).astype(BF16)
            sel_ref[...] = sel
            own_marks = marks_ref[...].astype(BF16)
            code_ref[...] = matmul_nt(own_marks, sel)
            far_code_ref[...] = matmul_nt(far_marks_ref[...].astype(BF16), far_sel)
            label_ref[...] = matmul_nt(sel, own_marks)

        @pl.when(step < meta[0])
        def _():
            stream = matmul(sel_ref[...], patches_ref[...])
            s_ref[...] = stream.astype(BF16)
            unit, _ = normed_rows(stream)
            normed = (unit * params_ref[:, :width] + params_ref[:, width : 2 * width]).astype(BF16)
            n_ref[...] = normed
            q_ref[...] = (matmul(normed, qkv_ref[:, :width]) * factor).astype(BF16)
            kv_ref[...] = matmul(normed, qkv_ref[:, width:]).astype(BF16)

    def last_tile(step, meta):
        return jnp.minimum(step, jnp.maximum(meta[0], meta[1]) - 1)

    lane_tile = pl.BlockSpec((MARKS, TILE), lambda step, meta: (0, last_tile(step, meta)))

    def tile(size):
        return pl.BlockSpec((TILE, size), lambda step, meta: (last_tile(step, meta), 0))

    operands = (patches, *raw, *far_raw, params, qkv)
    return call(
        order,
        kernel,
        "enc_in",
        meta,
        [whole(value.shape) for value in operands],
        operands,
        [tile(rows), lane_tile, lane_tile, tile(MARKS), out_whole((MARKS, rows)), out_whole((MARKS, rows)), out_whole((rows, MARKS))]
        + [live_tile(w) for w in (width, width, width, 2 * width)],
        [shaped(rows, rows, BF16), shaped(MARKS, rows, F32), shaped(MARKS, rows, F32), shaped(rows, MARKS, F32)]
        + [shaped(MARKS, rows, F32), shaped(MARKS, rows, F32), shaped(rows, MARKS, F32)]
        + [shaped(rows, w, BF16) for w in (width, width, width, 2 * width)],
        [pltpu.VMEM((8, rows), F32)],
        7.0,
        rows // TILE,
    )


def spread_keys(count, tiles, kv_ref, far_ref, far_tiles, k_s, v_s):
    size = count * TILE
    width = kv_ref.shape[1] // 2
    for source, live, base in ((kv_ref, tiles, 0), (far_ref, far_tiles, size)):
        ok = iota((size, LANES), 0) < live * TILE
        for group in range(width // LANES):
            at = slice(group * LANES, (group + 1) * LANES)
            value_at = slice(width + group * LANES, width + (group + 1) * LANES)
            k_s[group, base : base + size, :] = jnp.where(ok, source[:size, at].astype(F32), 0.0).astype(BF16)
            v_s[group, base : base + size, :LANES] = jnp.where(ok, source[:size, value_at].astype(F32), 0.0).astype(BF16)
            if v_s.shape[2] > LANES:
                v_s[group, base : base + size, LANES:] = jnp.ones((size, v_s.shape[2] - LANES), BF16)


def write_mask(mask_ref, label, code, far_code, size, step):
    shape = (label.shape[0], size)
    near = (label == code) | (iota(shape, 1) == step * TILE + iota(shape, 0))
    mask_ref[:, :size] = jnp.where(near, 0.0, NEVER)
    mask_ref[:, size : 2 * size] = jnp.where(label == far_code, 0.0, NEVER)


def enc_main(order, meta, s, q, kv, far_kv, label, code, far_code, params, out, up, down, embed, heads):
    rows, width = s.shape
    wide, lifted_width = up.shape[1], embed.shape[1]
    groups, head, most = width // LANES, width // heads, rows // TILE
    part = width

    def kernel(meta, s_ref, q_ref, kv_ref, far_ref, label_ref, code_ref, far_code_ref, params_ref, out_w, up_w, down_w, embed_w,
               o_ref, tot_ref, m_ref, n_ref, g_ref, gp_ref, e_ref, hi_ref, lo_ref, q_s, k_s, v_s, mask_s, o_s):
        step = pl.program_id(0)
        tiles, far_tiles = meta[0], meta[1]
        count = jnp.maximum(tiles, far_tiles)

        def param(start, size):
            return params_ref[:, start : start + size]

        @pl.when(step < tiles)
        def _():
            fill_groups(q_s, q_ref)
            for size in range(1, most + 1):

                @pl.when(count == size)
                def _(size=size):
                    @pl.when(step == 0)
                    def _():
                        spread_keys(size, tiles, kv_ref, far_ref, far_tiles, k_s, v_s)

                    span = size * TILE
                    write_mask(mask_s, label_ref[:, 1:2], code_ref[0:1, :span], far_code_ref[0:1, :span], span, step)
                    attend_forward(2 * span, head, q_s, k_s, v_s, mask_s, o_s, totals=tot_ref)

            for group in range(groups):
                o_ref[:, group * LANES : (group + 1) * LANES] = o_s[group].astype(BF16)
            middle = s_ref[...].astype(F32) + matmul(o_ref[...], out_w[...]) + param(2 * width, width)
            m_ref[...] = middle
            unit, _ = normed_rows(middle)
            normed = (unit * param(3 * width, width) + param(4 * width, width)).astype(BF16)
            n_ref[...] = normed
            encoded = middle + param(5 * width + wide, width)
            for j in range(0, wide, part):
                u = matmul(normed, up_w[:, j : j + part]) + param(5 * width + j, part)
                g, slope = gelu_pair(u)
                g = g.astype(BF16)
                g_ref[:, j : j + part] = g
                gp_ref[:, j : j + part] = slope.astype(BF16)
                encoded = encoded + matmul(g, down_w[j : j + part, :])
            low = encoded.astype(BF16)
            e_ref[...] = low
            lifted = matmul(low, embed_w[...]) + param(6 * width + wide, lifted_width)
            high = lifted.astype(BF16)
            hi_ref[...] = high
            lo_ref[...] = (lifted - high.astype(F32)).astype(BF16)

    tall = label.shape[1]
    return call(
        order,
        kernel,
        "enc_main",
        meta,
        [live_tile(width), live_tile(width), whole(kv.shape), whole(kv.shape), live_tile(tall), whole(code.shape), whole(code.shape)]
        + [whole(value.shape) for value in (params, out, up, down, embed)],
        (s, q, kv, far_kv, label, code, far_code, params, out, up, down, embed),
        [live_tile(w) for w in (width, LANES, width, width, wide, wide, width, lifted_width, lifted_width)],
        [shaped(rows, width, BF16), shaped(rows, LANES, F32), shaped(rows, width, F32), shaped(rows, width, BF16)]
        + [shaped(rows, wide, BF16)] * 2 + [shaped(rows, width, BF16)] + [shaped(rows, lifted_width, BF16)] * 2,
        [
            pltpu.VMEM((groups, TILE, LANES), F32),
            pltpu.VMEM((groups, 2 * rows, LANES), BF16),
            pltpu.VMEM((groups, 2 * rows, 2 * LANES), BF16),
            pltpu.VMEM((TILE, 2 * rows), F32),
            pltpu.VMEM((groups, TILE, LANES), F32),
        ],
        20.0,
        most,
    )


def dec_in(order, meta, sel, high, low, columns, params, qkv, heads):
    rows, width = high.shape
    tall = columns.shape[1]
    factor = (width // heads) ** (-0.5) * LOG2E

    def kernel(meta, sel_ref, hi_ref, lo_ref, col_ref, params_ref, qkv_ref, start_ref, n_ref, q_ref, kv_ref, total):
        total[...] = jnp.zeros_like(total)

        def add(tile, carry):
            at = pl.ds(pl.multiple_of(tile * TILE, TILE), TILE)
            total[...] += matmul_tn(sel_ref[at, :], hi_ref[at, :]) + matmul_tn(sel_ref[at, :], lo_ref[at, :])
            return carry

        lax.fori_loop(0, meta[0], add, 0)
        start = jnp.where(col_ref[:, 2:3] > 0, total[...], params_ref[:, params.shape[1] - width :])
        start_ref[...] = start
        unit, _ = normed_rows(start)
        normed = (unit * params_ref[:, :width] + params_ref[:, width : 2 * width]).astype(BF16)
        n_ref[...] = normed
        q_ref[...] = (matmul(normed, qkv_ref[:, :width]) * factor).astype(BF16)
        kv_ref[...] = matmul(normed, qkv_ref[:, width:]).astype(BF16)

    return call(
        order,
        kernel,
        "dec_in",
        meta,
        [pl.BlockSpec((rows, TILE), lambda step, meta: (0, step)), whole(high.shape), whole(low.shape), row_tile(tall)]
        + [whole(value.shape) for value in (params, qkv)],
        (sel, high, low, columns, params, qkv),
        [row_tile(w) for w in (width, width, width, 2 * width)],
        [shaped(rows, width, F32)] + [shaped(rows, w, BF16) for w in (width, width, 2 * width)],
        [pltpu.VMEM((TILE, width), F32)],
        7.0,
        rows // TILE,
    )


def give_key_grads(size, dk_s, dv_s, near_ref, far_ref):
    groups = dk_s.shape[0]
    for index, (source, factor) in enumerate(((dk_s, 1.0 / LOG2E), (dv_s, 1.0))):
        for group in range(groups):
            at = slice((index * groups + group) * LANES, (index * groups + group + 1) * LANES)
            near_ref[:size, at] = source[group, :, :size].T * factor
            far_ref[:size, at] = (source[group, :, size : 2 * size].T * factor).astype(BF16)


def dec_main(order, meta, start, q, kv, far_kv, columns, marks, far_marks, cotangent, params, out, up, down, heads):
    rows, width = start.shape
    wide = up.shape[1]
    groups, head, steps = width // LANES, width // heads, rows // TILE
    part = width
    tall = columns.shape[1]

    def kernel(meta, start_ref, q_ref, kv_ref, far_ref, col_ref, marks_ref, far_marks_ref, cot_ref, params_ref, out_w, up_w, down_w,
               dec_ref, o_ref, n_ref, g_ref, ub_ref, mb_ref, tm_ref, dq_ref, near_ref, back_ref,
               outb_ref, gainb_ref, shiftb_ref, upb_ref, downb_ref,
               q_s, k_s, v_s, mask_s, probs, o_s, inv_s, ob_s, dq_s, dk_s, dv_s, slope_s):
        step = pl.program_id(0)

        def param(begin, size):
            return params_ref[:, begin : begin + size]

        @pl.when(step == 0)
        def _():
            spread_keys(steps, steps, kv_ref, far_ref, steps, k_s, v_s)
            for ref in (dk_s, dv_s, outb_ref, gainb_ref, shiftb_ref, upb_ref, downb_ref):
                ref[...] = jnp.zeros_like(ref)

        fill_groups(q_s, q_ref)
        write_mask(mask_s, col_ref[:, 1:2], marks_ref[3:4, :], far_marks_ref[3:4, :], rows, step)
        attend_forward(2 * rows, head, q_s, k_s, v_s, mask_s, o_s, probs=probs, inverse_s=inv_s)
        for group in range(groups):
            o_ref[:, group * LANES : (group + 1) * LANES] = o_s[group].astype(BF16)
        middle = start_ref[...] + matmul(o_ref[...], out_w[...]) + param(2 * width, width)
        unit, inverse = normed_rows(middle)
        gain_b = param(3 * width, width)
        normed = (unit * gain_b + param(4 * width, width)).astype(BF16)
        n_ref[...] = normed
        decoded = middle + param(5 * width + wide, width)
        for j in range(0, wide, part):
            g, slope = gelu_pair(matmul(normed, up_w[:, j : j + part]) + param(5 * width + j, part))
            g = g.astype(BF16)
            g_ref[:, j : j + part] = g
            slope_s[:, j : j + part] = slope
            decoded = decoded + matmul(g, down_w[j : j + part, :])
        dec_ref[...] = decoded.astype(BF16)
        top = cot_ref[...]
        normed_grad = jnp.zeros((TILE, width), F32)
        for j in range(0, wide, part):
            low = (slope_s[:, j : j + part] * matmul_nt(top, down_w[j : j + part, :])).astype(BF16)
            ub_ref[:, j : j + part] = low
            upb_ref[:, j : j + part] += colsum(low)
            normed_grad = normed_grad + matmul_nt(low, up_w[:, j : j + part])
        downb_ref[...] += colsum(top)
        gainb_ref[...] += colsum(normed_grad * unit)
        shiftb_ref[...] += colsum(normed_grad)
        middle_grad = top.astype(F32) + norm_back(normed_grad, unit, inverse, gain_b)
        tm_ref[...] = middle_grad
        low = middle_grad.astype(BF16)
        mb_ref[...] = low
        outb_ref[...] += colsum(low)
        attended_grad = matmul_nt(low, out_w[...])
        for group in range(groups):
            scaled = attended_grad[:, group * LANES : (group + 1) * LANES] * inv_s[group]
            ob_s[group] = scaled.astype(BF16).astype(F32)
        attend_backward(2 * rows, head, q_s, k_s, v_s, o_s, ob_s, dq_s, dk_s, dv_s, probs=probs)
        scale = head ** (-0.5)
        for group in range(groups):
            dq_ref[:, group * LANES : (group + 1) * LANES] = (dq_s[group] * scale).astype(BF16)

        @pl.when(step == steps - 1)
        def _():
            give_key_grads(rows, dk_s, dv_s, near_ref, back_ref)

    small = [width, width, width, wide, width]
    return call(
        order,
        kernel,
        "dec_main",
        meta,
        [row_tile(width), row_tile(width), whole(kv.shape), whole(kv.shape), row_tile(tall), whole(marks.shape), whole(marks.shape)]
        + [row_tile(width)] + [whole(value.shape) for value in (params, out, up, down)],
        (start, q, kv, far_kv, columns, marks, far_marks, cotangent, params, out, up, down),
        [row_tile(w) for w in (width, width, width, wide, wide, width, width, width)]
        + [out_whole((rows, 2 * width))] * 2 + [out_whole((1, w)) for w in small],
        [shaped(rows, w, BF16) for w in (width, width, width, wide, wide, width)]
        + [shaped(rows, width, F32), shaped(rows, width, BF16), shaped(rows, 2 * width, F32), shaped(rows, 2 * width, BF16)]
        + [shaped(1, w, F32) for w in small],
        [
            pltpu.VMEM((groups, TILE, LANES), F32),
            pltpu.VMEM((groups, 2 * rows, LANES), BF16),
            pltpu.VMEM((groups, 2 * rows, 2 * LANES), BF16),
            pltpu.VMEM((TILE, 2 * rows), F32),
            pltpu.VMEM((heads, TILE, 2 * rows), BF16),
        ]
        + [pltpu.VMEM((groups, TILE, LANES), F32)] * 4
        + [pltpu.VMEM((groups, LANES, 2 * rows), F32)] * 2
        + [pltpu.VMEM((TILE, wide), F32)],
        95.0,
        steps,
    )


def dec_head(order, meta, start, dq, near, back, middle_grad, columns, params, qkv):
    rows, width = start.shape
    tall = columns.shape[1]

    def kernel(meta, start_ref, dq_ref, near_ref, back_ref, tm_ref, col_ref, params_ref, qkv_ref,
               dqkv_ref, lb_ref, gain_ref, shift_ref, bias_ref, token_ref):
        step = pl.program_id(0)

        @pl.when(step == 0)
        def _():
            for ref in (gain_ref, shift_ref, bias_ref, token_ref):
                ref[...] = jnp.zeros_like(ref)

        dqkv_ref[:, :width] = dq_ref[...]
        dqkv_ref[:, width:] = (near_ref[...] + back_ref[...].astype(F32)).astype(BF16)
        grad = matmul_nt(dqkv_ref[...], qkv_ref[...])
        unit, inverse = normed_rows(start_ref[...])
        gain_ref[...] += colsum(grad * unit)
        shift_ref[...] += colsum(grad)
        start_grad = tm_ref[...] + norm_back(grad, unit, inverse, params_ref[:, :width])
        seen = col_ref[:, 2:3] > 0
        token_ref[...] += colsum(jnp.where(seen, 0.0, start_grad))
        low = jnp.where(seen, start_grad, 0.0).astype(BF16)
        lb_ref[...] = low
        bias_ref[...] += colsum(low)

    return call(
        order,
        kernel,
        "dec_head",
        meta,
        [row_tile(width), row_tile(width), row_tile(2 * width), row_tile(2 * width), row_tile(width), row_tile(tall)]
        + [whole(params.shape), whole(qkv.shape)],
        (start, dq, near, back, middle_grad, columns, params, qkv),
        [row_tile(3 * width), row_tile(width)] + [out_whole((1, width))] * 4,
        [shaped(rows, 3 * width, BF16), shaped(rows, width, BF16)] + [shaped(1, width, F32)] * 4,
        [],
        40.0,
        rows // TILE,
    )


def enc_back(order, meta, sel, lb, slope, m, q, kv, far_kv, o, totals, label, code, far_code, params, out, up, down, embed, heads):
    rows, width = m.shape
    wide, lifted_width = up.shape[1], embed.shape[1]
    groups, head, most = width // LANES, width // heads, rows // TILE
    part = width
    tall = label.shape[1]

    def kernel(meta, sel_ref, lb_ref, slope_ref, m_ref, q_ref, kv_ref, far_ref, o_ref, tot_ref, label_ref, code_ref, far_code_ref,
               params_ref, out_w, up_w, down_w, embed_w,
               lbc_ref, tb_ref, ub_ref, mb_ref, tm_ref, dq_ref, near_ref, back_ref,
               outb_ref, gainb_ref, shiftb_ref, upb_ref, downb_ref,
               q_s, k_s, v_s, mask_s, o_s, ob_s, dq_s, dk_s, dv_s):
        step = pl.program_id(0)
        tiles, far_tiles = meta[0], meta[1]
        count = jnp.maximum(tiles, far_tiles)
        scale = head ** (-0.5)

        @pl.when(step == 0)
        def _():
            for ref in (dk_s, dv_s, outb_ref, gainb_ref, shiftb_ref, upb_ref, downb_ref):
                ref[...] = jnp.zeros_like(ref)

        @pl.when(step < tiles)
        def _():
            lb_here = matmul(sel_ref[...], lb_ref[...]).astype(BF16)
            lbc_ref[...] = lb_here
            grad_top = matmul_nt(lb_here, embed_w[...])
            top = grad_top.astype(BF16)
            tb_ref[...] = top
            normed_grad = jnp.zeros((TILE, width), F32)
            for j in range(0, wide, part):
                low = (slope_ref[:, j : j + part].astype(F32) * matmul_nt(top, down_w[j : j + part, :])).astype(BF16)
                ub_ref[:, j : j + part] = low
                upb_ref[:, j : j + part] += colsum(low)
                normed_grad = normed_grad + matmul_nt(low, up_w[:, j : j + part])
            unit, inverse = normed_rows(m_ref[...])
            downb_ref[...] += colsum(top)
            gainb_ref[...] += colsum(normed_grad * unit)
            shiftb_ref[...] += colsum(normed_grad)
            middle_grad = grad_top + norm_back(normed_grad, unit, inverse, params_ref[:, 3 * width : 4 * width])
            tm_ref[...] = middle_grad
            low = middle_grad.astype(BF16)
            mb_ref[...] = low
            outb_ref[...] += colsum(low)
            attended_grad = matmul_nt(low, out_w[...]).astype(BF16)
            fill_groups(ob_s, attended_grad)
            fill_groups(o_s, o_ref)
            fill_groups(q_s, q_ref)
            for size in range(1, most + 1):

                @pl.when(count == size)
                def _(size=size):
                    @pl.when(step == 0)
                    def _():
                        spread_keys(size, tiles, kv_ref, far_ref, far_tiles, k_s, v_s)

                    span = size * TILE
                    write_mask(mask_s, label_ref[:, 1:2], code_ref[0:1, :span], far_code_ref[0:1, :span], span, step)
                    attend_backward(
                        2 * span, head, q_s, k_s, v_s, o_s, ob_s, dq_s, dk_s, dv_s, mask_ref=mask_s, totals=tot_ref[...]
                    )

                    @pl.when(step == tiles - 1)
                    def _():
                        give_key_grads(span, dk_s, dv_s, near_ref, back_ref)

            for group in range(groups):
                dq_ref[:, group * LANES : (group + 1) * LANES] = (dq_s[group] * scale).astype(BF16)

    small = [width, width, width, wide, width]
    return call(
        order,
        kernel,
        "enc_back",
        meta,
        [live_tile(rows), whole(lb.shape), live_tile(wide), live_tile(width), live_tile(width), whole(kv.shape), whole(kv.shape)]
        + [live_tile(width), live_tile(LANES), live_tile(tall), whole(code.shape), whole(code.shape)]
        + [whole(value.shape) for value in (params, out, up, down, embed)],
        (sel, lb, slope, m, q, kv, far_kv, o, totals, label, code, far_code, params, out, up, down, embed),
        [live_tile(w) for w in (lifted_width, width, wide, width, width, width)]
        + [whole((rows, 2 * width))] * 2 + [out_whole((1, w)) for w in small],
        [shaped(rows, w, BF16) for w in (lifted_width, width, wide, width)]
        + [shaped(rows, width, F32), shaped(rows, width, BF16), shaped(rows, 2 * width, F32), shaped(rows, 2 * width, BF16)]
        + [shaped(1, w, F32) for w in small],
        [
            pltpu.VMEM((groups, TILE, LANES), F32),
            pltpu.VMEM((groups, 2 * rows, LANES), BF16),
            pltpu.VMEM((groups, 2 * rows, LANES), BF16),
            pltpu.VMEM((TILE, 2 * rows), F32),
        ]
        + [pltpu.VMEM((groups, TILE, LANES), F32)] * 3
        + [pltpu.VMEM((groups, LANES, 2 * rows), F32)] * 2,
        24.0,
        most,
    )


def enc_head(order, meta, sel, s, dq, near, back, middle_grad, params, qkv):
    rows, width = s.shape
    steps = rows // TILE

    def kernel(meta, sel_ref, s_ref, dq_ref, near_ref, back_ref, tm_ref, params_ref, qkv_ref,
               dqkv_ref, grad_ref, gain_ref, shift_ref, total):
        step = pl.program_id(0)

        @pl.when(step == 0)
        def _():
            for ref in (gain_ref, shift_ref, total):
                ref[...] = jnp.zeros_like(ref)

        @pl.when(step < meta[0])
        def _():
            dqkv_ref[:, :width] = dq_ref[...]
            dqkv_ref[:, width:] = (near_ref[...] + back_ref[...].astype(F32)).astype(BF16)
            grad = matmul_nt(dqkv_ref[...], qkv_ref[...])
            unit, inverse = normed_rows(s_ref[...].astype(F32))
            gain_ref[...] += colsum(grad * unit)
            shift_ref[...] += colsum(grad)
            stream_grad = tm_ref[...] + norm_back(grad, unit, inverse, params_ref[:, :width])
            total[...] += matmul_tn(sel_ref[...], stream_grad.astype(BF16))

        @pl.when(step == steps - 1)
        def _():
            grad_ref[...] = total[...].astype(BF16)

    return call(
        order,
        kernel,
        "enc_head",
        meta,
        [live_tile(w) for w in (rows, width, width, 2 * width, 2 * width, width)] + [whole(params.shape), whole(qkv.shape)],
        (sel, s, dq, near, back, middle_grad, params, qkv),
        [live_tile(3 * width), out_whole((rows, width))] + [out_whole((1, width))] * 2,
        [shaped(rows, 3 * width, BF16), shaped(rows, width, BF16)] + [shaped(1, width, F32)] * 2,
        [pltpu.VMEM((rows, width), F32)],
        40.0,
        steps,
    )


def joined(values):
    total, offset = sum(value.size for value in values), 0
    row = jnp.zeros((total,), F32)
    for value in values:
        row = row + jnp.pad(value.astype(F32), (offset, total - offset - value.size))
        offset += value.size
    return row.reshape(1, total)


def local(
    patches,
    visible,
    padding,
    field_ids,
    enc_gain_a,
    enc_shift_a,
    enc_qkv,
    enc_out,
    enc_out_bias,
    enc_gain_b,
    enc_shift_b,
    enc_up,
    enc_up_bias,
    enc_down,
    enc_down_bias,
    embed_map,
    embed_bias,
    mask_token,
    dec_gain_a,
    dec_shift_a,
    dec_qkv,
    dec_out,
    dec_out_bias,
    dec_gain_b,
    dec_shift_b,
    dec_up,
    dec_up_bias,
    dec_down,
    dec_down_bias,
    cotangent,
):
    rows = patches.shape[0]
    tiles_most = rows // TILE
    raw = [value.reshape(1, rows) for value in (visible, padding, field_ids)]
    far_raw = [across(value, "blk", 0) for value in raw]
    counts = jnp.stack([jnp.sum(raw[0]), jnp.sum(far_raw[0])]).astype(jnp.int32)
    meta = jnp.clip((counts + TILE - 1) // TILE, 1, tiles_most)

    enc_params = joined(
        [enc_gain_a, enc_shift_a, enc_out_bias, enc_gain_b, enc_shift_b, enc_up_bias, enc_down_bias, embed_bias]
    )
    dec_params = joined(
        [dec_gain_a, dec_shift_a, dec_out_bias, dec_gain_b, dec_shift_b, dec_up_bias, dec_down_bias, mask_token]
    )

    order = Order()
    shards = min(16, lax.axis_size("dp"))
    spots = jnp.stack([lax.axis_index("dp") & (shards - 1), lax.axis_index("blk")]).astype(jnp.int32)
    de, dd = enc_qkv.shape[0], dec_qkv.shape[0]
    rd, re = dd // shards, de // shards

    sel, code, far_code, label, marks, far_marks, columns, s, n1, q, kv = enc_in(order, meta, patches, raw, far_raw, enc_params, enc_qkv, HE)
    far_kv = across(kv, "blk", 0)
    o, totals, m, n2, g, slope, low, lift_high, lift_low = enc_main(
        order, meta, s, q, kv, far_kv, label, code, far_code, enc_params, enc_out, enc_up, enc_down, embed_map, HE
    )
    start, dn1, dq_rows, dkv = dec_in(order, meta, sel, lift_high, lift_low, columns, dec_params, dec_qkv, HD)
    far_dkv = across(dkv, "blk", 0)
    (decoded, d_o, d_n2, d_g, d_ub, d_mb, d_tm, d_dq, d_near, d_back, d_outb, d_gainb, d_shiftb, d_upb, d_downb) = dec_main(
        order, meta, start, dq_rows, dkv, far_dkv, columns, marks, far_marks, cotangent, dec_params, dec_out, dec_up, dec_down, HD
    )
    d_back = across(d_back, "blk", 0)

    def bundle(bits, *entries, short=()):
        return Bundle(order, bits, spots, meta, [Entry(*entry) for entry in entries], short)

    dec = bundle(
        DEC_BITS,
        ("wide", d_n2, d_ub, rd, 4, dd // 2, dec_up.shape, False),
        ("tall", d_g, cotangent, rd, 4, dd // 2, dec_down.shape, False),
        ("wide", d_o, d_mb, rd, 1, dd // 2, dec_out.shape, False),
    )
    dec.weigh()
    d_dqkv, lb, d_gaina, d_shifta, embed_b, token_grad = dec_head(
        order, meta, start, d_dq, d_near, d_back, d_tm, columns, dec_params, dec_qkv
    )
    dec.step()
    (lbc, tb, ub, mb, tm, dq, near, back, outb, gainb, shiftb, upb, downb) = enc_back(
        order, meta, sel, lb, slope, m, q, kv, far_kv, o, totals, label, code, far_code,
        enc_params, enc_out, enc_up, enc_down, embed_map, HE,
    )
    back = across(back, "blk", 0)
    dec.step()
    enc_a = bundle(
        ENC_BITS[0],
        ("wide", n2, ub, re, 4, de // 2, enc_up.shape, True),
        ("wide", o, mb, re, 1, de // 2, enc_out.shape, True),
    )
    enc_b = bundle(
        ENC_BITS[1],
        ("tall", g, tb, re, 4, de // 2, enc_down.shape, True),
        ("wide", low, lbc, re, 1, dd // 2, embed_map.shape, True),
    )
    enc_a.weigh()
    enc_b.weigh()
    enc_a.step()
    dqkv, patches_grad, gaina, shifta = enc_head(order, meta, sel, s, dq, near, back, tm, enc_params, enc_qkv)
    enc_b.step()
    dec.step()
    short = [gaina, shifta, outb, gainb, shiftb, upb, downb, embed_b, token_grad]
    short += [d_gaina, d_shifta, d_outb, d_gainb, d_shiftb, d_upb, d_downb]
    enc_c = bundle(
        ENC_BITS[2],
        ("wide", n1, dqkv, re, 3, de // 2, enc_qkv.shape, True),
        ("wide", dn1, d_dqkv, rd, 3 * dd // de, de // 2, dec_qkv.shape, False),
        short=short,
    )
    enc_c.weigh()
    bundles = {"d": dec, "a": enc_a, "b": enc_b, "c": enc_c}
    for name in STEPS:
        bundles[name].step()
    g_dec_up, g_dec_down, g_dec_out = dec.placed
    g_enc_up, g_enc_out = enc_a.placed
    g_enc_down, g_embed = enc_b.placed
    g_enc_qkv, g_dec_qkv, sums = enc_c.placed
    sums = sums[:, : SHORT // LANES, :].reshape(-1)
    small, offset = [], 0
    for value in short:
        small.append(sums[offset : offset + value.size])
        offset += value.size
    return (
        (decoded, patches_grad)
        + (small[0], small[1], g_enc_qkv, g_enc_out, small[2], small[3], small[4])
        + (g_enc_up, small[5], g_enc_down, small[6], g_embed, small[7], small[8])
        + (small[9], small[10], g_dec_qkv, g_dec_out, small[11], small[12], small[13])
        + (g_dec_up, small[14], g_dec_down, small[15])
    )


def solution(mesh):
    return jax.shard_map(
        local,
        mesh=mesh,
        in_specs=(
            P(("dp", "blk"), None),
            P(("dp", "blk")),
            P(("dp", "blk")),
            P(("dp", "blk")),
            P(),
            P(),
            P(),
            P(),
            P(),
            P(),
            P(),
            P(),
            P(),
            P(),
            P(),
            P(),
            P(),
            P(),
            P(),
            P(),
            P(),
            P(),
            P(),
            P(),
            P(),
            P(),
            P(),
            P(),
            P(),
            P(("dp", "blk"), None),
        ),
        out_specs=(
            P(("dp", "blk"), None),
            P(("dp", "blk"), None),
            P(),
            P(),
            P(),
            P(),
            P(),
            P(),
            P(),
            P(),
            P(),
            P(),
            P(),
            P(),
            P(),
            P(),
            P(),
            P(),
            P(),
            P(),
            P(),
            P(),
            P(),
            P(),
            P(),
            P(),
            P(),
        ),
        check_vma=False,
    )
```

profile of v0, /device:TPU:0, one launch (start us, length us, event | category | flops | bytes accessed | tf_op | source)
XLA Modules:
  0.0 459.7 jit_solution(8888703912827701179)
XLA Ops:
  7.1 2.0 fusion.meta
  9.7 8.2 %enc_in.1 = (bf16[768,768]{1,0:T(8,128)(2,1)}, f32[16,768]{1,0:T(8,128)}, f32[16,768]{1,0:T(8,128)}, f32[768,16]{1,0:T(8,128)}, f32[16,768]{1,0:T(8,128)}, /*ind...) custom-call(s32[2]{0:T(128)} %fusion.meta, ...), custom_call_target="tpu_custom_call" | custom-call | flops 8049999872 | bytes 25200000 | tf_op jit(solution)/shard_map/enc_in/pallas_call | solution.py:78
  18.7 4.0 collective-permute-done.3.refs_3_.refs_6_
  24.2 20.0 %enc_main.1 = (bf16[768,768]{1,0:T(8,128)(2,1)}, f32[768,128]{1,0:T(8,128)}, f32[768,768]{1,0:T(8,128)}, bf16[768,768]{1,0:T(8,128)(2,1)}, bf16[768,3072]{1,0:T(...) custom-call(s32[2]{0:T(128)} %fusion.meta, ...), custom_call_target="tpu_custom_call" | custom-call | flops 23000000512 | bytes 72000000 | tf_op jit(solution)/shard_map/enc_main/pallas_call | solution.py:78
  44.2 7.4 %dec_in.1 = (f32[768,512]{1,0:T(8,128)}, bf16[768,512]{1,0:T(8,128)(2,1)}, bf16[768,512]{1,0:T(8,128)(2,1)}, bf16[768,1024]{1,0:T(8,128)(2,1)}, f32[8,128]{1,0:T(8,128)}) custom-call(s32[2]{0:T(128)} %fusion.meta, bf16[768,768]{1,0:T(8,128)(2,1)} %get-tuple-element.201.refs_0_, bf16[768,512]{1,0:T(8,128)(2,1)} %get-tuple-element.209.refs_1_, ...), custom_call_target="tpu_custom_call" | custom-call | flops 8049999872 | bytes 25200000 | tf_op jit(solution)/shard_map/dec_in/pallas_call | solution.py:78
  51.9 3.4 collective-permute-done.4.refs_3_
  56.4 94.6 %dec_main.1 = (bf16[768,512]{1,0:T(8,128)(2,1)}, bf16[768,512]{1,0:T(8,128)(2,1)}, bf16[768,512]{1,0:T(8,128)(2,1)}, bf16[768,2048]{1,0:T(8,128)(2,1)}, bf16[768...) custom-call(s32[2]{0:T(128)} %fusion.meta, ...), custom_call_target="tpu_custom_call" | custom-call | flops 109250002944 | bytes 342000000 | tf_op jit(solution)/shard_map/dec_main/pallas_call | solution.py:78
  151.2 1.9 copy-done.14
  153.1 1.9 copy-done.15
  159.1 7.9 %weight_grads.4 = (bf16[16,288,256]{2,1,0:T(8,128)(2,1)S(1)}, bf16[16,288,256]{2,1,0:T(8,128)(2,1)S(1)}, f32[8,128]{1,0:T(8,128)S(1)}) custom-call(s32[3]{0:T(128)S(1)} %pad_add_fusion.meta, bf16[768,512]{1,0:T(8,128)(2,1)S(1)} %copy-done.24, bf16[768,2048]{1,0:T(8,128)(2,1)S(1)} %copy-done.15, bf16[768,2048]{1,0:T(8,128)(2,1)S(1)} %copy-done.15, ...), custom_call_target="tpu_custom_call" | custom-call | flops 46000001024 | bytes 144000000 | tf_op jit(solution)/shard_map/weight_grads/pallas_call | solution.py:78
  169.3 8.1 %dec_head.1 = (bf16[768,1536]{1,0:T(8,128)(2,1)}, bf16[768,512]{1,0:T(8,128)(2,1)}, f32[1,512]{1,0:T(1,128)}, f32[1,512]{1,0:T(1,128)}, f32[1,512]{1,0:T(1,128)}, /*index=5*/f32[1,512]{1,0:T(1,128)}, f32[8,128]{1,0:T(8,128)}) custom-call(s32[2]{0:T(128)} %fusion.meta, f32[768,512]{1,0:T(8,128)} %get-tuple-element.213.refs_0_, ...), custom_call_target="tpu_custom_call" | custom-call | flops 46000001024 | bytes 144000000 | tf_op jit(solution)/shard_map/dec_head/pallas_call | solution.py:78
  179.8 2.3 halve.16
  182.6 2.7 collective-permute-start.8
  185.3 24.6 %enc_back.1 = (bf16[768,512]{1,0:T(8,128)(2,1)}, bf16[768,768]{1,0:T(8,128)(2,1)}, bf16[768,3072]{1,0:T(8,128)(2,1)}, bf16[768,768]{1,0:T(8,128)(2,1)}, f32[768,...) custom-call(s32[2]{0:T(128)} %fusion.meta, ...), custom_call_target="tpu_custom_call" | custom-call | flops 27599998976 | bytes 86400000 | tf_op jit(solution)/shard_map/enc_back/pallas_call | solution.py:78
  216.3 5.1 %weight_grads.5 = (bf16[16,240,384]{2,1,0:T(8,128)(2,1)S(1)}, bf16[16,240,384]{2,1,0:T(8,128)(2,1)S(1)}, f32[8,128]{1,0:T(8,128)S(1)}) custom-call(s32[3]{0:T(128)S(1)} %pad_add_fusion.meta, bf16[3,256,768]{2,1,0:T(8,128)(2,1)S(1)} %bitcast.48, bf16[3,256,3072]{2,1,0:T(8,128)(2,1)S(1)} %bitcast.36, bf16[3,256,3072]{2,1,0:T(8,128)(2,1)S(1)} %bitcast.37, ...), custom_call_target="tpu_custom_call" | custom-call | flops 46000001024 | bytes 144000000 | tf_op jit(solution)/shard_map/weight_grads/pallas_call | solution.py:78
  223.0 2.3 copy-done.1
  225.3 5.3 %weight_grads.6 = (bf16[16,240,384]{2,1,0:T(8,128)(2,1)S(1)}, bf16[16,240,384]{2,1,0:T(8,128)(2,1)S(1)}, f32[8,128]{1,0:T(8,128)S(1)}) custom-call(s32[3]{0:T(128)S(1)} %pad_add_fusion.meta, bf16[3,256,3072]{2,1,0:T(8,128)(2,1)S(1)} %bitcast.34, bf16[3,256,768]{2,1,0:T(8,128)(2,1)S(1)} %bitcast.50, bf16[3,256,768]{2,1,0:T(8,128)(2,1)S(1)} %bitcast.51, ...), custom_call_target="tpu_custom_call" | custom-call | flops 46000001024 | bytes 144000000 | tf_op jit(solution)/shard_map/weight_grads/pallas_call | solution.py:78
  231.2 1.9 halve.18
  236.6 8.3 %enc_head.1 = (bf16[768,2304]{1,0:T(8,128)(2,1)}, bf16[768,768]{1,0:T(8,128)(2,1)}, f32[1,768]{1,0:T(1,128)}, f32[1,768]{1,0:T(1,128)}, f32[8,128]{1,0:T(8,128)}) custom-call(s32[2]{0:T(128)} %fusion.meta, bf16[768,768]{1,0:T(8,128)(2,1)} %get-tuple-element.201.refs_0_, bf16[768,768]{1,0:T(8,128)(2,1)} %get-tuple-element.202.refs_0_.refs_1_, ...), custom_call_target="tpu_custom_call" | custom-call | flops 46000001024 | bytes 144000000 | tf_op jit(solution)/shard_map/enc_head/pallas_call | solution.py:78
  244.9 1.8 copy-done.17
  247.4 3.8 halve.19
  256.1 6.3 %weight_grads.7 = (bf16[16,224,384]{2,1,0:T(8,128)(2,1)S(1)}, bf16[16,224,384]{2,1,0:T(8,128)(2,1)S(1)}, f32[8,128]{1,0:T(8,128)S(1)}) custom-call(s32[3]{0:T(128)S(1)} %pad_add_fusion.meta, bf16[3,256,768]{2,1,0:T(8,128)(2,1)S(1)} %bitcast.42, bf16[3,256,2304]{2,1,0:T(8,128)(2,1)S(1)} %bitcast.39, bf16[3,256,2304]{2,1,0:T(8,128)(2,1)S(1)} %bitcast.40, ...), custom_call_target="tpu_custom_call" | custom-call | flops 46000001024 | bytes 144000000 | tf_op jit(solution)/shard_map/weight_grads/pallas_call | solution.py:78
  262.6 2.6 collective-permute-start.17
  265.2 2.4 collective-permute-done.12.refs_1_
  268.9 3.8 collective-permute-done.15.refs_1_
  274.5 1.9 collective-permute-start.18
  277.9 12.0 %collective-permute-done.19.refs_1_ = bf16[8,240,384]{2,1,0:T(8,128)(2,1)} collective-permute-done((bf16[8,240,384]{2,1,0:T(8,128)(2,1)}, bf16[8,240,384]{2,1,0:T(8,128)(2,1)}, u32[]{:S(2)}, u32[]{:S(2)}) %collective-permute-start.19) | collective-permute-done | bytes 1474592 | tf_op jit(solution)/shard_map/ppermute | solution.py:48
  292.5 11.6 %collective-permute-done.16.refs_1_ = bf16[4,240,384]{2,1,0:T(8,128)(2,1)S(1)} collective-permute-done((bf16[4,240,384]{2,1,0:T(8,128)(2,1)S(1)}, bf16[4,240,384]{2,1,0:T(8,128)(2,1)S(1)}, u32[]{:S(2)}, u32[]{:S(2)}) %collective-permute-start.16) | collective-permute-done | bytes 737312 | tf_op jit(solution)/shard_map/ppermute | solution.py:48
  305.3 2.0 collective-permute-done.23.refs_1_
  310.2 5.7 %collective-permute-done.21.refs_1_ = bf16[2,240,384]{2,1,0:T(8,128)(2,1)S(1)} collective-permute-done((bf16[2,240,384]{2,1,0:T(8,128)(2,1)S(1)}, bf16[2,240,384]{2,1,0:T(8,128)(2,1)S(1)}, u32[]{:S(2)}, u32[]{:S(2)}) %collective-permute-start.21) | collective-permute-done | bytes 368672 | tf_op jit(solution)/shard_map/ppermute | solution.py:48
  316.0 7.4 %collective-permute-done.20.refs_1_ = bf16[4,224,384]{2,1,0:T(8,128)(2,1)S(1)} collective-permute-done((bf16[4,224,384]{2,1,0:T(8,128)(2,1)S(1)}, bf16[4,224,384]{2,1,0:T(8,128)(2,1)S(1)}, u32[]{:S(2)}, u32[]{:S(2)}) %collective-permute-start.20) | collective-permute-done | bytes 688160 | tf_op jit(solution)/shard_map/ppermute | solution.py:48
  325.3 2.6 collective-permute-start.25
  328.4 6.4 %collective-permute-done.25.refs_1_ = bf16[1,240,384]{2,1,0:T(8,128)(2,1)S(1)} collective-permute-done((bf16[1,240,384]{2,1,0:T(8,128)(2,1)S(1)}, bf16[1,240,384]{2,1,0:T(8,128)(2,1)S(1)}, u32[]{:S(2)}, u32[]{:S(2)}) %collective-permute-start.25) | collective-permute-done | bytes 184352 | tf_op jit(solution)/shard_map/ppermute | solution.py:48
  337.9 9.9 %collective-permute-done.29.refs_2_ = bf16[8,288,256]{2,1,0:T(8,128)(2,1)S(1)} collective-permute-done((bf16[8,288,256]{2,1,0:T(8,128)(2,1)S(1)}, bf16[8,288,256]{2,1,0:T(8,128)(2,1)S(1)}, u32[]{:S(2)}, u32[]{:S(2)}) %collective-permute-start.29) | collective-permute-done | bytes 1179680 | tf_op jit(solution)/shard_map/ppermute | solution.py:48
  347.9 2.7 collective-permute-start.28
  352.4 4.5 place_shards.4
  357.0 6.3 %collective-permute-done.28.refs_1_ = bf16[1,224,384]{2,1,0:T(8,128)(2,1)S(1)} collective-permute-done((bf16[1,224,384]{2,1,0:T(8,128)(2,1)S(1)}, bf16[1,224,384]{2,1,0:T(8,128)(2,1)S(1)}, u32[]{:S(2)}, u32[]{:S(2)}) %collective-permute-start.28) | collective-permute-done | bytes 172064 | tf_op jit(solution)/shard_map/ppermute | solution.py:48
  363.4 7.4 %collective-permute-done.35.refs_1_ = bf16[1,240,384]{2,1,0:T(8,128)(2,1)S(1)} collective-permute-done((bf16[1,240,384]{2,1,0:T(8,128)(2,1)S(1)}, bf16[1,240,384]{2,1,0:T(8,128)(2,1)S(1)}, u32[]{:S(2)}, u32[]{:S(2)}) %collective-permute-start.35) | collective-permute-done | bytes 184352 | tf_op jit(solution)/shard_map/ppermute | solution.py:48
  374.6 6.9 %collective-permute-done.39.refs_1_ = bf16[2,240,384]{2,1,0:T(8,128)(2,1)S(1)} collective-permute-done((bf16[2,240,384]{2,1,0:T(8,128)(2,1)S(1)}, bf16[2,240,384]{2,1,0:T(8,128)(2,1)S(1)}, u32[]{:S(2)}, u32[]{:S(2)}) %collective-permute-start.39) | collective-permute-done | bytes 368672 | tf_op jit(solution)/shard_map/ppermute | solution.py:48
  381.6 7.9 %collective-permute-done.38.refs_1_ = bf16[4,240,384]{2,1,0:T(8,128)(2,1)S(1)} collective-permute-done((bf16[4,240,384]{2,1,0:T(8,128)(2,1)S(1)}, bf16[4,240,384]{2,1,0:T(8,128)(2,1)S(1)}, u32[]{:S(2)}, u32[]{:S(2)}) %collective-permute-start.38) | collective-permute-done | bytes 737312 | tf_op jit(solution)/shard_map/ppermute | solution.py:48
  391.4 9.9 %collective-permute-done.41.refs_1_ = bf16[4,240,384]{2,1,0:T(8,128)(2,1)S(1)} collective-permute-done((bf16[4,240,384]{2,1,0:T(8,128)(2,1)S(1)}, bf16[4,240,384]{2,1,0:T(8,128)(2,1)S(1)}, u32[]{:S(2)}, u32[]{:S(2)}) %collective-permute-start.41) | collective-permute-done | bytes 737312 | tf_op jit(solution)/shard_map/ppermute | solution.py:48
  401.4 4.6 %collective-permute-done.40.refs_1_ = bf16[4,224,384]{2,1,0:T(8,128)(2,1)S(1)} collective-permute-done((bf16[4,224,384]{2,1,0:T(8,128)(2,1)S(1)}, bf16[4,224,384]{2,1,0:T(8,128)(2,1)S(1)}, u32[]{:S(2)}, u32[]{:S(2)}) %collective-permute-start.40) | collective-permute-done | bytes 688160 | tf_op jit(solution)/shard_map/ppermute | solution.py:48
  409.3 22.7 %collective-permute-done.45.refs_2_ = bf16[8,240,384]{2,1,0:T(8,128)(2,1)S(1)} collective-permute-done((bf16[8,240,384]{2,1,0:T(8,128)(2,1)S(1)}, bf16[8,240,384]{2,1,0:T(8,128)(2,1)S(1)}, u32[]{:S(2)}, u32[]{:S(2)}) %collective-permute-start.45) | collective-permute-done | bytes 1474592 | tf_op jit(solution)/shard_map/ppermute | solution.py:48
  432.5 3.7 collective-permute-done.42.refs_2_
  436.8 5.7 %collective-permute-done.48.refs_2_ = bf16[8,240,384]{2,1,0:T(8,128)(2,1)S(1)} collective-permute-done((bf16[8,240,384]{2,1,0:T(8,128)(2,1)S(1)}, bf16[8,240,384]{2,1,0:T(8,128)(2,1)S(1)}, u32[]{:S(2)}, u32[]{:S(2)}) %collective-permute-start.48) | collective-permute-done | bytes 1474592 | tf_op jit(solution)/shard_map/ppermute | solution.py:48
  442.5 4.9 %place_shards.5 = (f32[768,3072]{1,0:T(8,128)}, f32[768,768]{1,0:T(8,128)}, f32[8,128]{1,0:T(8,128)S(1)}) custom-call(s32[2]{0:T(128)S(1)} %pad_add_fusion.1.refs_0_, bf16[8,240,384]{2,1,0:T(8,128)(2,1)S(1)} %get-tuple-element.360.refs_1_, bf16[8,240,384]{2,1,0:T(8,128)(2,1)S(1)} %collective-permute-done.45.refs_2_, ...), custom_call_target="tpu_custom_call" | custom-call | flops 4600000000 | bytes 14400000 | tf_op jit(solution)/shard_map/place_shards/pallas_call | solution.py:109
  447.5 4.8 %place_shards.6 = (f32[768,2304]{1,0:T(8,128)}, f32[512,1536]{1,0:T(8,128)}, f32[32,8,128]{2,1,0:T(8,128)S(1)}, f32[8,128]{1,0:T(8,128)S(1)}) custom-call(s32[2]{0:T(128)S(1)} %pad_add_fusion.1.refs_0_, bf16[8,224,384]{2,1,0:T(8,128)(2,1)S(1)} %get-tuple-element.359.refs_1_, bf16[8,224,384]{2,1,0:T(8,128)(2,1)S(1)} %collective-permute-done.42.refs_2_, ...), custom_call_target="tpu_custom_call" | custom-call | flops 4600000000 | bytes 14400000 | tf_op jit(solution)/shard_map/place_shards/pallas_call | solution.py:109
  454.7 4.8 %place_shards.7 = (f32[3072,768]{1,0:T(8,128)}, f32[768,512]{1,0:T(8,128)}, f32[8,128]{1,0:T(8,128)}) custom-call(s32[2]{0:T(128)S(1)} %pad_add_fusion.1.refs_0_, bf16[8,240,384]{2,1,0:T(8,128)(2,1)S(1)} %get-tuple-element.367.refs_1_, bf16[8,240,384]{2,1,0:T(8,128)(2,1)S(1)} %collective-permute-done.48.refs_2_, ...), custom_call_target="tpu_custom_call" | custom-call | flops 4600000000 | bytes 14400000 | tf_op jit(solution)/shard_map/place_shards/pallas_call | solution.py:109
  (253 shorter events, 69.3 us)
Async XLA Ops:
  1.4 5.1 %collective-permute-start = (s32[1,768]{1,0:T(1,128)S(1)}, s32[1,768]{1,0:T(1,128)S(1)}, u32[]{:S(2)}, u32[]{:S(2)}) collective-permute-start(s32[1,768]{1,0:T(1,128)S(1)} %reshape.111.refs_1_), channel_id=1, source_target_pairs={{0,1},{1,0},{2,3},{3,2},{4,5},{5,4},{6,7},{7,6},{8,9},{9,8},{10,11... | collective-permute-start | bytes 9224 | tf_op jit(solution)/shard_map/ppermute | solution.py:48
  2.5 6.6 %collective-permute-start.2 = (s32[1,768]{1,0:T(1,128)S(1)}, s32[1,768]{1,0:T(1,128)S(1)}, u32[]{:S(2)}, u32[]{:S(2)}) collective-permute-start(s32[1,768]{1,0:T(1,128)S(1)} %reshape.113.refs_3_), channel_id=1, source_target_pairs={{0,1},{1,0},{2,3},{3,2},{4,5},{5,4},{6,7},{7,6},{8,9},{9,8},{10,11... | collective-permute-start | bytes 9224 | tf_op jit(solution)/shard_map/ppermute | solution.py:48
  3.3 5.8 %collective-permute-start.1 = (s32[1,768]{1,0:T(1,128)S(1)}, s32[1,768]{1,0:T(1,128)S(1)}, u32[]{:S(2)}, u32[]{:S(2)}) collective-permute-start(s32[1,768]{1,0:T(1,128)S(1)} %reshape.112.refs_2_), channel_id=1, source_target_pairs={{0,1},{1,0},{2,3},{3,2},{4,5},{5,4},{6,7},{7,6},{8,9},{9,8},{10,11... | collective-permute-start | bytes 9224 | tf_op jit(solution)/shard_map/ppermute | solution.py:48
  151.0 18.3 %collective-permute-start.5 = (bf16[768,1024]{1,0:T(8,128)(2,1)}, bf16[768,1024]{1,0:T(8,128)(2,1)}, u32[]{:S(2)}, u32[]{:S(2)}) collective-permute-start(bf16[768,1024]{1,0:T(8,128)(2,1)} %get-tuple-element.222), channel_id=1, source_target_pairs={{0,1},{1,0},{2,3},{3,2},{4,5},{5,4},{6,7},{7,6},{8,9},{9,8},{10,11... | collective-permute-start | bytes 4718600 | tf_op jit(solution)/shard_map/ppermute | solution.py:48
  168.9 8.5 %collective-permute-start.6 = (bf16[16,288,256]{2,1,0:T(8,128)(2,1)S(1)}, bf16[16,288,256]{2,1,0:T(8,128)(2,1)}, u32[]{:S(2)}, u32[]{:S(2)}) collective-permute-start(bf16[16,288,256]{2,1,0:T(8,128)(2,1)S(1)} %get-tuple-element.237), channel_id=1, source_target_pairs={{0,1},{1,0},{2,3},{3,2},{4,5},{5,4},{6,7},{7,6},{8,9},{9,8},{10,11... | collective-permute-start | bytes 7077896 | tf_op jit(solution)/shard_map/ppermute | solution.py:48
  182.6 29.1 %collective-permute-start.8 = (bf16[8,288,256]{2,1,0:T(8,128)(2,1)S(1)}, bf16[8,288,256]{2,1,0:T(8,128)(2,1)S(1)}, u32[]{:S(2)}, u32[]{:S(2)}) collective-permute-start(bf16[8,288,256]{2,1,0:T(8,128)(2,1)S(1)} %get-tuple-element.248), channel_id=1, source_target_pairs={{0,4},{2,6},{4,0},{6,2},{8,12},{10,14},{12,8},{14,10},{16,20},{18,... | collective-permute-start | bytes 3538952 | tf_op jit(solution)/shard_map/ppermute | solution.py:48
  209.9 26.7 %collective-permute-start.7 = (bf16[768,1536]{1,0:T(8,128)(2,1)}, bf16[768,1536]{1,0:T(8,128)(2,1)}, u32[]{:S(2)}, u32[]{:S(2)}) collective-permute-start(bf16[768,1536]{1,0:T(8,128)(2,1)} %get-tuple-element.242), channel_id=1, source_target_pairs={{0,1},{1,0},{2,3},{3,2},{4,5},{5,4},{6,7},{7,6},{8,9},{9,8},{10,11... | collective-permute-start | bytes 7077896 | tf_op jit(solution)/shard_map/ppermute | solution.py:48
  214.4 36.8 %collective-permute-start.10 = (bf16[4,288,256]{2,1,0:T(8,128)(2,1)}, bf16[4,288,256]{2,1,0:T(8,128)(2,1)}, u32[]{:S(2)}, u32[]{:S(2)}) collective-permute-start(bf16[4,288,256]{2,1,0:T(8,128)(2,1)} %get-tuple-element.282), channel_id=1, source_target_pairs={{0,8},{2,10},{4,12},{6,14},{8,0},{10,2},{12,4},{14,6},{16,24},{18,... | collective-permute-start | bytes 1769480 | tf_op jit(solution)/shard_map/ppermute | solution.py:48
  223.0 8.2 %collective-permute-start.9 = (bf16[16,240,384]{2,1,0:T(8,128)(2,1)S(1)}, bf16[16,240,384]{2,1,0:T(8,128)(2,1)S(1)}, u32[]{:S(2)}, u32[]{:S(2)}) collective-permute-start(bf16[16,240,384]{2,1,0:T(8,128)(2,1)S(1)} %get-tuple-element.252), channel_id=1, source_target_pairs={{0,1},{1,0},{2,3},{3,2},{4,5},{5,4},{6,7},{7,6},{8,9},{9,8},{10,11... | collective-permute-start | bytes 8847368 | tf_op jit(solution)/shard_map/ppermute | solution.py:48
  230.6 14.3 %collective-permute-start.11 = (bf16[16,240,384]{2,1,0:T(8,128)(2,1)S(1)}, bf16[16,240,384]{2,1,0:T(8,128)(2,1)}, u32[]{:S(2)}, u32[]{:S(2)}) collective-permute-start(bf16[16,240,384]{2,1,0:T(8,128)(2,1)S(1)} %get-tuple-element.284), channel_id=1, source_target_pairs={{0,1},{1,0},{2,3},{3,2},{4,5},{5,4},{6,7},{7,6},{8,9},{9,8},{10,11... | collective-permute-start | bytes 8847368 | tf_op jit(solution)/shard_map/ppermute | solution.py:48
  234.8 37.9 %collective-permute-start.15 = (bf16[8,240,384]{2,1,0:T(8,128)(2,1)}, bf16[8,240,384]{2,1,0:T(8,128)(2,1)}, u32[]{:S(2)}, u32[]{:S(2)}) collective-permute-start(bf16[8,240,384]{2,1,0:T(8,128)(2,1)} %get-tuple-element.297), channel_id=1, source_target_pairs={{0,8},{2,10},{4,12},{6,14},{8,0},{10,2},{12,4},{14,6},{16,24},{18,... | collective-permute-start | bytes 4423688 | tf_op jit(solution)/shard_map/ppermute | solution.py:48
  252.8 9.7 %collective-permute-start.13 = (bf16[2,288,256]{2,1,0:T(8,128)(2,1)S(1)}, bf16[2,288,256]{2,1,0:T(8,128)(2,1)S(1)}, u32[]{:S(2)}, u32[]{:S(2)}) collective-permute-start(bf16[2,288,256]{2,1,0:T(8,128)(2,1)S(1)} %get-tuple-element.291), channel_id=1, source_target_pairs={{0,2},{2,0},{4,6},{6,4},{8,10},{10,8},{12,14},{14,12},{16,18},{18,... | collective-permute-start | bytes 884744 | tf_op jit(solution)/shard_map/ppermute | solution.py:48
  254.3 35.5 %collective-permute-start.19 = (bf16[8,240,384]{2,1,0:T(8,128)(2,1)}, bf16[8,240,384]{2,1,0:T(8,128)(2,1)}, u32[]{:S(2)}, u32[]{:S(2)}) collective-permute-start(bf16[8,240,384]{2,1,0:T(8,128)(2,1)} %get-tuple-element.306), channel_id=1, source_target_pairs={{0,4},{2,6},{4,0},{6,2},{8,12},{10,14},{12,8},{14,10},{16,20},{18,... | collective-permute-start | bytes 4423688 | tf_op jit(solution)/shard_map/ppermute | solution.py:48
  262.4 5.2 %collective-permute-start.12 = (bf16[16,224,384]{2,1,0:T(8,128)(2,1)S(1)}, bf16[16,224,384]{2,1,0:T(8,128)(2,1)S(1)}, u32[]{:S(2)}, u32[]{:S(2)}) collective-permute-start(bf16[16,224,384]{2,1,0:T(8,128)(2,1)S(1)} %get-tuple-element.289), channel_id=1, source_target_pairs={{0,1},{1,0},{2,3},{3,2},{4,5},{5,4},{6,7},{7,6},{8,9},{9,8},{10,11... | collective-permute-start | bytes 8257544 | tf_op jit(solution)/shard_map/ppermute | solution.py:48
  262.6 11.9 %collective-permute-start.17 = (bf16[1,288,256]{2,1,0:T(8,128)(2,1)S(1)}, bf16[1,288,256]{2,1,0:T(8,128)(2,1)S(1)}, u32[]{:S(2)}, u32[]{:S(2)}) collective-permute-start(bf16[1,288,256]{2,1,0:T(8,128)(2,1)S(1)} %get-tuple-element.302), channel_id=1, source_target_pairs={{0,16},{2,18},{4,20},{6,22},{8,24},{10,26},{12,28},{14,30},{16,0},... | collective-permute-start | bytes 442376 | tf_op jit(solution)/shard_map/ppermute | solution.py:48
  268.3 36.6 %collective-permute-start.14 = (bf16[8,224,384]{2,1,0:T(8,128)(2,1)S(1)}, bf16[8,224,384]{2,1,0:T(8,128)(2,1)S(1)}, u32[]{:S(2)}, u32[]{:S(2)}) collective-permute-start(bf16[8,224,384]{2,1,0:T(8,128)(2,1)S(1)} %get-tuple-element.295), channel_id=1, source_target_pairs={{0,2},{2,0},{4,6},{6,4},{8,10},{10,8},{12,14},{14,12},{16,18},{18,... | collective-permute-start | bytes 4128776 | tf_op jit(solution)/shard_map/ppermute | solution.py:48
  274.5 17.7 %collective-permute-start.18 = (bf16[1,288,256]{2,1,0:T(8,128)(2,1)S(1)}, bf16[1,288,256]{2,1,0:T(8,128)(2,1)S(1)}, u32[]{:S(2)}, u32[]{:S(2)}) collective-permute-start(bf16[1,288,256]{2,1,0:T(8,128)(2,1)S(1)} %get-tuple-element.304.refs_0_), channel_id=1, source_target_pairs={{0,16},{2,18},{4,20},{6,22},{8,24},{10,26},{12,28},{14,30},{16,0},... | collective-permute-start | bytes 442376 | tf_op jit(solution)/shard_map/ppermute | solution.py:48
  276.4 27.7 %collective-permute-start.16 = (bf16[4,240,384]{2,1,0:T(8,128)(2,1)S(1)}, bf16[4,240,384]{2,1,0:T(8,128)(2,1)S(1)}, u32[]{:S(2)}, u32[]{:S(2)}) collective-permute-start(bf16[4,240,384]{2,1,0:T(8,128)(2,1)S(1)} %get-tuple-element.300), channel_id=1, source_target_pairs={{0,4},{2,6},{4,0},{6,2},{8,12},{10,14},{12,8},{14,10},{16,20},{18,... | collective-permute-start | bytes 2211848 | tf_op jit(solution)/shard_map/ppermute | solution.py:48
  291.6 15.7 %collective-permute-start.23 = (bf16[4,240,384]{2,1,0:T(8,128)(2,1)S(1)}, bf16[4,240,384]{2,1,0:T(8,128)(2,1)S(1)}, u32[]{:S(2)}, u32[]{:S(2)}) collective-permute-start(bf16[4,240,384]{2,1,0:T(8,128)(2,1)S(1)} %get-tuple-element.317), channel_id=1, source_target_pairs={{0,8},{2,10},{4,12},{6,14},{8,0},{10,2},{12,4},{14,6},{16,24},{18,... | collective-permute-start | bytes 2211848 | tf_op jit(solution)/shard_map/ppermute | solution.py:48
  292.2 17.4 %collective-permute-start.22 = (bf16[2,288,256]{2,1,0:T(8,128)(2,1)S(1)}, bf16[2,288,256]{2,1,0:T(8,128)(2,1)S(1)}, u32[]{:S(2)}, u32[]{:S(2)}) collective-permute-start(bf16[2,288,256]{2,1,0:T(8,128)(2,1)S(1)} %get-tuple-element.315.refs_0_), channel_id=1, source_target_pairs={{0,2},{2,0},{4,6},{6,4},{8,10},{10,8},{12,14},{14,12},{16,18},{18,... | collective-permute-start | bytes 884744 | tf_op jit(solution)/shard_map/ppermute | solution.py:48
  304.3 11.6 %collective-permute-start.21 = (bf16[2,240,384]{2,1,0:T(8,128)(2,1)S(1)}, bf16[2,240,384]{2,1,0:T(8,128)(2,1)S(1)}, u32[]{:S(2)}, u32[]{:S(2)}) collective-permute-start(bf16[2,240,384]{2,1,0:T(8,128)(2,1)S(1)} %get-tuple-element.314), channel_id=1, source_target_pairs={{0,2},{2,0},{4,6},{6,4},{8,10},{10,8},{12,14},{14,12},{16,18},{18,... | collective-permute-start | bytes 1105928 | tf_op jit(solution)/shard_map/ppermute | solution.py:48
  307.5 20.8 %collective-permute-start.26 = (bf16[2,240,384]{2,1,0:T(8,128)(2,1)S(1)}, bf16[2,240,384]{2,1,0:T(8,128)(2,1)S(1)}, u32[]{:S(2)}, u32[]{:S(2)}) collective-permute-start(bf16[2,240,384]{2,1,0:T(8,128)(2,1)S(1)} %get-tuple-element.327), channel_id=1, source_target_pairs={{0,2},{2,0},{4,6},{6,4},{8,10},{10,8},{12,14},{14,12},{16,18},{18,... | collective-permute-start | bytes 1105928 | tf_op jit(solution)/shard_map/ppermute | solution.py:48
  308.1 15.2 %collective-permute-start.20 = (bf16[4,224,384]{2,1,0:T(8,128)(2,1)S(1)}, bf16[4,224,384]{2,1,0:T(8,128)(2,1)S(1)}, u32[]{:S(2)}, u32[]{:S(2)}) collective-permute-start(bf16[4,224,384]{2,1,0:T(8,128)(2,1)S(1)} %get-tuple-element.312), channel_id=1, source_target_pairs={{0,4},{2,6},{4,0},{6,2},{8,12},{10,14},{12,8},{14,10},{16,20},{18,... | collective-permute-start | bytes 2064392 | tf_op jit(solution)/shard_map/ppermute | solution.py:48
  309.7 13.9 %collective-permute-start.27 = (bf16[4,288,256]{2,1,0:T(8,128)(2,1)S(1)}, bf16[4,288,256]{2,1,0:T(8,128)(2,1)S(1)}, u32[]{:S(2)}, u32[]{:S(2)}) collective-permute-start(bf16[4,288,256]{2,1,0:T(8,128)(2,1)S(1)} %get-tuple-element.328.refs_0_), channel_id=1, source_target_pairs={{0,8},{2,10},{4,12},{6,14},{8,0},{10,2},{12,4},{14,6},{16,24},{18,... | collective-permute-start | bytes 1769480 | tf_op jit(solution)/shard_map/ppermute | solution.py:48
  323.6 24.1 %collective-permute-start.29 = (bf16[8,288,256]{2,1,0:T(8,128)(2,1)S(1)}, bf16[8,288,256]{2,1,0:T(8,128)(2,1)S(1)}, u32[]{:S(2)}, u32[]{:S(2)}) collective-permute-start(bf16[8,288,256]{2,1,0:T(8,128)(2,1)S(1)} %get-tuple-element.335.refs_1_), channel_id=1, source_target_pairs={{0,4},{2,6},{4,0},{6,2},{8,12},{10,14},{12,8},{14,10},{16,20},{18,... | collective-permute-start | bytes 3538952 | tf_op jit(solution)/shard_map/ppermute | solution.py:48
  325.3 9.6 %collective-permute-start.25 = (bf16[1,240,384]{2,1,0:T(8,128)(2,1)S(1)}, bf16[1,240,384]{2,1,0:T(8,128)(2,1)S(1)}, u32[]{:S(2)}, u32[]{:S(2)}) collective-permute-start(bf16[1,240,384]{2,1,0:T(8,128)(2,1)S(1)} %get-tuple-element.325), channel_id=1, source_target_pairs={{0,16},{2,18},{4,20},{6,22},{8,24},{10,26},{12,28},{14,30},{16,0},... | collective-permute-start | bytes 552968 | tf_op jit(solution)/shard_map/ppermute | solution.py:48
  327.9 24.5 %collective-permute-start.30 = (bf16[8,288,256]{2,1,0:T(8,128)(2,1)S(1)}, bf16[8,288,256]{2,1,0:T(8,128)(2,1)S(1)}, u32[]{:S(2)}, u32[]{:S(2)}) collective-permute-start(bf16[8,288,256]{2,1,0:T(8,128)(2,1)S(1)} %get-tuple-element.335.refs_1_), channel_id=1, source_target_pairs={{0,1},{1,0},{2,3},{3,2},{4,5},{5,4},{6,7},{7,6},{8,9},{9,8},{10,11... | collective-permute-start | bytes 3538952 | tf_op jit(solution)/shard_map/ppermute | solution.py:48
  327.9 19.9 %collective-permute-start.24 = (bf16[2,224,384]{2,1,0:T(8,128)(2,1)S(1)}, bf16[2,224,384]{2,1,0:T(8,128)(2,1)S(1)}, u32[]{:S(2)}, u32[]{:S(2)}) collective-permute-start(bf16[2,224,384]{2,1,0:T(8,128)(2,1)S(1)} %get-tuple-element.323), channel_id=1, source_target_pairs={{0,8},{2,10},{4,12},{6,14},{8,0},{10,2},{12,4},{14,6},{16,24},{18,... | collective-permute-start | bytes 1032200 | tf_op jit(solution)/shard_map/ppermute | solution.py:48
  334.9 16.1 %collective-permute-start.32 = (bf16[1,240,384]{2,1,0:T(8,128)(2,1)S(1)}, bf16[1,240,384]{2,1,0:T(8,128)(2,1)S(1)}, u32[]{:S(2)}, u32[]{:S(2)}) collective-permute-start(bf16[1,240,384]{2,1,0:T(8,128)(2,1)S(1)} %get-tuple-element.336.refs_0_), channel_id=1, source_target_pairs={{0,16},{2,18},{4,20},{6,22},{8,24},{10,26},{12,28},{14,30},{16,0},... | collective-permute-start | bytes 552968 | tf_op jit(solution)/shard_map/ppermute | solution.py:48
  336.4 14.2 %collective-permute-start.33 = (bf16[1,240,384]{2,1,0:T(8,128)(2,1)S(1)}, bf16[1,240,384]{2,1,0:T(8,128)(2,1)S(1)}, u32[]{:S(2)}, u32[]{:S(2)}) collective-permute-start(bf16[1,240,384]{2,1,0:T(8,128)(2,1)S(1)} %get-tuple-element.338), channel_id=1, source_target_pairs={{0,16},{2,18},{4,20},{6,22},{8,24},{10,26},{12,28},{14,30},{16,0},... | collective-permute-start | bytes 552968 | tf_op jit(solution)/shard_map/ppermute | solution.py:48
  347.9 15.3 %collective-permute-start.28 = (bf16[1,224,384]{2,1,0:T(8,128)(2,1)S(1)}, bf16[1,224,384]{2,1,0:T(8,128)(2,1)S(1)}, u32[]{:S(2)}, u32[]{:S(2)}) collective-permute-start(bf16[1,224,384]{2,1,0:T(8,128)(2,1)S(1)} %get-tuple-element.334), channel_id=1, source_target_pairs={{0,16},{2,18},{4,20},{6,22},{8,24},{10,26},{12,28},{14,30},{16,0},... | collective-permute-start | bytes 516104 | tf_op jit(solution)/shard_map/ppermute | solution.py:48
  350.7 20.1 %collective-permute-start.35 = (bf16[1,240,384]{2,1,0:T(8,128)(2,1)S(1)}, bf16[1,240,384]{2,1,0:T(8,128)(2,1)S(1)}, u32[]{:S(2)}, u32[]{:S(2)}) collective-permute-start(bf16[1,240,384]{2,1,0:T(8,128)(2,1)S(1)} %get-tuple-element.344.refs_0_), channel_id=1, source_target_pairs={{0,16},{2,18},{4,20},{6,22},{8,24},{10,26},{12,28},{14,30},{16,0},... | collective-permute-start | bytes 552968 | tf_op jit(solution)/shard_map/ppermute | solution.py:48
  351.0 12.3 %collective-permute-start.36 = (bf16[2,240,384]{2,1,0:T(8,128)(2,1)S(1)}, bf16[2,240,384]{2,1,0:T(8,128)(2,1)S(1)}, u32[]{:S(2)}, u32[]{:S(2)}) collective-permute-start(bf16[2,240,384]{2,1,0:T(8,128)(2,1)S(1)} %get-tuple-element.345.refs_0_), channel_id=1, source_target_pairs={{0,2},{2,0},{4,6},{6,4},{8,10},{10,8},{12,14},{14,12},{16,18},{18,... | collective-permute-start | bytes 1105928 | tf_op jit(solution)/shard_map/ppermute | solution.py:48
  363.3 11.2 %collective-permute-start.34 = (bf16[1,224,384]{2,1,0:T(8,128)(2,1)S(1)}, bf16[1,224,384]{2,1,0:T(8,128)(2,1)S(1)}, u32[]{:S(2)}, u32[]{:S(2)}) collective-permute-start(bf16[1,224,384]{2,1,0:T(8,128)(2,1)S(1)} %get-tuple-element.343.refs_0_), channel_id=1, source_target_pairs={{0,16},{2,18},{4,20},{6,22},{8,24},{10,26},{12,28},{14,30},{16,0},... | collective-permute-start | bytes 516104 | tf_op jit(solution)/shard_map/ppermute | solution.py:48
  370.9 10.6 %collective-permute-start.39 = (bf16[2,240,384]{2,1,0:T(8,128)(2,1)S(1)}, bf16[2,240,384]{2,1,0:T(8,128)(2,1)S(1)}, u32[]{:S(2)}, u32[]{:S(2)}) collective-permute-start(bf16[2,240,384]{2,1,0:T(8,128)(2,1)S(1)} %get-tuple-element.351.refs_0_), channel_id=1, source_target_pairs={{0,2},{2,0},{4,6},{6,4},{8,10},{10,8},{12,14},{14,12},{16,18},{18,... | collective-permute-start | bytes 1105928 | tf_op jit(solution)/shard_map/ppermute | solution.py:48
  371.4 18.1 %collective-permute-start.38 = (bf16[4,240,384]{2,1,0:T(8,128)(2,1)S(1)}, bf16[4,240,384]{2,1,0:T(8,128)(2,1)S(1)}, u32[]{:S(2)}, u32[]{:S(2)}) collective-permute-start(bf16[4,240,384]{2,1,0:T(8,128)(2,1)S(1)} %get-tuple-element.350.refs_0_), channel_id=1, source_target_pairs={{0,4},{2,6},{4,0},{6,2},{8,12},{10,14},{12,8},{14,10},{16,20},{18,... | collective-permute-start | bytes 2211848 | tf_op jit(solution)/shard_map/ppermute | solution.py:48
  374.5 15.2 %collective-permute-start.37 = (bf16[2,224,384]{2,1,0:T(8,128)(2,1)S(1)}, bf16[2,224,384]{2,1,0:T(8,128)(2,1)S(1)}, u32[]{:S(2)}, u32[]{:S(2)}) collective-permute-start(bf16[2,224,384]{2,1,0:T(8,128)(2,1)S(1)} %get-tuple-element.349.refs_0_), channel_id=1, source_target_pairs={{0,8},{2,10},{4,12},{6,14},{8,0},{10,2},{12,4},{14,6},{16,24},{18,... | collective-permute-start | bytes 1032200 | tf_op jit(solution)/shard_map/ppermute | solution.py:48
  381.5 19.8 %collective-permute-start.41 = (bf16[4,240,384]{2,1,0:T(8,128)(2,1)S(1)}, bf16[4,240,384]{2,1,0:T(8,128)(2,1)S(1)}, u32[]{:S(2)}, u32[]{:S(2)}) collective-permute-start(bf16[4,240,384]{2,1,0:T(8,128)(2,1)S(1)} %get-tuple-element.356.refs_0_), channel_id=1, source_target_pairs={{0,8},{2,10},{4,12},{6,14},{8,0},{10,2},{12,4},{14,6},{16,24},{18,... | collective-permute-start | bytes 2211848 | tf_op jit(solution)/shard_map/ppermute | solution.py:48
  389.8 16.3 %collective-permute-start.40 = (bf16[4,224,384]{2,1,0:T(8,128)(2,1)S(1)}, bf16[4,224,384]{2,1,0:T(8,128)(2,1)S(1)}, u32[]{:S(2)}, u32[]{:S(2)}) collective-permute-start(bf16[4,224,384]{2,1,0:T(8,128)(2,1)S(1)} %get-tuple-element.355.refs_0_), channel_id=1, source_target_pairs={{0,4},{2,6},{4,0},{6,2},{8,12},{10,14},{12,8},{14,10},{16,20},{18,... | collective-permute-start | bytes 2064392 | tf_op jit(solution)/shard_map/ppermute | solution.py:48
  391.4 40.6 %collective-permute-start.45 = (bf16[8,240,384]{2,1,0:T(8,128)(2,1)S(1)}, bf16[8,240,384]{2,1,0:T(8,128)(2,1)S(1)}, u32[]{:S(2)}, u32[]{:S(2)}) collective-permute-start(bf16[8,240,384]{2,1,0:T(8,128)(2,1)S(1)} %get-tuple-element.360.refs_1_), channel_id=1, source_target_pairs={{0,8},{2,10},{4,12},{6,14},{8,0},{10,2},{12,4},{14,6},{16,24},{18,... | collective-permute-start | bytes 4423688 | tf_op jit(solution)/shard_map/ppermute | solution.py:48
  406.2 30.1 %collective-permute-start.42 = (bf16[8,224,384]{2,1,0:T(8,128)(2,1)S(1)}, bf16[8,224,384]{2,1,0:T(8,128)(2,1)S(1)}, u32[]{:S(2)}, u32[]{:S(2)}) collective-permute-start(bf16[8,224,384]{2,1,0:T(8,128)(2,1)S(1)} %get-tuple-element.359.refs_1_), channel_id=1, source_target_pairs={{0,2},{2,0},{4,6},{6,4},{8,10},{10,8},{12,14},{14,12},{16,18},{18,... | collective-permute-start | bytes 4128776 | tf_op jit(solution)/shard_map/ppermute | solution.py:48
  407.8 28.5 %collective-permute-start.46 = (bf16[8,240,384]{2,1,0:T(8,128)(2,1)S(1)}, bf16[8,240,384]{2,1,0:T(8,128)(2,1)S(1)}, u32[]{:S(2)}, u32[]{:S(2)}) collective-permute-start(bf16[8,240,384]{2,1,0:T(8,128)(2,1)S(1)} %get-tuple-element.360.refs_1_), channel_id=1, source_target_pairs={{0,1},{1,0},{2,3},{3,2},{4,5},{5,4},{6,7},{7,6},{8,9},{9,8},{10,11... | collective-permute-start | bytes 4423688 | tf_op jit(solution)/shard_map/ppermute | solution.py:48
  407.8 34.7 %collective-permute-start.48 = (bf16[8,240,384]{2,1,0:T(8,128)(2,1)S(1)}, bf16[8,240,384]{2,1,0:T(8,128)(2,1)S(1)}, u32[]{:S(2)}, u32[]{:S(2)}) collective-permute-start(bf16[8,240,384]{2,1,0:T(8,128)(2,1)S(1)} %get-tuple-element.367.refs_1_), channel_id=1, source_target_pairs={{0,4},{2,6},{4,0},{6,2},{8,12},{10,14},{12,8},{14,10},{16,20},{18,... | collective-permute-start | bytes 4423688 | tf_op jit(solution)/shard_map/ppermute | solution.py:48
  432.0 10.5 %collective-permute-start.47 = (bf16[8,240,384]{2,1,0:T(8,128)(2,1)S(1)}, bf16[8,240,384]{2,1,0:T(8,128)(2,1)S(1)}, u32[]{:S(2)}, u32[]{:S(2)}) collective-permute-start(bf16[8,240,384]{2,1,0:T(8,128)(2,1)S(1)} %collective-permute-done.45.refs_2_), channel_id=1, source_target_pairs={{0,1},{1,0},{2,3},{3,2},{4,5},{5,4},{6,7},{7,6},{8,9},{9,8},{10,11... | collective-permute-start | bytes 4423688 | tf_op jit(solution)/shard_map/ppermute | solution.py:48
  432.0 15.4 %collective-permute-start.43 = (bf16[8,224,384]{2,1,0:T(8,128)(2,1)S(1)}, bf16[8,224,384]{2,1,0:T(8,128)(2,1)S(1)}, u32[]{:S(2)}, u32[]{:S(2)}) collective-permute-start(bf16[8,224,384]{2,1,0:T(8,128)(2,1)S(1)} %get-tuple-element.359.refs_1_), channel_id=1, source_target_pairs={{0,1},{1,0},{2,3},{3,2},{4,5},{5,4},{6,7},{7,6},{8,9},{9,8},{10,11... | collective-permute-start | bytes 4128776 | tf_op jit(solution)/shard_map/ppermute | solution.py:48
  436.3 11.2 %collective-permute-start.44 = (bf16[8,224,384]{2,1,0:T(8,128)(2,1)S(1)}, bf16[8,224,384]{2,1,0:T(8,128)(2,1)S(1)}, u32[]{:S(2)}, u32[]{:S(2)}) collective-permute-start(bf16[8,224,384]{2,1,0:T(8,128)(2,1)S(1)} %collective-permute-done.42.refs_2_), channel_id=1, source_target_pairs={{0,1},{1,0},{2,3},{3,2},{4,5},{5,4},{6,7},{7,6},{8,9},{9,8},{10,11... | collective-permute-start | bytes 4128776 | tf_op jit(solution)/shard_map/ppermute | solution.py:48
  436.3 18.4 %collective-permute-start.49 = (bf16[8,240,384]{2,1,0:T(8,128)(2,1)S(1)}, bf16[8,240,384]{2,1,0:T(8,128)(2,1)S(1)}, u32[]{:S(2)}, u32[]{:S(2)}) collective-permute-start(bf16[8,240,384]{2,1,0:T(8,128)(2,1)S(1)} %get-tuple-element.367.refs_1_), channel_id=1, source_target_pairs={{0,1},{1,0},{2,3},{3,2},{4,5},{5,4},{6,7},{7,6},{8,9},{9,8},{10,11... | collective-permute-start | bytes 4423688 | tf_op jit(solution)/shard_map/ppermute | solution.py:48
  442.5 12.2 %collective-permute-start.50 = (bf16[8,240,384]{2,1,0:T(8,128)(2,1)S(1)}, bf16[8,240,384]{2,1,0:T(8,128)(2,1)S(1)}, u32[]{:S(2)}, u32[]{:S(2)}) collective-permute-start(bf16[8,240,384]{2,1,0:T(8,128)(2,1)S(1)} %collective-permute-done.48.refs_2_), channel_id=1, source_target_pairs={{0,1},{1,0},{2,3},{3,2},{4,5},{5,4},{6,7},{7,6},{8,9},{9,8},{10,11... | collective-permute-start | bytes 4423688 | tf_op jit(solution)/shard_map/ppermute | solution.py:48
  (71 other events, 377.0 us)
where the time goes:
time: 464 us; the launch traced here: 460 us
  Pallas kernels  232 us (50%)
  waiting for transfers between devices  147 us (32%)
  starting transfers between devices  42.8 us (9%)
  local copies, waits for them, and re-layouts  31 us (7%)
  other arithmetic  5.54 us (1%)
    pallas_call x11, Pallas kernels, run(): pl.pallas_call(body, out_shape=[*out_shape, TOKEN], grid_spec=pltpu.Prefe...  196 us
    ppermute x51, waiting for transfers between devices, across(): return lax.ppermute(value, axis, [(i, i ^ 1 << bit) for i in range(count)])  147 us
    ppermute x51, starting transfers between devices, across(): return lax.ppermute(value, axis, [(i, i ^ 1 << bit) for i in range(count)])  42.8 us
    pallas_call x36, Pallas kernels, run_small(): pl.pallas_call(body, out_shape=[*out_shape, TOKEN], in_specs=in_specs, ou...  35.8 us
    unnamed x136, local copies, waits for them, and re-layouts  25.9 us
  transfers between devices with their start and end apart: 51, of which 23 were waited for; matrix products, arithmetic and copies ran while one was open for 2% of the time, Pallas kernels for 21%

commit v1 on v0

--- a/solution.py
+++ b/solution.py
@@ -11,9 +11,9 @@
 HD = 16
 TILE = 256
 VMEM_LIMIT = 60 * 1024 * 1024
-DEC_BITS = (1, 2, 0, 3)
-ENC_BITS = ((2, 1, 0, 3), (1, 2, 0, 3), (0, 1, 2, 3))
-STEPS = "dcadbdacbdacdbacbdadcabcbacbcacbacb"
+DEC_BITS = ((1, 0, 2, 3), (0, 1, 2, 3))
+ENC_BITS = (((2, 0, 1, 3), (1, 2, 0, 3)), ((1, 0, 2, 3), (0, 2, 1, 3)), ((0, 1, 2, 3), (1, 0, 2, 3)))
+STEPS = "abdcabdcabdcabdcabdcabdcabdcabcabcc"
 SHORT = 512
 WEIGHT_LIMIT = 40 * 1024 * 1024
 SMALL_LIMIT = 24 * 1024 * 1024
@@ -55,6 +55,12 @@
 
 
 TOKEN = jax.ShapeDtypeStruct((8, 128), jnp.float32)
+
+
+def across_bits(value, bits):
+    count, cores = lax.axis_size("dp"), lax.axis_size("blk")
+    pairs = [(i * cores + b, (i ^ (1 << bits[b])) * cores + b) for i in range(count) for b in range(cores)]
+    return lax.ppermute(value, ("dp", "blk"), pairs)
 
 
 class Order:
@@ -88,14 +94,17 @@
         self.token = results[-1]
         return results[:-1]
 
-    def run_small(self, kernel, name, operands, out_shape, scalars=None, out_specs=None, scratch=()):
-        micros = 40.0 if self.smalls < 8 else 4.0
+    def run_small(self, kernel, name, operands, out_shape, scalars=None, out_specs=None, scratch=(), earlier=()):
+        micros = 12.0 if self.smalls < 8 else 4.0
         self.smalls += 1
         count, outs = len(operands), len(out_shape)
         in_specs = [pl.BlockSpec(memory_space=pltpu.VMEM)] * count
         first = []
         if scalars is not None:
             in_specs, first = [pl.BlockSpec(memory_space=pltpu.SMEM), *in_specs], [scalars]
+        aliases = {len(in_specs) + index: index for index in range(len(earlier))}
+        in_specs = [*in_specs, *[pl.BlockSpec(memory_space=pl.ANY)] * len(earlier)]
+        operands, count = [*operands, *earlier], count + len(earlier)
         if self.token is not None:
             in_specs = [*in_specs, pl.BlockSpec(memory_space=pl.ANY)]
             operands = [*operands, self.token]
@@ -112,6 +121,7 @@
             in_specs=in_specs,
             out_specs=[*out_specs, pl.BlockSpec(memory_space=pl.ANY)],
             scratch_shapes=list(scratch),
+            input_output_aliases=aliases,
             compiler_params=pltpu.CompilerParams(vmem_limit_bytes=SMALL_LIMIT),
             cost_estimate=cost(micros),
             name=name,
@@ -130,7 +140,8 @@
     def __init__(self, order, bits, spots, tiles, entries, short=()):
         self.order, self.run, self.entries = order, order.run, entries
         self.shards = min(16, lax.axis_size("dp"))
-        self.bits = [bit for bit in bits if bit < bits_of(self.shards)]
+        self.bits = [[bit for bit in each if bit < bits_of(self.shards)] for each in bits]
+        self.stages = len(self.bits[0])
         self.spots, self.tiles = spots, tiles
         self.width = max(entry.width for entry in entries)
         self.firsts, self.bases, first, base = [], [], 0, 0
@@ -151,11 +162,23 @@
     def size(self, count):
         return 2 * count * self.rows * self.width
 
-    def spot_of(self, index):
-        spot = jnp.int32(0)
-        for at, bit in enumerate(self.bits):
-            spot = spot | ((lax.shift_right_logical(index, bit) & 1) << (len(self.bits) - 1 - at))
-        return spot
+    def spot_of(self, index, core):
+        spots = []
+        for bits in self.bits:
+            spot = jnp.int32(0)
+            for at, bit in enumerate(bits):
+                spot = spot | ((lax.shift_right_logical(index, bit) & 1) << (len(bits) - 1 - at))
+            spots.append(spot)
+        return jnp.where(core == 0, *spots)
+
+    def index_of(self, spot, core):
+        indices = []
+        for bits in self.bits:
+            index = jnp.int32(0)
+            for at, bit in enumerate(bits):
+                index = index | ((lax.shift_right_logical(spot, len(bits) - 1 - at) & 1) << bit)
+            indices.append(index)
+        return jnp.where(core == 0, *indices)
 
     def weigh(self):
         entries, shards, width = self.entries, self.shards, self.width
@@ -171,19 +194,19 @@
             def block(ref):
                 return ref[0] if entry.counted else ref[...]
 
-            def put(out_ref, value):
+            def put(out_ref, value, core):
                 value = value.astype(BF16)
                 if entry.kind == "wide":
                     at = pl.ds(pl.multiple_of(offset + unit * r, 16), r)
                     for shard in range(shards):
-                        target = self.spot_of(lax.bitwise_xor(jnp.int32(shard), spot))
+                        target = self.spot_of(lax.bitwise_xor(jnp.int32(shard), spot), core)
                         out_ref[target, at, :span] = value[shard * r : (shard + 1) * r]
                         if span < width:
                             out_ref[target, at, span:] = jnp.zeros((r, width - span), BF16)
                 else:
                     each, tall = shards // n, n * r
                     for inner in range(each):
-                        target = self.spot_of(lax.bitwise_xor(unit * each + inner, spot))
+                        target = self.spot_of(lax.bitwise_xor(unit * each + inner, spot), core)
                         out_ref[target, offset : offset + tall, :span] = value[inner * tall : (inner + 1) * tall]
 
             def turn():
@@ -221,18 +244,18 @@
 
             for flip, rhs_ref, out_ref in ((1, refs[1], sent_ref), (0, refs[2], kept_ref)):
                 if not entry.counted:
-                    put(out_ref, product(rhs_ref))
+                    put(out_ref, product(rhs_ref), half ^ flip)
                     continue
 
                 @pl.when(live == 1)
-                def _(rhs_ref=rhs_ref, out_ref=out_ref):
-                    put(out_ref, product(rhs_ref))
+                def _(flip=flip, rhs_ref=rhs_ref, out_ref=out_ref):
+                    put(out_ref, product(rhs_ref), half ^ flip)
 
                 @pl.when(live > 1)
                 def _(flip=flip, rhs_ref=rhs_ref, out_ref=out_ref):
                     total[:height, :span] = product(rhs_ref)
                     add_rest(flip)
-                    put(out_ref, total[:height, :span])
+                    put(out_ref, total[:height, :span], half ^ flip)
 
         starts, in_specs, operands = [], [], []
         for first, entry in zip(self.firsts, entries):
@@ -285,7 +308,7 @@
                     first_row = row_s[:, pl.ds(pl.multiple_of(at, LANES), width)]
                     next_row = row_s[:, pl.ds(pl.multiple_of(at + width, LANES), width)]
                     value = jnp.where(row == 0, first_row, jnp.where((row == 1) & (lane < SHORT - width), next_row, 0.0))
-                    target = self.spot_of(lax.bitwise_xor(jnp.int32(shard), spot))
+                    target = self.spot_of(lax.bitwise_xor(jnp.int32(shard), spot), half ^ flip)
                     out_ref[target, base : base + 16, :] = value.astype(BF16)
 
         def kernel(meta, *refs):
@@ -319,21 +342,21 @@
                 pltpu.SemaphoreType.DMA((2,)),
             ]
             + [pltpu.VMEM((1, (2 * shards + 2) * SHORT), F32)] * bool(self.short),
-            micros=40.0,
+            micros=6.0,
             steps=self.steps,
             limit=WEIGHT_LIMIT,
         )
         self.terms = (kept, across(sent, "blk", 0))
-        self.due, self.stage = list(self.bits), 0
+        self.due, self.stage = list(zip(*self.bits)), 0
 
     def step(self):
-        bits = len(self.bits)
-        for last, step in ((bits, self.halve), (bits + 1, self.own), (2 * bits, self.join), (2 * bits + 1, self.finish)):
+        bits = self.stages
+        for last, step in ((bits, self.halve), (bits + 1, self.own), (2 * bits, self.join), (2 * bits + 1, self.place_first)):
             if self.stage < last:
                 self.stage += 1
                 step()
                 return
-        self.placed = self.place()
+        self.placed = self.place(1, self.half_placed)
 
     def halve(self):
         bit = self.due.pop(0)
@@ -352,7 +375,7 @@
         sent, stay = self.order.run_small(
             kernel, "halve", [first, second], [self.shaped(count)] * 2
         )
-        self.terms = (stay, across(sent, "dp", bit))
+        self.terms = (stay, across_bits(sent, bit))
 
     def own(self):
         def kernel(a_ref, b_ref, out_ref):
@@ -364,12 +387,14 @@
         total = add(*self.terms)
         for bit in range(bits_of(self.shards), bits_of(lax.axis_size("dp"))):
             total = add(total, across(total, "dp", bit))
-        self.due = list(reversed(self.bits))
+        self.due = list(reversed(list(zip(*self.bits))))
         self.spread(total)
 
     def spread(self, held):
         bit = self.due.pop(0)
-        self.held = (held, across(held, "dp", bit))
+        self.held = (held, across_bits(held, bit))
+        if not self.due:
+            self.other = [across(held, "blk", 0)]
 
     def join(self):
         count = self.held[0].shape[0]
@@ -383,83 +408,86 @@
         )
         self.spread(held)
 
-    def finish(self):
-        self.other = [across(held, "blk", 0) for held in self.held]
-
-    def place(self):
-        entries, shards, bits, slots = self.entries, self.shards, self.bits, 4
+    def place_first(self):
+        self.half_placed = self.place(0, [])
+        self.other.append(across(self.held[1], "blk", 0))
+
+    def place(self, part, earlier):
+        entries, shards, slots = self.entries, self.shards, 4
         half_count = shards // 2
-        heights = [entry.r if entry.kind == "wide" else entry.n * entry.r for entry in entries]
+        sizes = [
+            (entry.r, entry.n * entry.width) if entry.kind == "wide" else (entry.n * entry.r, entry.width) for entry in entries
+        ]
         more = bool(self.short)
         count = len(entries) + more
 
         def kernel(meta, *refs):
-            sources = refs[:4]
-            outs, stages, sems = refs[4 : 4 + count], refs[4 + count : 4 + 2 * count], refs[-1]
+            sources, refs = refs[:2], refs[2 + len(earlier) :]
+            outs, stages, sems = refs[:count], refs[count : 2 * count], refs[-1]
             side = meta[1]
 
-            def copies(slot, row_block):
+            def copies(slot, shard, which):
                 pairs = [
-                    (stage.at[slot], out_ref.at[pl.ds(pl.multiple_of(row_block * height, 8), height), :])
-                    for stage, out_ref, height in zip(stages, outs, heights)
+                    (
+                        stage.at[slot],
+                        out_ref.at[
+                            pl.ds(pl.multiple_of(shard * height, 8), height), pl.ds(pl.multiple_of(which * size, LANES), size)
+                        ],
+                    )
+                    for stage, out_ref, (height, size) in zip(stages, outs, sizes)
                 ]
                 if more:
-                    pairs += [(stages[-1].at[slot, which], outs[-1].at[which * shards + row_block]) for which in range(2)]
+                    pairs.append((stages[-1].at[slot], outs[-1].at[which * shards + shard]))
                 return [pltpu.make_async_copy(*pair, sems.at[index, slot]) for index, pair in enumerate(pairs)]
 
-            for upper in range(2):
-                mine, other = sources[upper], sources[2 + upper]
-
-                def one(index, carry, upper=upper, mine=mine, other=other):
-                    step = upper * half_count + index
+            for turn, source in enumerate(sources):
+                which = side ^ turn
+
+                def one(index, carry, turn=turn, source=source, which=which):
+                    step = turn * half_count + index
                     slot = lax.rem(step, slots)
 
                     @pl.when(step >= slots)
                     def _():
-                        for copy in copies(slot, 0):
+                        for copy in copies(slot, 0, 0):
                             copy.wait()
 
                     for entry, offset, stage in zip(entries, self.bases, stages):
                         span = entry.width
-                        for which, source in ((side, mine), (1 - side, other)):
-                            for unit in range(entry.n):
-                                row = offset + unit * entry.r
-                                value = source[index, row : row + entry.r, :span].astype(F32)
-                                if entry.kind == "wide":
-                                    at = pl.ds(pl.multiple_of((which * entry.n + unit) * span, LANES), span)
-                                    stage[slot, :, at] = value
-                                else:
-                                    at = pl.ds(pl.multiple_of(which * span, LANES), span)
-                                    stage[slot, unit * entry.r : (unit + 1) * entry.r, at] = value
+                        for unit in range(entry.n):
+                            row = offset + unit * entry.r
+                            value = source[index, row : row + entry.r, :span].astype(F32)
+                            if entry.kind == "wide":
+                                stage[slot, :, unit * span : (unit + 1) * span] = value
+                            else:
+                                stage[slot, unit * entry.r : (unit + 1) * entry.r, :] = value
                     if more:
-                        for which, source in ((side, mine), (1 - side, other)):
-                            value = source[index, self.short_base : self.short_base + 16, :].astype(F32)
-                            for at in range(SHORT // LANES):
-                                row, lane = divmod(at * LANES, self.width)
-                                stages[-1][slot, which, at : at + 1, :] = value[row : row + 1, lane : lane + LANES]
-                    shard = jnp.int32(0)
-                    for at, bit in enumerate(bits):
-                        shard = shard | ((lax.shift_right_logical(step, len(bits) - 1 - at) & 1) << bit)
-                    for copy in copies(slot, lax.bitwise_xor(shard, meta[0])):
+                        value = source[index, self.short_base : self.short_base + 16, :].astype(F32)
+                        for at in range(SHORT // LANES):
+                            row, lane = divmod(at * LANES, self.width)
+                            stages[-1][slot, at : at + 1, :] = value[row : row + 1, lane : lane + LANES]
+                    shard = lax.bitwise_xor(self.index_of(part * half_count + index, which), meta[0])
+                    for copy in copies(slot, shard, which):
                         copy.start()
                     return carry
 
                 lax.fori_loop(0, half_count, one, 0)
             for step in range(max(shards - slots, 0), shards):
-                for copy in copies(step % slots, 0):
+                for copy in copies(step % slots, 0, 0):
                     copy.wait()
 
         return self.order.run_small(
             kernel,
             "place_shards",
-            [self.held[0], self.held[1], *self.other],
+            [self.held[part], self.other[part]],
             [jax.ShapeDtypeStruct(entry.shape, jnp.float32) for entry in entries]
             + [jax.ShapeDtypeStruct((2 * shards, 8, LANES), jnp.float32)] * more,
             scalars=self.spots,
             out_specs=[pl.BlockSpec(memory_space=pl.ANY)] * count,
-            scratch=[pltpu.VMEM((slots, height, entry.shape[1]), F32) for height, entry in zip(heights, entries)]
-            + [pltpu.VMEM((slots, 2, 8, LANES), F32)] * more
-            + [pltpu.SemaphoreType.DMA((count + more, slots))],
+            scratch=[pltpu.VMEM((slots, *size), F32) for size in sizes]
+            + [pltpu.VMEM((slots, 8, LANES), F32)] * more
+            + [pltpu.SemaphoreType.DMA((count, slots))],
+            earlier=earlier,
         )
 
 
@@ -1097,7 +1125,7 @@
         [live_tile(3 * width), out_whole((rows, width))] + [out_whole((1, width))] * 2,
         [shaped(rows, 3 * width, BF16), shaped(rows, width, BF16)] + [shaped(1, width, F32)] * 2,
         [pltpu.VMEM((rows, width), F32)],
-        40.0,
+        8.0,
         steps,
     )
 

time: 464 us -> 460 us (level)
  waiting for transfers between devices: 147 us -> 114 us
  starting transfers between devices: 42.8 us -> 57 us
  Pallas kernels: 232 us -> 241 us
  local copies, waits for them, and re-layouts: 31 us -> 36.1 us
    ppermute x51 -> x19, waiting for transfers between devices: 147 us -> 7.53 us  [across(): return lax.ppermute(value, axis, [(i, i ^ 1 << bit) for i in range(count)])]
    ppermute x0 -> x32, waiting for transfers between devices: none -> 106 us  [across_bits(): return lax.ppermute(value, ('dp', 'blk'), pairs)]
    ppermute x0 -> x32, starting transfers between devices: none -> 53.3 us  [across_bits(): return lax.ppermute(value, ('dp', 'blk'), pairs)]
    ppermute x51 -> x19, starting transfers between devices: 42.8 us -> 3.62 us  [across(): return lax.ppermute(value, axis, [(i, i ^ 1 << bit) for i in range(count)])]
    pallas_call x36 -> x40, Pallas kernels: 35.8 us -> 45 us  [run_small(): pl.pallas_call(body, out_shape=[*out_shape, TOKEN], in_specs=in_specs, ou...]
    unnamed x136 -> x140, local copies, waits for them, and re-layouts: 25.9 us -> 31 us
  transfers between devices with their start and end apart: 51 -> 51, of which waited for: 23 -> 16; matrix products, arithmetic and copies ran while one was open for 2% -> 2% of each run, Pallas kernels for 21% -> 22%
where the time goes in v1:
time: 460 us; the launch traced here: 455 us
  Pallas kernels  241 us (52%)
  waiting for transfers between devices  114 us (25%)
  starting transfers between devices  57 us (12%)
  local copies, waits for them, and re-layouts  36.1 us (8%)
  other arithmetic  5.45 us (1%)
    pallas_call x11, Pallas kernels, run(): pl.pallas_call(body, out_shape=[*out_shape, TOKEN], grid_spec=pltpu.Prefe...  196 us
    ppermute x32, waiting for transfers between devices, across_bits(): return lax.ppermute(value, ('dp', 'blk'), pairs)  106 us
    ppermute x32, starting transfers between devices, across_bits(): return lax.ppermute(value, ('dp', 'blk'), pairs)  53.3 us
    pallas_call x40, Pallas kernels, run_small(): pl.pallas_call(body, out_shape=[*out_shape, TOKEN], in_specs=in_specs, ou...  45 us
    unnamed x140, local copies, waits for them, and re-layouts  31 us
  transfers between devices with their start and end apart: 51, of which 16 were waited for; matrix products, arithmetic and copies ran while one was open for 2% of the time, Pallas kernels for 22%

profile of v1, /device:TPU:0, one launch (start us, length us, event | category | flops | bytes accessed | tf_op | source)
XLA Modules:
  0.0 455.0 jit_solution(18194751356972939382)
XLA Ops:
  7.1 1.9 fusion.meta
  9.6 8.2 %enc_in.1 = (bf16[768,768]{1,0:T(8,128)(2,1)}, f32[16,768]{1,0:T(8,128)}, f32[16,768]{1,0:T(8,128)}, f32[768,16]{1,0:T(8,128)}, f32[16,768]{1,0:T(8,128)}, /*ind...) custom-call(s32[2]{0:T(128)} %fusion.meta, ...), custom_call_target="tpu_custom_call" | custom-call | flops 8049999872 | bytes 25200000 | tf_op jit(solution)/shard_map/enc_in/pallas_call | solution.py:84
  18.6 4.0 collective-permute-done.3.refs_3_.refs_6_
  24.1 20.0 %enc_main.1 = (bf16[768,768]{1,0:T(8,128)(2,1)}, f32[768,128]{1,0:T(8,128)}, f32[768,768]{1,0:T(8,128)}, bf16[768,768]{1,0:T(8,128)(2,1)}, bf16[768,3072]{1,0:T(...) custom-call(s32[2]{0:T(128)} %fusion.meta, ...), custom_call_target="tpu_custom_call" | custom-call | flops 23000000512 | bytes 72000000 | tf_op jit(solution)/shard_map/enc_main/pallas_call | solution.py:84
  44.1 7.4 %dec_in.1 = (f32[768,512]{1,0:T(8,128)}, bf16[768,512]{1,0:T(8,128)(2,1)}, bf16[768,512]{1,0:T(8,128)(2,1)}, bf16[768,1024]{1,0:T(8,128)(2,1)}, f32[8,128]{1,0:T(8,128)}) custom-call(s32[2]{0:T(128)} %fusion.meta, bf16[768,768]{1,0:T(8,128)(2,1)} %get-tuple-element.215.refs_0_, bf16[768,512]{1,0:T(8,128)(2,1)} %get-tuple-element.223.refs_1_, ...), custom_call_target="tpu_custom_call" | custom-call | flops 8049999872 | bytes 25200000 | tf_op jit(solution)/shard_map/dec_in/pallas_call | solution.py:84
  51.6 3.5 collective-permute-done.4.refs_3_
  56.2 94.6 %dec_main.1 = (bf16[768,512]{1,0:T(8,128)(2,1)}, bf16[768,512]{1,0:T(8,128)(2,1)}, bf16[768,512]{1,0:T(8,128)(2,1)}, bf16[768,2048]{1,0:T(8,128)(2,1)}, bf16[768...) custom-call(s32[2]{0:T(128)} %fusion.meta, ...), custom_call_target="tpu_custom_call" | custom-call | flops 109250002944 | bytes 342000000 | tf_op jit(solution)/shard_map/dec_main/pallas_call | solution.py:84
  151.1 1.9 copy-done.16
  153.0 1.9 copy-done.17
  159.0 8.0 %weight_grads.4 = (bf16[16,288,256]{2,1,0:T(8,128)(2,1)S(1)}, bf16[16,288,256]{2,1,0:T(8,128)(2,1)S(1)}, f32[8,128]{1,0:T(8,128)S(1)}) custom-call(s32[3]{0:T(128)S(1)} %pad_add_fusion.meta, bf16[768,512]{1,0:T(8,128)(2,1)S(1)} %copy-done.22, bf16[768,2048]{1,0:T(8,128)(2,1)S(1)} %copy-done.17, bf16[768,2048]{1,0:T(8,128)(2,1)S(1)} %copy-done.17, ...), custom_call_target="tpu_custom_call" | custom-call | flops 6899999744 | bytes 21600000 | tf_op jit(solution)/shard_map/weight_grads/pallas_call | solution.py:84
  169.4 8.1 %dec_head.1 = (bf16[768,1536]{1,0:T(8,128)(2,1)}, bf16[768,512]{1,0:T(8,128)(2,1)}, f32[1,512]{1,0:T(1,128)}, f32[1,512]{1,0:T(1,128)}, f32[1,512]{1,0:T(1,128)}, /*index=5*/f32[1,512]{1,0:T(1,128)}, f32[8,128]{1,0:T(8,128)}) custom-call(s32[2]{0:T(128)} %fusion.meta, f32[768,512]{1,0:T(8,128)} %get-tuple-element.227.refs_0_, ...), custom_call_target="tpu_custom_call" | custom-call | flops 46000001024 | bytes 144000000 | tf_op jit(solution)/shard_map/dec_head/pallas_call | solution.py:84
  179.8 2.3 halve.16
  183.7 2.6 collective-permute-start.8
  186.3 24.6 %enc_back.1 = (bf16[768,512]{1,0:T(8,128)(2,1)}, bf16[768,768]{1,0:T(8,128)(2,1)}, bf16[768,3072]{1,0:T(8,128)(2,1)}, bf16[768,768]{1,0:T(8,128)(2,1)}, f32[768,...) custom-call(s32[2]{0:T(128)} %fusion.meta, ...), custom_call_target="tpu_custom_call" | custom-call | flops 27599998976 | bytes 86400000 | tf_op jit(solution)/shard_map/enc_back/pallas_call | solution.py:84
  216.5 5.1 %weight_grads.5 = (bf16[16,240,384]{2,1,0:T(8,128)(2,1)S(1)}, bf16[16,240,384]{2,1,0:T(8,128)(2,1)S(1)}, f32[8,128]{1,0:T(8,128)S(1)}) custom-call(s32[3]{0:T(128)S(1)} %pad_add_fusion.meta, bf16[3,256,768]{2,1,0:T(8,128)(2,1)S(1)} %bitcast.48, bf16[3,256,3072]{2,1,0:T(8,128)(2,1)S(1)} %bitcast.36, bf16[3,256,3072]{2,1,0:T(8,128)(2,1)S(1)} %bitcast.37, ...), custom_call_target="tpu_custom_call" | custom-call | flops 6899999744 | bytes 21600000 | tf_op jit(solution)/shard_map/weight_grads/pallas_call | solution.py:84
  223.7 2.3 copy-done.1
  226.1 5.3 %weight_grads.6 = (bf16[16,240,384]{2,1,0:T(8,128)(2,1)S(1)}, bf16[16,240,384]{2,1,0:T(8,128)(2,1)S(1)}, f32[8,128]{1,0:T(8,128)S(1)}) custom-call(s32[3]{0:T(128)S(1)} %pad_add_fusion.meta, bf16[3,256,3072]{2,1,0:T(8,128)(2,1)S(1)} %bitcast.34, bf16[3,256,768]{2,1,0:T(8,128)(2,1)S(1)} %bitcast.50, bf16[3,256,768]{2,1,0:T(8,128)(2,1)S(1)} %bitcast.51, ...), custom_call_target="tpu_custom_call" | custom-call | flops 6899999744 | bytes 21600000 | tf_op jit(solution)/shard_map/weight_grads/pallas_call | solution.py:84
  238.2 8.3 %enc_head.1 = (bf16[768,2304]{1,0:T(8,128)(2,1)}, bf16[768,768]{1,0:T(8,128)(2,1)}, f32[1,768]{1,0:T(1,128)}, f32[1,768]{1,0:T(1,128)}, f32[8,128]{1,0:T(8,128)}) custom-call(s32[2]{0:T(128)} %fusion.meta, bf16[768,768]{1,0:T(8,128)(2,1)} %get-tuple-element.215.refs_0_, bf16[768,768]{1,0:T(8,128)(2,1)} %get-tuple-element.216.refs_0_.refs_1_, ...), custom_call_target="tpu_custom_call" | custom-call | flops 9200000000 | bytes 28800000 | tf_op jit(solution)/shard_map/enc_head/pallas_call | solution.py:84
  249.0 2.7 halve.19
  255.2 6.2 %weight_grads.7 = (bf16[16,224,384]{2,1,0:T(8,128)(2,1)S(1)}, bf16[16,224,384]{2,1,0:T(8,128)(2,1)S(1)}, f32[8,128]{1,0:T(8,128)S(1)}) custom-call(s32[3]{0:T(128)S(1)} %pad_add_fusion.meta, bf16[3,256,768]{2,1,0:T(8,128)(2,1)S(1)} %bitcast.42, bf16[3,256,2304]{2,1,0:T(8,128)(2,1)S(1)} %bitcast.39, bf16[3,256,2304]{2,1,0:T(8,128)(2,1)S(1)} %bitcast.40, ...), custom_call_target="tpu_custom_call" | custom-call | flops 6899999744 | bytes 21600000 | tf_op jit(solution)/shard_map/weight_grads/pallas_call | solution.py:84
  264.4 9.0 %collective-permute-done.14.refs_1_ = bf16[8,240,384]{2,1,0:T(8,128)(2,1)S(1)} collective-permute-done((bf16[8,240,384]{2,1,0:T(8,128)(2,1)S(1)}, bf16[8,240,384]{2,1,0:T(8,128)(2,1)S(1)}, u32[]{:S(2)}, u32[]{:S(2)}) %collective-permute-start.14) | collective-permute-done | bytes 1474592 | tf_op jit(solution)/shard_map/ppermute | solution.py:63
  276.8 2.6 collective-permute-start.17
  280.1 7.7 %collective-permute-done.18.refs_1_ = bf16[4,240,384]{2,1,0:T(8,128)(2,1)S(1)} collective-permute-done((bf16[4,240,384]{2,1,0:T(8,128)(2,1)S(1)}, bf16[4,240,384]{2,1,0:T(8,128)(2,1)S(1)}, u32[]{:S(2)}, u32[]{:S(2)}) %collective-permute-start.18) | collective-permute-done | bytes 737312 | tf_op jit(solution)/shard_map/ppermute | solution.py:63
  288.1 2.7 collective-permute-start.21
  292.4 16.9 %collective-permute-done.16.refs_1_ = bf16[8,224,384]{2,1,0:T(8,128)(2,1)S(1)} collective-permute-done((bf16[8,224,384]{2,1,0:T(8,128)(2,1)S(1)}, bf16[8,224,384]{2,1,0:T(8,128)(2,1)S(1)}, u32[]{:S(2)}, u32[]{:S(2)}) %collective-permute-start.16) | collective-permute-done | bytes 1376288 | tf_op jit(solution)/shard_map/ppermute | solution.py:63
  311.3 3.3 collective-permute-start.26
  314.8 5.8 %collective-permute-done.20.refs_1_ = bf16[4,224,384]{2,1,0:T(8,128)(2,1)S(1)} collective-permute-done((bf16[4,224,384]{2,1,0:T(8,128)(2,1)S(1)}, bf16[4,224,384]{2,1,0:T(8,128)(2,1)S(1)}, u32[]{:S(2)}, u32[]{:S(2)}) %collective-permute-start.20) | collective-permute-done | bytes 688160 | tf_op jit(solution)/shard_map/ppermute | solution.py:63
  320.8 3.8 collective-permute-done.27.refs_1_
  324.9 2.9 collective-permute-start.31
  327.8 3.4 collective-permute-start.24
  331.2 5.0 %collective-permute-start.29 = (bf16[4,288,256]{2,1,0:T(8,128)(2,1)S(1)}, bf16[4,288,256]{2,1,0:T(8,128)(2,1)S(1)}, u32[]{:S(2)}, u32[]{:S(2)}) collective-permute-start(bf16[4,288,256]{2,1,0:T(8,128)(2,1)S(1)} %get-tuple-element.350.refs_0_), channel_id=1, source_target_pairs={{0,2},{1,5},{2,0},{3,7},{4,6},{5,1},{6,4},{7,3},{8,10},{9,13},{10,... | collective-permute-start | bytes 1769480 | tf_op jit(solution)/shard_map/ppermute | solution.py:63
  336.3 3.3 collective-permute-done.24.refs_1_
  339.6 7.0 %collective-permute-start.28 = (bf16[1,224,384]{2,1,0:T(8,128)(2,1)S(1)}, bf16[1,224,384]{2,1,0:T(8,128)(2,1)S(1)}, u32[]{:S(2)}, u32[]{:S(2)}) collective-permute-start(bf16[1,224,384]{2,1,0:T(8,128)(2,1)S(1)} %get-tuple-element.349), channel_id=1, source_target_pairs={{0,16},{1,17},{2,18},{3,19},{4,20},{5,21},{6,22},{7,23},{8,24},{9,... | collective-permute-start | bytes 516104 | tf_op jit(solution)/shard_map/ppermute | solution.py:63
  346.7 2.5 collective-permute-start.34
  353.3 3.5 collective-permute-done.35.refs_1_
  359.0 10.4 %collective-permute-done.37.refs_1_ = bf16[8,288,256]{2,1,0:T(8,128)(2,1)S(1)} collective-permute-done((bf16[8,288,256]{2,1,0:T(8,128)(2,1)S(1)}, bf16[8,288,256]{2,1,0:T(8,128)(2,1)S(1)}, u32[]{:S(2)}, u32[]{:S(2)}) %collective-permute-start.37) | collective-permute-done | bytes 1179680 | tf_op jit(solution)/shard_map/ppermute | solution.py:63
  369.4 3.8 place_shards.8
  373.3 6.4 %collective-permute-done.40.refs_1_ = bf16[4,240,384]{2,1,0:T(8,128)(2,1)S(1)} collective-permute-done((bf16[4,240,384]{2,1,0:T(8,128)(2,1)S(1)}, bf16[4,240,384]{2,1,0:T(8,128)(2,1)S(1)}, u32[]{:S(2)}, u32[]{:S(2)}) %collective-permute-start.40) | collective-permute-done | bytes 737312 | tf_op jit(solution)/shard_map/ppermute | solution.py:63
  379.8 2.5 collective-permute-start.49
  384.8 3.8 place_shards.9
  388.6 18.4 %collective-permute-done.36.refs_1_ = bf16[2,224,384]{2,1,0:T(8,128)(2,1)S(1)} collective-permute-done((bf16[2,224,384]{2,1,0:T(8,128)(2,1)S(1)}, bf16[2,224,384]{2,1,0:T(8,128)(2,1)S(1)}, u32[]{:S(2)}, u32[]{:S(2)}) %collective-permute-start.36) | collective-permute-done | bytes 344096 | tf_op jit(solution)/shard_map/ppermute | solution.py:63
  408.9 4.0 place_shards.10
  412.9 3.9 place_shards.11
  419.1 17.5 %collective-permute-done.44.refs_1_ = bf16[8,224,384]{2,1,0:T(8,128)(2,1)S(1)} collective-permute-done((bf16[8,224,384]{2,1,0:T(8,128)(2,1)S(1)}, bf16[8,224,384]{2,1,0:T(8,128)(2,1)S(1)}, u32[]{:S(2)}, u32[]{:S(2)}) %collective-permute-start.44) | collective-permute-done | bytes 1376288 | tf_op jit(solution)/shard_map/ppermute | solution.py:63
  436.6 4.0 place_shards.12
  440.6 3.9 place_shards.13
  444.6 3.9 place_shards.14
  448.5 3.9 place_shards.15
  (261 shorter events, 68.5 us)
Async XLA Ops:
  2.5 6.5 %collective-permute-start.2 = (s32[1,768]{1,0:T(1,128)S(1)}, s32[1,768]{1,0:T(1,128)S(1)}, u32[]{:S(2)}, u32[]{:S(2)}) collective-permute-start(s32[1,768]{1,0:T(1,128)S(1)} %reshape.113.refs_3_), channel_id=1, source_target_pairs={{0,1},{1,0},{2,3},{3,2},{4,5},{5,4},{6,7},{7,6},{8,9},{9,8},{10,11... | collective-permute-start | bytes 9224 | tf_op jit(solution)/shard_map/ppermute | solution.py:48
  3.3 5.7 %collective-permute-start.1 = (s32[1,768]{1,0:T(1,128)S(1)}, s32[1,768]{1,0:T(1,128)S(1)}, u32[]{:S(2)}, u32[]{:S(2)}) collective-permute-start(s32[1,768]{1,0:T(1,128)S(1)} %reshape.112.refs_2_), channel_id=1, source_target_pairs={{0,1},{1,0},{2,3},{3,2},{4,5},{5,4},{6,7},{7,6},{8,9},{9,8},{10,11... | collective-permute-start | bytes 9224 | tf_op jit(solution)/shard_map/ppermute | solution.py:48
  150.8 18.5 %collective-permute-start.5 = (bf16[768,1024]{1,0:T(8,128)(2,1)}, bf16[768,1024]{1,0:T(8,128)(2,1)}, u32[]{:S(2)}, u32[]{:S(2)}) collective-permute-start(bf16[768,1024]{1,0:T(8,128)(2,1)} %get-tuple-element.236), channel_id=1, source_target_pairs={{0,1},{1,0},{2,3},{3,2},{4,5},{5,4},{6,7},{7,6},{8,9},{9,8},{10,11... | collective-permute-start | bytes 4718600 | tf_op jit(solution)/shard_map/ppermute | solution.py:48
  169.0 8.5 %collective-permute-start.6 = (bf16[16,288,256]{2,1,0:T(8,128)(2,1)S(1)}, bf16[16,288,256]{2,1,0:T(8,128)(2,1)}, u32[]{:S(2)}, u32[]{:S(2)}) collective-permute-start(bf16[16,288,256]{2,1,0:T(8,128)(2,1)S(1)} %get-tuple-element.251), channel_id=1, source_target_pairs={{0,1},{1,0},{2,3},{3,2},{4,5},{5,4},{6,7},{7,6},{8,9},{9,8},{10,11... | collective-permute-start | bytes 7077896 | tf_op jit(solution)/shard_map/ppermute | solution.py:48
  183.7 27.2 %collective-permute-start.8 = (bf16[8,288,256]{2,1,0:T(8,128)(2,1)S(1)}, bf16[8,288,256]{2,1,0:T(8,128)(2,1)S(1)}, u32[]{:S(2)}, u32[]{:S(2)}) collective-permute-start(bf16[8,288,256]{2,1,0:T(8,128)(2,1)S(1)} %get-tuple-element.262), channel_id=1, source_target_pairs={{0,4},{1,3},{2,6},{3,1},{4,0},{5,7},{6,2},{7,5},{8,12},{9,11},{10,... | collective-permute-start | bytes 3538952 | tf_op jit(solution)/shard_map/ppermute | solution.py:63
  223.2 9.8 %collective-permute-start.9 = (bf16[16,240,384]{2,1,0:T(8,128)(2,1)S(1)}, bf16[16,240,384]{2,1,0:T(8,128)(2,1)S(1)}, u32[]{:S(2)}, u32[]{:S(2)}) collective-permute-start(bf16[16,240,384]{2,1,0:T(8,128)(2,1)S(1)} %get-tuple-element.266), channel_id=1, source_target_pairs={{0,1},{1,0},{2,3},{3,2},{4,5},{5,4},{6,7},{7,6},{8,9},{9,8},{10,11... | collective-permute-start | bytes 8847368 | tf_op jit(solution)/shard_map/ppermute | solution.py:48
  223.3 14.9 %collective-permute-start.7 = (bf16[768,1536]{1,0:T(8,128)(2,1)}, bf16[768,1536]{1,0:T(8,128)(2,1)}, u32[]{:S(2)}, u32[]{:S(2)}) collective-permute-start(bf16[768,1536]{1,0:T(8,128)(2,1)} %get-tuple-element.256), channel_id=1, source_target_pairs={{0,1},{1,0},{2,3},{3,2},{4,5},{5,4},{6,7},{7,6},{8,9},{9,8},{10,11... | collective-permute-start | bytes 7077896 | tf_op jit(solution)/shard_map/ppermute | solution.py:48
  231.4 15.1 %collective-permute-start.11 = (bf16[16,240,384]{2,1,0:T(8,128)(2,1)S(1)}, bf16[16,240,384]{2,1,0:T(8,128)(2,1)}, u32[]{:S(2)}, u32[]{:S(2)}) collective-permute-start(bf16[16,240,384]{2,1,0:T(8,128)(2,1)S(1)} %get-tuple-element.298), channel_id=1, source_target_pairs={{0,1},{1,0},{2,3},{3,2},{4,5},{5,4},{6,7},{7,6},{8,9},{9,8},{10,11... | collective-permute-start | bytes 8847368 | tf_op jit(solution)/shard_map/ppermute | solution.py:48
  231.6 20.1 %collective-permute-start.10 = (bf16[4,288,256]{2,1,0:T(8,128)(2,1)S(1)}, bf16[4,288,256]{2,1,0:T(8,128)(2,1)}, u32[]{:S(2)}, u32[]{:S(2)}) collective-permute-start(bf16[4,288,256]{2,1,0:T(8,128)(2,1)S(1)} %get-tuple-element.296), channel_id=1, source_target_pairs={{0,2},{1,5},{2,0},{3,7},{4,6},{5,1},{6,4},{7,3},{8,10},{9,13},{10,... | collective-permute-start | bytes 1769480 | tf_op jit(solution)/shard_map/ppermute | solution.py:63
  236.6 24.9 %collective-permute-start.15 = (bf16[8,240,384]{2,1,0:T(8,128)(2,1)}, bf16[8,240,384]{2,1,0:T(8,128)(2,1)}, u32[]{:S(2)}, u32[]{:S(2)}) collective-permute-start(bf16[8,240,384]{2,1,0:T(8,128)(2,1)} %get-tuple-element.309), channel_id=1, source_target_pairs={{0,8},{1,5},{2,10},{3,7},{4,12},{5,1},{6,14},{7,3},{8,0},{9,13},{1... | collective-permute-start | bytes 4423688 | tf_op jit(solution)/shard_map/ppermute | solution.py:63
  253.5 21.0 %collective-permute-start.13 = (bf16[2,288,256]{2,1,0:T(8,128)(2,1)S(1)}, bf16[2,288,256]{2,1,0:T(8,128)(2,1)S(1)}, u32[]{:S(2)}, u32[]{:S(2)}) collective-permute-start(bf16[2,288,256]{2,1,0:T(8,128)(2,1)S(1)} %get-tuple-element.305), channel_id=1, source_target_pairs={{0,8},{1,9},{2,10},{3,11},{4,12},{5,13},{6,14},{7,15},{8,0},{9,1},... | collective-permute-start | bytes 884744 | tf_op jit(solution)/shard_map/ppermute | solution.py:63
  254.0 19.4 %collective-permute-start.14 = (bf16[8,240,384]{2,1,0:T(8,128)(2,1)S(1)}, bf16[8,240,384]{2,1,0:T(8,128)(2,1)S(1)}, u32[]{:S(2)}, u32[]{:S(2)}) collective-permute-start(bf16[8,240,384]{2,1,0:T(8,128)(2,1)S(1)} %get-tuple-element.307), channel_id=1, source_target_pairs={{0,4},{1,3},{2,6},{3,1},{4,0},{5,7},{6,2},{7,5},{8,12},{9,11},{10,... | collective-permute-start | bytes 4423688 | tf_op jit(solution)/shard_map/ppermute | solution.py:63
  261.4 13.1 %collective-permute-start.12 = (bf16[16,224,384]{2,1,0:T(8,128)(2,1)S(1)}, bf16[16,224,384]{2,1,0:T(8,128)(2,1)S(1)}, u32[]{:S(2)}, u32[]{:S(2)}) collective-permute-start(bf16[16,224,384]{2,1,0:T(8,128)(2,1)S(1)} %get-tuple-element.303), channel_id=1, source_target_pairs={{0,1},{1,0},{2,3},{3,2},{4,5},{5,4},{6,7},{7,6},{8,9},{9,8},{10,11... | collective-permute-start | bytes 8257544 | tf_op jit(solution)/shard_map/ppermute | solution.py:48
  263.3 16.6 %collective-permute-start.19 = (bf16[4,240,384]{2,1,0:T(8,128)(2,1)S(1)}, bf16[4,240,384]{2,1,0:T(8,128)(2,1)S(1)}, u32[]{:S(2)}, u32[]{:S(2)}) collective-permute-start(bf16[4,240,384]{2,1,0:T(8,128)(2,1)S(1)} %get-tuple-element.321), channel_id=1, source_target_pairs={{0,2},{1,9},{2,0},{3,11},{4,6},{5,13},{6,4},{7,15},{8,10},{9,1},{1... | collective-permute-start | bytes 2211848 | tf_op jit(solution)/shard_map/ppermute | solution.py:63
  273.8 14.1 %collective-permute-start.18 = (bf16[4,240,384]{2,1,0:T(8,128)(2,1)S(1)}, bf16[4,240,384]{2,1,0:T(8,128)(2,1)S(1)}, u32[]{:S(2)}, u32[]{:S(2)}) collective-permute-start(bf16[4,240,384]{2,1,0:T(8,128)(2,1)S(1)} %get-tuple-element.319), channel_id=1, source_target_pairs={{0,2},{1,9},{2,0},{3,11},{4,6},{5,13},{6,4},{7,15},{8,10},{9,1},{1... | collective-permute-start | bytes 2211848 | tf_op jit(solution)/shard_map/ppermute | solution.py:63
  275.3 34.0 %collective-permute-start.16 = (bf16[8,224,384]{2,1,0:T(8,128)(2,1)S(1)}, bf16[8,224,384]{2,1,0:T(8,128)(2,1)S(1)}, u32[]{:S(2)}, u32[]{:S(2)}) collective-permute-start(bf16[8,224,384]{2,1,0:T(8,128)(2,1)S(1)} %get-tuple-element.315), channel_id=1, source_target_pairs={{0,2},{1,5},{2,0},{3,7},{4,6},{5,1},{6,4},{7,3},{8,10},{9,13},{10,... | collective-permute-start | bytes 4128776 | tf_op jit(solution)/shard_map/ppermute | solution.py:63
  276.8 11.2 %collective-permute-start.17 = (bf16[1,288,256]{2,1,0:T(8,128)(2,1)S(1)}, bf16[1,288,256]{2,1,0:T(8,128)(2,1)S(1)}, u32[]{:S(2)}, u32[]{:S(2)}) collective-permute-start(bf16[1,288,256]{2,1,0:T(8,128)(2,1)S(1)} %get-tuple-element.317), channel_id=1, source_target_pairs={{0,16},{1,17},{2,18},{3,19},{4,20},{5,21},{6,22},{7,23},{8,24},{9,... | collective-permute-start | bytes 442376 | tf_op jit(solution)/shard_map/ppermute | solution.py:63
  288.1 26.6 %collective-permute-start.21 = (bf16[1,288,256]{2,1,0:T(8,128)(2,1)S(1)}, bf16[1,288,256]{2,1,0:T(8,128)(2,1)S(1)}, u32[]{:S(2)}, u32[]{:S(2)}) collective-permute-start(bf16[1,288,256]{2,1,0:T(8,128)(2,1)S(1)} %get-tuple-element.328.refs_0_), channel_id=1, source_target_pairs={{0,16},{1,17},{2,18},{3,19},{4,20},{5,21},{6,22},{7,23},{8,24},{9,... | collective-permute-start | bytes 442376 | tf_op jit(solution)/shard_map/ppermute | solution.py:63
  290.8 20.4 %collective-permute-start.22 = (bf16[2,240,384]{2,1,0:T(8,128)(2,1)S(1)}, bf16[2,240,384]{2,1,0:T(8,128)(2,1)S(1)}, u32[]{:S(2)}, u32[]{:S(2)}) collective-permute-start(bf16[2,240,384]{2,1,0:T(8,128)(2,1)S(1)} %get-tuple-element.330), channel_id=1, source_target_pairs={{0,8},{1,5},{2,10},{3,7},{4,12},{5,1},{6,14},{7,3},{8,0},{9,13},{1... | collective-permute-start | bytes 1105928 | tf_op jit(solution)/shard_map/ppermute | solution.py:63
  291.2 19.9 %collective-permute-start.23 = (bf16[2,240,384]{2,1,0:T(8,128)(2,1)S(1)}, bf16[2,240,384]{2,1,0:T(8,128)(2,1)S(1)}, u32[]{:S(2)}, u32[]{:S(2)}) collective-permute-start(bf16[2,240,384]{2,1,0:T(8,128)(2,1)S(1)} %get-tuple-element.332), channel_id=1, source_target_pairs={{0,4},{1,3},{2,6},{3,1},{4,0},{5,7},{6,2},{7,5},{8,12},{9,11},{10,... | collective-permute-start | bytes 1105928 | tf_op jit(solution)/shard_map/ppermute | solution.py:63
  309.6 11.0 %collective-permute-start.20 = (bf16[4,224,384]{2,1,0:T(8,128)(2,1)S(1)}, bf16[4,224,384]{2,1,0:T(8,128)(2,1)S(1)}, u32[]{:S(2)}, u32[]{:S(2)}) collective-permute-start(bf16[4,224,384]{2,1,0:T(8,128)(2,1)S(1)} %get-tuple-element.327), channel_id=1, source_target_pairs={{0,4},{1,3},{2,6},{3,1},{4,0},{5,7},{6,2},{7,5},{8,12},{9,11},{10,... | collective-permute-start | bytes 2064392 | tf_op jit(solution)/shard_map/ppermute | solution.py:63
  311.3 13.4 %collective-permute-start.26 = (bf16[1,240,384]{2,1,0:T(8,128)(2,1)S(1)}, bf16[1,240,384]{2,1,0:T(8,128)(2,1)S(1)}, u32[]{:S(2)}, u32[]{:S(2)}) collective-permute-start(bf16[1,240,384]{2,1,0:T(8,128)(2,1)S(1)} %get-tuple-element.341), channel_id=1, source_target_pairs={{0,16},{1,17},{2,18},{3,19},{4,20},{5,21},{6,22},{7,23},{8,24},{9,... | collective-permute-start | bytes 552968 | tf_op jit(solution)/shard_map/ppermute | solution.py:63
  314.6 10.0 %collective-permute-start.27 = (bf16[1,240,384]{2,1,0:T(8,128)(2,1)S(1)}, bf16[1,240,384]{2,1,0:T(8,128)(2,1)S(1)}, u32[]{:S(2)}, u32[]{:S(2)}) collective-permute-start(bf16[1,240,384]{2,1,0:T(8,128)(2,1)S(1)} %get-tuple-element.343), channel_id=1, source_target_pairs={{0,16},{1,17},{2,18},{3,19},{4,20},{5,21},{6,22},{7,23},{8,24},{9,... | collective-permute-start | bytes 552968 | tf_op jit(solution)/shard_map/ppermute | solution.py:63
  314.7 16.4 %collective-permute-start.25 = (bf16[2,288,256]{2,1,0:T(8,128)(2,1)S(1)}, bf16[2,288,256]{2,1,0:T(8,128)(2,1)S(1)}, u32[]{:S(2)}, u32[]{:S(2)}) collective-permute-start(bf16[2,288,256]{2,1,0:T(8,128)(2,1)S(1)} %get-tuple-element.339.refs_0_), channel_id=1, source_target_pairs={{0,8},{1,9},{2,10},{3,11},{4,12},{5,13},{6,14},{7,15},{8,0},{9,1},... | collective-permute-start | bytes 884744 | tf_op jit(solution)/shard_map/ppermute | solution.py:63
  324.8 21.9 %collective-permute-start.30 = (bf16[1,240,384]{2,1,0:T(8,128)(2,1)S(1)}, bf16[1,240,384]{2,1,0:T(8,128)(2,1)S(1)}, u32[]{:S(2)}, u32[]{:S(2)}) collective-permute-start(bf16[1,240,384]{2,1,0:T(8,128)(2,1)S(1)} %get-tuple-element.351.refs_0_), channel_id=1, source_target_pairs={{0,16},{1,17},{2,18},{3,19},{4,20},{5,21},{6,22},{7,23},{8,24},{9,... | collective-permute-start | bytes 552968 | tf_op jit(solution)/shard_map/ppermute | solution.py:63
  324.9 21.8 %collective-permute-start.31 = (bf16[1,240,384]{2,1,0:T(8,128)(2,1)S(1)}, bf16[1,240,384]{2,1,0:T(8,128)(2,1)S(1)}, u32[]{:S(2)}, u32[]{:S(2)}) collective-permute-start(bf16[1,240,384]{2,1,0:T(8,128)(2,1)S(1)} %get-tuple-element.352.refs_0_), channel_id=1, source_target_pairs={{0,16},{1,17},{2,18},{3,19},{4,20},{5,21},{6,22},{7,23},{8,24},{9,... | collective-permute-start | bytes 552968 | tf_op jit(solution)/shard_map/ppermute | solution.py:63
  327.8 11.8 %collective-permute-start.24 = (bf16[2,224,384]{2,1,0:T(8,128)(2,1)S(1)}, bf16[2,224,384]{2,1,0:T(8,128)(2,1)S(1)}, u32[]{:S(2)}, u32[]{:S(2)}) collective-permute-start(bf16[2,224,384]{2,1,0:T(8,128)(2,1)S(1)} %get-tuple-element.338), channel_id=1, source_target_pairs={{0,8},{1,9},{2,10},{3,11},{4,12},{5,13},{6,14},{7,15},{8,0},{9,1},... | collective-permute-start | bytes 1032200 | tf_op jit(solution)/shard_map/ppermute | solution.py:63
  331.2 18.9 %collective-permute-start.29 = (bf16[4,288,256]{2,1,0:T(8,128)(2,1)S(1)}, bf16[4,288,256]{2,1,0:T(8,128)(2,1)S(1)}, u32[]{:S(2)}, u32[]{:S(2)}) collective-permute-start(bf16[4,288,256]{2,1,0:T(8,128)(2,1)S(1)} %get-tuple-element.350.refs_0_), channel_id=1, source_target_pairs={{0,2},{1,5},{2,0},{3,7},{4,6},{5,1},{6,4},{7,3},{8,10},{9,13},{10,... | collective-permute-start | bytes 1769480 | tf_op jit(solution)/shard_map/ppermute | solution.py:63
  339.6 13.5 %collective-permute-start.28 = (bf16[1,224,384]{2,1,0:T(8,128)(2,1)S(1)}, bf16[1,224,384]{2,1,0:T(8,128)(2,1)S(1)}, u32[]{:S(2)}, u32[]{:S(2)}) collective-permute-start(bf16[1,224,384]{2,1,0:T(8,128)(2,1)S(1)} %get-tuple-element.349), channel_id=1, source_target_pairs={{0,16},{1,17},{2,18},{3,19},{4,20},{5,21},{6,22},{7,23},{8,24},{9,... | collective-permute-start | bytes 516104 | tf_op jit(solution)/shard_map/ppermute | solution.py:63
  346.7 10.1 %collective-permute-start.34 = (bf16[2,240,384]{2,1,0:T(8,128)(2,1)S(1)}, bf16[2,240,384]{2,1,0:T(8,128)(2,1)S(1)}, u32[]{:S(2)}, u32[]{:S(2)}) collective-permute-start(bf16[2,240,384]{2,1,0:T(8,128)(2,1)S(1)} %get-tuple-element.359.refs_0_), channel_id=1, source_target_pairs={{0,8},{1,5},{2,10},{3,7},{4,12},{5,1},{6,14},{7,3},{8,0},{9,13},{1... | collective-permute-start | bytes 1105928 | tf_op jit(solution)/shard_map/ppermute | solution.py:63
  349.2 7.5 %collective-permute-start.35 = (bf16[2,240,384]{2,1,0:T(8,128)(2,1)S(1)}, bf16[2,240,384]{2,1,0:T(8,128)(2,1)S(1)}, u32[]{:S(2)}, u32[]{:S(2)}) collective-permute-start(bf16[2,240,384]{2,1,0:T(8,128)(2,1)S(1)} %get-tuple-element.360.refs_0_), channel_id=1, source_target_pairs={{0,4},{1,3},{2,6},{3,1},{4,0},{5,7},{6,2},{7,5},{8,12},{9,11},{10,... | collective-permute-start | bytes 1105928 | tf_op jit(solution)/shard_map/ppermute | solution.py:63
  350.2 19.2 %collective-permute-start.37 = (bf16[8,288,256]{2,1,0:T(8,128)(2,1)S(1)}, bf16[8,288,256]{2,1,0:T(8,128)(2,1)S(1)}, u32[]{:S(2)}, u32[]{:S(2)}) collective-permute-start(bf16[8,288,256]{2,1,0:T(8,128)(2,1)S(1)} %get-tuple-element.358.refs_1_), channel_id=1, source_target_pairs={{0,4},{1,3},{2,6},{3,1},{4,0},{5,7},{6,2},{7,5},{8,12},{9,11},{10,... | collective-permute-start | bytes 3538952 | tf_op jit(solution)/shard_map/ppermute | solution.py:63
  351.4 18.0 %collective-permute-start.33 = (bf16[8,288,256]{2,1,0:T(8,128)(2,1)S(1)}, bf16[8,288,256]{2,1,0:T(8,128)(2,1)S(1)}, u32[]{:S(2)}, u32[]{:S(2)}) collective-permute-start(bf16[8,288,256]{2,1,0:T(8,128)(2,1)S(1)} %get-tuple-element.358.refs_1_), channel_id=1, source_target_pairs={{0,1},{1,0},{2,3},{3,2},{4,5},{5,4},{6,7},{7,6},{8,9},{9,8},{10,11... | collective-permute-start | bytes 3538952 | tf_op jit(solution)/shard_map/ppermute | solution.py:48
  353.2 20.0 %collective-permute-start.32 = (bf16[1,224,384]{2,1,0:T(8,128)(2,1)S(1)}, bf16[1,224,384]{2,1,0:T(8,128)(2,1)S(1)}, u32[]{:S(2)}, u32[]{:S(2)}) collective-permute-start(bf16[1,224,384]{2,1,0:T(8,128)(2,1)S(1)} %get-tuple-element.357.refs_0_), channel_id=1, source_target_pairs={{0,16},{1,17},{2,18},{3,19},{4,20},{5,21},{6,22},{7,23},{8,24},{9,... | collective-permute-start | bytes 516104 | tf_op jit(solution)/shard_map/ppermute | solution.py:63
  356.9 25.5 %collective-permute-start.39 = (bf16[4,240,384]{2,1,0:T(8,128)(2,1)S(1)}, bf16[4,240,384]{2,1,0:T(8,128)(2,1)S(1)}, u32[]{:S(2)}, u32[]{:S(2)}) collective-permute-start(bf16[4,240,384]{2,1,0:T(8,128)(2,1)S(1)} %get-tuple-element.369.refs_0_), channel_id=1, source_target_pairs={{0,2},{1,9},{2,0},{3,11},{4,6},{5,13},{6,4},{7,15},{8,10},{9,1},{1... | collective-permute-start | bytes 2211848 | tf_op jit(solution)/shard_map/ppermute | solution.py:63
  357.7 21.9 %collective-permute-start.40 = (bf16[4,240,384]{2,1,0:T(8,128)(2,1)S(1)}, bf16[4,240,384]{2,1,0:T(8,128)(2,1)S(1)}, u32[]{:S(2)}, u32[]{:S(2)}) collective-permute-start(bf16[4,240,384]{2,1,0:T(8,128)(2,1)S(1)} %get-tuple-element.370.refs_0_), channel_id=1, source_target_pairs={{0,2},{1,9},{2,0},{3,11},{4,6},{5,13},{6,4},{7,15},{8,10},{9,1},{1... | collective-permute-start | bytes 2211848 | tf_op jit(solution)/shard_map/ppermute | solution.py:63
  369.4 15.3 %collective-permute-start.38 = (bf16[8,288,256]{2,1,0:T(8,128)(2,1)S(1)}, bf16[8,288,256]{2,1,0:T(8,128)(2,1)S(1)}, u32[]{:S(2)}, u32[]{:S(2)}) collective-permute-start(bf16[8,288,256]{2,1,0:T(8,128)(2,1)S(1)} %collective-permute-done.37.refs_1_), channel_id=1, source_target_pairs={{0,1},{1,0},{2,3},{3,2},{4,5},{5,4},{6,7},{7,6},{8,9},{9,8},{10,11... | collective-permute-start | bytes 3538952 | tf_op jit(solution)/shard_map/ppermute | solution.py:48
  379.8 29.1 %collective-permute-start.49 = (bf16[8,240,384]{2,1,0:T(8,128)(2,1)S(1)}, bf16[8,240,384]{2,1,0:T(8,128)(2,1)S(1)}, u32[]{:S(2)}, u32[]{:S(2)}) collective-permute-start(bf16[8,240,384]{2,1,0:T(8,128)(2,1)S(1)} %get-tuple-element.377.refs_1_), channel_id=1, source_target_pairs={{0,8},{1,5},{2,10},{3,7},{4,12},{5,1},{6,14},{7,3},{8,0},{9,13},{1... | collective-permute-start | bytes 4423688 | tf_op jit(solution)/shard_map/ppermute | solution.py:63
  382.4 26.5 %collective-permute-start.43 = (bf16[8,240,384]{2,1,0:T(8,128)(2,1)S(1)}, bf16[8,240,384]{2,1,0:T(8,128)(2,1)S(1)}, u32[]{:S(2)}, u32[]{:S(2)}) collective-permute-start(bf16[8,240,384]{2,1,0:T(8,128)(2,1)S(1)} %get-tuple-element.377.refs_1_), channel_id=1, source_target_pairs={{0,1},{1,0},{2,3},{3,2},{4,5},{5,4},{6,7},{7,6},{8,9},{9,8},{10,11... | collective-permute-start | bytes 4423688 | tf_op jit(solution)/shard_map/ppermute | solution.py:48
  382.5 30.4 %collective-permute-start.42 = (bf16[8,240,384]{2,1,0:T(8,128)(2,1)S(1)}, bf16[8,240,384]{2,1,0:T(8,128)(2,1)S(1)}, u32[]{:S(2)}, u32[]{:S(2)}) collective-permute-start(bf16[8,240,384]{2,1,0:T(8,128)(2,1)S(1)} %get-tuple-element.376.refs_1_), channel_id=1, source_target_pairs={{0,1},{1,0},{2,3},{3,2},{4,5},{5,4},{6,7},{7,6},{8,9},{9,8},{10,11... | collective-permute-start | bytes 4423688 | tf_op jit(solution)/shard_map/ppermute | solution.py:48
  383.1 35.5 %collective-permute-start.47 = (bf16[8,240,384]{2,1,0:T(8,128)(2,1)S(1)}, bf16[8,240,384]{2,1,0:T(8,128)(2,1)S(1)}, u32[]{:S(2)}, u32[]{:S(2)}) collective-permute-start(bf16[8,240,384]{2,1,0:T(8,128)(2,1)S(1)} %get-tuple-element.376.refs_1_), channel_id=1, source_target_pairs={{0,4},{1,3},{2,6},{3,1},{4,0},{5,7},{6,2},{7,5},{8,12},{9,11},{10,... | collective-permute-start | bytes 4423688 | tf_op jit(solution)/shard_map/ppermute | solution.py:63
  384.7 22.3 %collective-permute-start.36 = (bf16[2,224,384]{2,1,0:T(8,128)(2,1)S(1)}, bf16[2,224,384]{2,1,0:T(8,128)(2,1)S(1)}, u32[]{:S(2)}, u32[]{:S(2)}) collective-permute-start(bf16[2,224,384]{2,1,0:T(8,128)(2,1)S(1)} %get-tuple-element.365.refs_0_), channel_id=1, source_target_pairs={{0,8},{1,9},{2,10},{3,11},{4,12},{5,13},{6,14},{7,15},{8,0},{9,1},... | collective-permute-start | bytes 1032200 | tf_op jit(solution)/shard_map/ppermute | solution.py:63
  407.1 11.0 %collective-permute-start.41 = (bf16[4,224,384]{2,1,0:T(8,128)(2,1)S(1)}, bf16[4,224,384]{2,1,0:T(8,128)(2,1)S(1)}, u32[]{:S(2)}, u32[]{:S(2)}) collective-permute-start(bf16[4,224,384]{2,1,0:T(8,128)(2,1)S(1)} %get-tuple-element.375.refs_0_), channel_id=1, source_target_pairs={{0,4},{1,3},{2,6},{3,1},{4,0},{5,7},{6,2},{7,5},{8,12},{9,11},{10,... | collective-permute-start | bytes 2064392 | tf_op jit(solution)/shard_map/ppermute | solution.py:63
  408.9 27.8 %collective-permute-start.50 = (bf16[8,240,384]{2,1,0:T(8,128)(2,1)S(1)}, bf16[8,240,384]{2,1,0:T(8,128)(2,1)S(1)}, u32[]{:S(2)}, u32[]{:S(2)}) collective-permute-start(bf16[8,240,384]{2,1,0:T(8,128)(2,1)S(1)} %collective-permute-done.49.refs_1_), channel_id=1, source_target_pairs={{0,1},{1,0},{2,3},{3,2},{4,5},{5,4},{6,7},{7,6},{8,9},{9,8},{10,11... | collective-permute-start | bytes 4423688 | tf_op jit(solution)/shard_map/ppermute | solution.py:48
  418.3 18.4 %collective-permute-start.44 = (bf16[8,224,384]{2,1,0:T(8,128)(2,1)S(1)}, bf16[8,224,384]{2,1,0:T(8,128)(2,1)S(1)}, u32[]{:S(2)}, u32[]{:S(2)}) collective-permute-start(bf16[8,224,384]{2,1,0:T(8,128)(2,1)S(1)} %get-tuple-element.381.refs_1_), channel_id=1, source_target_pairs={{0,2},{1,5},{2,0},{3,7},{4,6},{5,1},{6,4},{7,3},{8,10},{9,13},{10,... | collective-permute-start | bytes 4128776 | tf_op jit(solution)/shard_map/ppermute | solution.py:63
  418.6 22.0 %collective-permute-start.48 = (bf16[8,240,384]{2,1,0:T(8,128)(2,1)S(1)}, bf16[8,240,384]{2,1,0:T(8,128)(2,1)S(1)}, u32[]{:S(2)}, u32[]{:S(2)}) collective-permute-start(bf16[8,240,384]{2,1,0:T(8,128)(2,1)S(1)} %collective-permute-done.47.refs_1_), channel_id=1, source_target_pairs={{0,1},{1,0},{2,3},{3,2},{4,5},{5,4},{6,7},{7,6},{8,9},{9,8},{10,11... | collective-permute-start | bytes 4423688 | tf_op jit(solution)/shard_map/ppermute | solution.py:48
  418.6 25.9 %collective-permute-start.46 = (bf16[8,224,384]{2,1,0:T(8,128)(2,1)S(1)}, bf16[8,224,384]{2,1,0:T(8,128)(2,1)S(1)}, u32[]{:S(2)}, u32[]{:S(2)}) collective-permute-start(bf16[8,224,384]{2,1,0:T(8,128)(2,1)S(1)} %get-tuple-element.381.refs_1_), channel_id=1, source_target_pairs={{0,1},{1,0},{2,3},{3,2},{4,5},{5,4},{6,7},{7,6},{8,9},{9,8},{10,11... | collective-permute-start | bytes 4128776 | tf_op jit(solution)/shard_map/ppermute | solution.py:48
  436.6 11.8 %collective-permute-start.45 = (bf16[8,224,384]{2,1,0:T(8,128)(2,1)S(1)}, bf16[8,224,384]{2,1,0:T(8,128)(2,1)S(1)}, u32[]{:S(2)}, u32[]{:S(2)}) collective-permute-start(bf16[8,224,384]{2,1,0:T(8,128)(2,1)S(1)} %collective-permute-done.44.refs_1_), channel_id=1, source_target_pairs={{0,1},{1,0},{2,3},{3,2},{4,5},{5,4},{6,7},{7,6},{8,9},{9,8},{10,11... | collective-permute-start | bytes 4128776 | tf_op jit(solution)/shard_map/ppermute | solution.py:48
  (73 other events, 440.0 us)

commit v2 on v1

--- a/solution.py
+++ b/solution.py
@@ -13,7 +13,7 @@
 VMEM_LIMIT = 60 * 1024 * 1024
 DEC_BITS = ((1, 0, 2, 3), (0, 1, 2, 3))
 ENC_BITS = (((2, 0, 1, 3), (1, 2, 0, 3)), ((1, 0, 2, 3), (0, 2, 1, 3)), ((0, 1, 2, 3), (1, 0, 2, 3)))
-STEPS = "abdcabdcabdcabdcabdcabdcabdcabcabcc"
+STEPS = "abdcabdcabdcabdcabdcabcdabcdcabcabc"
 SHORT = 512
 WEIGHT_LIMIT = 40 * 1024 * 1024
 SMALL_LIMIT = 24 * 1024 * 1024
@@ -413,7 +413,7 @@
         self.other.append(across(self.held[1], "blk", 0))
 
     def place(self, part, earlier):
-        entries, shards, slots = self.entries, self.shards, 4
+        entries, shards, slots = self.entries, self.shards, self.shards
         half_count = shards // 2
         sizes = [
             (entry.r, entry.n * entry.width) if entry.kind == "wide" else (entry.n * entry.r, entry.width) for entry in entries

time: 460 us -> 457 us (level)
  starting transfers between devices: 57 us -> 82.8 us
  waiting for transfers between devices: 114 us -> 90.8 us
  Pallas kernels: 241 us -> 235 us
    ppermute x19, starting transfers between devices: 3.62 us -> 29.3 us  [across(): return lax.ppermute(value, axis, [(i, i ^ 1 << bit) for i in range(count)])]
    ppermute x32, waiting for transfers between devices: 106 us -> 83.2 us  [across_bits(): return lax.ppermute(value, ('dp', 'blk'), pairs)]
    pallas_call x40, Pallas kernels: 45 us -> 39.8 us  [run_small(): pl.pallas_call(body, out_shape=[*out_shape, TOKEN], in_specs=in_specs, ou...]
  transfers between devices with their start and end apart: 51 -> 51, of which waited for: 16 -> 14; matrix products, arithmetic and copies ran while one was open for 2% -> 2% of each run, Pallas kernels for 22% -> 21%
where the time goes in v2:
time: 457 us; the launch traced here: 453 us
  Pallas kernels  235 us (51%)
  waiting for transfers between devices  90.8 us (20%)
  starting transfers between devices  82.8 us (18%)
  local copies, waits for them, and re-layouts  36.7 us (8%)
  other arithmetic  5.45 us (1%)
    pallas_call x11, Pallas kernels, run(): pl.pallas_call(body, out_shape=[*out_shape, TOKEN], grid_spec=pltpu.Prefe...  196 us
    ppermute x32, waiting for transfers between devices, across_bits(): return lax.ppermute(value, ('dp', 'blk'), pairs)  83.2 us
    ppermute x32, starting transfers between devices, across_bits(): return lax.ppermute(value, ('dp', 'blk'), pairs)  53.6 us
    pallas_call x40, Pallas kernels, run_small(): pl.pallas_call(body, out_shape=[*out_shape, TOKEN], in_specs=in_specs, ou...  39.8 us
    unnamed x140, local copies, waits for them, and re-layouts  31.6 us
    ppermute x19, starting transfers between devices, across(): return lax.ppermute(value, axis, [(i, i ^ 1 << bit) for i in range(count)])  29.3 us
  transfers between devices with their start and end apart: 51, of which 14 were waited for; matrix products, arithmetic and copies ran while one was open for 2% of the time, Pallas kernels for 21%

profile of v2, /device:TPU:0, one launch (start us, length us, event | category | flops | bytes accessed | tf_op | source)
XLA Modules:
  0.0 453.0 jit_solution(17736507601095097018)
XLA Ops:
  9.6 8.2 %enc_in.1 = (bf16[768,768]{1,0:T(8,128)(2,1)}, f32[16,768]{1,0:T(8,128)}, f32[16,768]{1,0:T(8,128)}, f32[768,16]{1,0:T(8,128)}, f32[16,768]{1,0:T(8,128)}, /*ind...) custom-call(s32[2]{0:T(128)} %fusion.meta, ...), custom_call_target="tpu_custom_call" | custom-call | flops 8049999872 | bytes 25200000 | tf_op jit(solution)/shard_map/enc_in/pallas_call | solution.py:84
  18.6 4.0 collective-permute-done.3.refs_3_.refs_6_
  24.1 20.0 %enc_main.1 = (bf16[768,768]{1,0:T(8,128)(2,1)}, f32[768,128]{1,0:T(8,128)}, f32[768,768]{1,0:T(8,128)}, bf16[768,768]{1,0:T(8,128)(2,1)}, bf16[768,3072]{1,0:T(...) custom-call(s32[2]{0:T(128)} %fusion.meta, ...), custom_call_target="tpu_custom_call" | custom-call | flops 23000000512 | bytes 72000000 | tf_op jit(solution)/shard_map/enc_main/pallas_call | solution.py:84
  44.1 7.4 %dec_in.1 = (f32[768,512]{1,0:T(8,128)}, bf16[768,512]{1,0:T(8,128)(2,1)}, bf16[768,512]{1,0:T(8,128)(2,1)}, bf16[768,1024]{1,0:T(8,128)(2,1)}, f32[8,128]{1,0:T(8,128)}) custom-call(s32[2]{0:T(128)} %fusion.meta, bf16[768,768]{1,0:T(8,128)(2,1)} %get-tuple-element.215.refs_0_, bf16[768,512]{1,0:T(8,128)(2,1)} %get-tuple-element.223.refs_1_, ...), custom_call_target="tpu_custom_call" | custom-call | flops 8049999872 | bytes 25200000 | tf_op jit(solution)/shard_map/dec_in/pallas_call | solution.py:84
  51.6 3.5 collective-permute-done.4.refs_3_
  56.2 94.6 %dec_main.1 = (bf16[768,512]{1,0:T(8,128)(2,1)}, bf16[768,512]{1,0:T(8,128)(2,1)}, bf16[768,512]{1,0:T(8,128)(2,1)}, bf16[768,2048]{1,0:T(8,128)(2,1)}, bf16[768...) custom-call(s32[2]{0:T(128)} %fusion.meta, ...), custom_call_target="tpu_custom_call" | custom-call | flops 109250002944 | bytes 342000000 | tf_op jit(solution)/shard_map/dec_main/pallas_call | solution.py:84
  159.0 8.0 %weight_grads.4 = (bf16[16,288,256]{2,1,0:T(8,128)(2,1)S(1)}, bf16[16,288,256]{2,1,0:T(8,128)(2,1)S(1)}, f32[8,128]{1,0:T(8,128)S(1)}) custom-call(s32[3]{0:T(128)S(1)} %pad_add_fusion.meta, bf16[768,512]{1,0:T(8,128)(2,1)S(1)} %copy-done.22, bf16[768,2048]{1,0:T(8,128)(2,1)S(1)} %copy-done.17, bf16[768,2048]{1,0:T(8,128)(2,1)S(1)} %copy-done.17, ...), custom_call_target="tpu_custom_call" | custom-call | flops 6899999744 | bytes 21600000 | tf_op jit(solution)/shard_map/weight_grads/pallas_call | solution.py:84
  169.4 8.1 %dec_head.1 = (bf16[768,1536]{1,0:T(8,128)(2,1)}, bf16[768,512]{1,0:T(8,128)(2,1)}, f32[1,512]{1,0:T(1,128)}, f32[1,512]{1,0:T(1,128)}, f32[1,512]{1,0:T(1,128)}, /*index=5*/f32[1,512]{1,0:T(1,128)}, f32[8,128]{1,0:T(8,128)}) custom-call(s32[2]{0:T(128)} %fusion.meta, f32[768,512]{1,0:T(8,128)} %get-tuple-element.227.refs_0_, ...), custom_call_target="tpu_custom_call" | custom-call | flops 46000001024 | bytes 144000000 | tf_op jit(solution)/shard_map/dec_head/pallas_call | solution.py:84
  179.8 2.3 halve.16
  183.7 2.6 collective-permute-start.8
  186.3 24.6 %enc_back.1 = (bf16[768,512]{1,0:T(8,128)(2,1)}, bf16[768,768]{1,0:T(8,128)(2,1)}, bf16[768,3072]{1,0:T(8,128)(2,1)}, bf16[768,768]{1,0:T(8,128)(2,1)}, f32[768,...) custom-call(s32[2]{0:T(128)} %fusion.meta, ...), custom_call_target="tpu_custom_call" | custom-call | flops 27599998976 | bytes 86400000 | tf_op jit(solution)/shard_map/enc_back/pallas_call | solution.py:84
  216.5 5.1 %weight_grads.5 = (bf16[16,240,384]{2,1,0:T(8,128)(2,1)S(1)}, bf16[16,240,384]{2,1,0:T(8,128)(2,1)S(1)}, f32[8,128]{1,0:T(8,128)S(1)}) custom-call(s32[3]{0:T(128)S(1)} %pad_add_fusion.meta, bf16[3,256,768]{2,1,0:T(8,128)(2,1)S(1)} %bitcast.48, bf16[3,256,3072]{2,1,0:T(8,128)(2,1)S(1)} %bitcast.36, bf16[3,256,3072]{2,1,0:T(8,128)(2,1)S(1)} %bitcast.37, ...), custom_call_target="tpu_custom_call" | custom-call | flops 6899999744 | bytes 21600000 | tf_op jit(solution)/shard_map/weight_grads/pallas_call | solution.py:84
  223.7 2.3 copy-done.1
  226.1 5.3 %weight_grads.6 = (bf16[16,240,384]{2,1,0:T(8,128)(2,1)S(1)}, bf16[16,240,384]{2,1,0:T(8,128)(2,1)S(1)}, f32[8,128]{1,0:T(8,128)S(1)}) custom-call(s32[3]{0:T(128)S(1)} %pad_add_fusion.meta, bf16[3,256,3072]{2,1,0:T(8,128)(2,1)S(1)} %bitcast.34, bf16[3,256,768]{2,1,0:T(8,128)(2,1)S(1)} %bitcast.50, bf16[3,256,768]{2,1,0:T(8,128)(2,1)S(1)} %bitcast.51, ...), custom_call_target="tpu_custom_call" | custom-call | flops 6899999744 | bytes 21600000 | tf_op jit(solution)/shard_map/weight_grads/pallas_call | solution.py:84
  238.2 8.3 %enc_head.1 = (bf16[768,2304]{1,0:T(8,128)(2,1)}, bf16[768,768]{1,0:T(8,128)(2,1)}, f32[1,768]{1,0:T(1,128)}, f32[1,768]{1,0:T(1,128)}, f32[8,128]{1,0:T(8,128)}) custom-call(s32[2]{0:T(128)} %fusion.meta, bf16[768,768]{1,0:T(8,128)(2,1)} %get-tuple-element.215.refs_0_, bf16[768,768]{1,0:T(8,128)(2,1)} %get-tuple-element.216.refs_0_.refs_1_, ...), custom_call_target="tpu_custom_call" | custom-call | flops 9200000000 | bytes 28800000 | tf_op jit(solution)/shard_map/enc_head/pallas_call | solution.py:84
  249.0 2.7 halve.19
  255.9 6.2 %weight_grads.7 = (bf16[16,224,384]{2,1,0:T(8,128)(2,1)S(1)}, bf16[16,224,384]{2,1,0:T(8,128)(2,1)S(1)}, f32[8,128]{1,0:T(8,128)S(1)}) custom-call(s32[3]{0:T(128)S(1)} %pad_add_fusion.meta, bf16[3,256,768]{2,1,0:T(8,128)(2,1)S(1)} %bitcast.42, bf16[3,256,2304]{2,1,0:T(8,128)(2,1)S(1)} %bitcast.39, bf16[3,256,2304]{2,1,0:T(8,128)(2,1)S(1)} %bitcast.40, ...), custom_call_target="tpu_custom_call" | custom-call | flops 6899999744 | bytes 21600000 | tf_op jit(solution)/shard_map/weight_grads/pallas_call | solution.py:84
  265.5 7.0 %collective-permute-done.14.refs_1_ = bf16[8,240,384]{2,1,0:T(8,128)(2,1)S(1)} collective-permute-done((bf16[8,240,384]{2,1,0:T(8,128)(2,1)S(1)}, bf16[8,240,384]{2,1,0:T(8,128)(2,1)S(1)}, u32[]{:S(2)}, u32[]{:S(2)}) %collective-permute-start.14) | collective-permute-done | bytes 1474592 | tf_op jit(solution)/shard_map/ppermute | solution.py:63
  276.0 2.6 collective-permute-start.17
  280.0 8.7 %collective-permute-done.18.refs_1_ = bf16[4,240,384]{2,1,0:T(8,128)(2,1)S(1)} collective-permute-done((bf16[4,240,384]{2,1,0:T(8,128)(2,1)S(1)}, bf16[4,240,384]{2,1,0:T(8,128)(2,1)S(1)}, u32[]{:S(2)}, u32[]{:S(2)}) %collective-permute-start.18) | collective-permute-done | bytes 737312 | tf_op jit(solution)/shard_map/ppermute | solution.py:63
  290.6 2.7 collective-permute-start.21
  293.3 15.2 %collective-permute-done.16.refs_1_ = bf16[8,224,384]{2,1,0:T(8,128)(2,1)S(1)} collective-permute-done((bf16[8,224,384]{2,1,0:T(8,128)(2,1)S(1)}, bf16[8,224,384]{2,1,0:T(8,128)(2,1)S(1)}, u32[]{:S(2)}, u32[]{:S(2)}) %collective-permute-start.16) | collective-permute-done | bytes 1376288 | tf_op jit(solution)/shard_map/ppermute | solution.py:63
  310.2 2.7 collective-permute-start.27
  313.4 2.9 collective-permute-start.25
  316.4 5.9 %collective-permute-done.20.refs_1_ = bf16[4,224,384]{2,1,0:T(8,128)(2,1)S(1)} collective-permute-done((bf16[4,224,384]{2,1,0:T(8,128)(2,1)S(1)}, bf16[4,224,384]{2,1,0:T(8,128)(2,1)S(1)}, u32[]{:S(2)}, u32[]{:S(2)}) %collective-permute-start.20) | collective-permute-done | bytes 688160 | tf_op jit(solution)/shard_map/ppermute | solution.py:63
  322.4 5.3 %collective-permute-start.24 = (bf16[2,224,384]{2,1,0:T(8,128)(2,1)S(1)}, bf16[2,224,384]{2,1,0:T(8,128)(2,1)S(1)}, u32[]{:S(2)}, u32[]{:S(2)}) collective-permute-start(bf16[2,224,384]{2,1,0:T(8,128)(2,1)S(1)} %get-tuple-element.338), channel_id=1, source_target_pairs={{0,8},{1,9},{2,10},{3,11},{4,12},{5,13},{6,14},{7,15},{8,0},{9,1},... | collective-permute-start | bytes 1032200 | tf_op jit(solution)/shard_map/ppermute | solution.py:63
  327.7 2.8 collective-permute-start.31
  332.0 5.8 %collective-permute-done.24.refs_1_ = bf16[2,224,384]{2,1,0:T(8,128)(2,1)S(1)} collective-permute-done((bf16[2,224,384]{2,1,0:T(8,128)(2,1)S(1)}, bf16[2,224,384]{2,1,0:T(8,128)(2,1)S(1)}, u32[]{:S(2)}, u32[]{:S(2)}) %collective-permute-start.24) | collective-permute-done | bytes 344096 | tf_op jit(solution)/shard_map/ppermute | solution.py:63
  340.2 2.0 collective-permute-done.30.refs_1_
  342.3 2.6 collective-permute-start.33
  346.1 3.4 collective-permute-start.32
  351.9 5.8 %collective-permute-done.32.refs_1_ = bf16[1,224,384]{2,1,0:T(8,128)(2,1)S(1)} collective-permute-done((bf16[1,224,384]{2,1,0:T(8,128)(2,1)S(1)}, bf16[1,224,384]{2,1,0:T(8,128)(2,1)S(1)}, u32[]{:S(2)}, u32[]{:S(2)}) %collective-permute-start.32) | collective-permute-done | bytes 172064 | tf_op jit(solution)/shard_map/ppermute | solution.py:63
  359.1 2.2 collective-permute-done.40.refs_1_
  361.3 7.0 %collective-permute-start.41 = (bf16[8,288,256]{2,1,0:T(8,128)(2,1)S(1)}, bf16[8,288,256]{2,1,0:T(8,128)(2,1)S(1)}, u32[]{:S(2)}, u32[]{:S(2)}) collective-permute-start(bf16[8,288,256]{2,1,0:T(8,128)(2,1)S(1)} %collective-permute-done.40.refs_1_), channel_id=1, source_target_pairs={{0,1},{1,0},{2,3},{3,2},{4,5},{5,4},{6,7},{7,6},{8,9},{9,8},{10,11... | collective-permute-start | bytes 3538952 | tf_op jit(solution)/shard_map/ppermute | solution.py:48
  368.2 3.1 place_shards.8
  371.5 5.0 %collective-permute-done.36.refs_1_ = bf16[4,240,384]{2,1,0:T(8,128)(2,1)S(1)} collective-permute-done((bf16[4,240,384]{2,1,0:T(8,128)(2,1)S(1)}, bf16[4,240,384]{2,1,0:T(8,128)(2,1)S(1)}, u32[]{:S(2)}, u32[]{:S(2)}) %collective-permute-start.36) | collective-permute-done | bytes 737312 | tf_op jit(solution)/shard_map/ppermute | solution.py:63
  378.2 2.0 collective-permute-start.49
  381.5 3.1 place_shards.9
  384.6 10.0 %collective-permute-done.39.refs_1_ = bf16[4,224,384]{2,1,0:T(8,128)(2,1)S(1)} collective-permute-done((bf16[4,224,384]{2,1,0:T(8,128)(2,1)S(1)}, bf16[4,224,384]{2,1,0:T(8,128)(2,1)S(1)}, u32[]{:S(2)}, u32[]{:S(2)}) %collective-permute-start.39) | collective-permute-done | bytes 688160 | tf_op jit(solution)/shard_map/ppermute | solution.py:63
  397.6 15.0 %collective-permute-start.50 = (bf16[8,240,384]{2,1,0:T(8,128)(2,1)S(1)}, bf16[8,240,384]{2,1,0:T(8,128)(2,1)S(1)}, u32[]{:S(2)}, u32[]{:S(2)}) collective-permute-start(bf16[8,240,384]{2,1,0:T(8,128)(2,1)S(1)} %collective-permute-done.49.refs_1_), channel_id=1, source_target_pairs={{0,1},{1,0},{2,3},{3,2},{4,5},{5,4},{6,7},{7,6},{8,9},{9,8},{10,11... | collective-permute-start | bytes 4423688 | tf_op jit(solution)/shard_map/ppermute | solution.py:48
  412.6 13.7 %collective-permute-done.47.refs_1_ = bf16[8,240,384]{2,1,0:T(8,128)(2,1)S(1)} collective-permute-done((bf16[8,240,384]{2,1,0:T(8,128)(2,1)S(1)}, bf16[8,240,384]{2,1,0:T(8,128)(2,1)S(1)}, u32[]{:S(2)}, u32[]{:S(2)}) %collective-permute-start.47) | collective-permute-done | bytes 1474592 | tf_op jit(solution)/shard_map/ppermute | solution.py:63
  426.2 3.4 place_shards.10
  429.6 4.3 collective-permute-start.43
  433.9 3.2 place_shards.11
  437.2 3.3 place_shards.12
  440.5 3.4 place_shards.13
  443.8 3.2 place_shards.14
  447.1 3.3 place_shards.15
  (261 shorter events, 77.6 us)
Async XLA Ops:
  2.5 6.5 %collective-permute-start.1 = (s32[1,768]{1,0:T(1,128)S(1)}, s32[1,768]{1,0:T(1,128)S(1)}, u32[]{:S(2)}, u32[]{:S(2)}) collective-permute-start(s32[1,768]{1,0:T(1,128)S(1)} %reshape.112.refs_2_), channel_id=1, source_target_pairs={{0,1},{1,0},{2,3},{3,2},{4,5},{5,4},{6,7},{7,6},{8,9},{9,8},{10,11... | collective-permute-start | bytes 9224 | tf_op jit(solution)/shard_map/ppermute | solution.py:48
  3.3 5.7 %collective-permute-start.2 = (s32[1,768]{1,0:T(1,128)S(1)}, s32[1,768]{1,0:T(1,128)S(1)}, u32[]{:S(2)}, u32[]{:S(2)}) collective-permute-start(s32[1,768]{1,0:T(1,128)S(1)} %reshape.113.refs_3_), channel_id=1, source_target_pairs={{0,1},{1,0},{2,3},{3,2},{4,5},{5,4},{6,7},{7,6},{8,9},{9,8},{10,11... | collective-permute-start | bytes 9224 | tf_op jit(solution)/shard_map/ppermute | solution.py:48
  150.8 18.5 %collective-permute-start.5 = (bf16[768,1024]{1,0:T(8,128)(2,1)}, bf16[768,1024]{1,0:T(8,128)(2,1)}, u32[]{:S(2)}, u32[]{:S(2)}) collective-permute-start(bf16[768,1024]{1,0:T(8,128)(2,1)} %get-tuple-element.236), channel_id=1, source_target_pairs={{0,1},{1,0},{2,3},{3,2},{4,5},{5,4},{6,7},{7,6},{8,9},{9,8},{10,11... | collective-permute-start | bytes 4718600 | tf_op jit(solution)/shard_map/ppermute | solution.py:48
  169.0 8.5 %collective-permute-start.6 = (bf16[16,288,256]{2,1,0:T(8,128)(2,1)S(1)}, bf16[16,288,256]{2,1,0:T(8,128)(2,1)}, u32[]{:S(2)}, u32[]{:S(2)}) collective-permute-start(bf16[16,288,256]{2,1,0:T(8,128)(2,1)S(1)} %get-tuple-element.251), channel_id=1, source_target_pairs={{0,1},{1,0},{2,3},{3,2},{4,5},{5,4},{6,7},{7,6},{8,9},{9,8},{10,11... | collective-permute-start | bytes 7077896 | tf_op jit(solution)/shard_map/ppermute | solution.py:48
  183.7 27.2 %collective-permute-start.8 = (bf16[8,288,256]{2,1,0:T(8,128)(2,1)S(1)}, bf16[8,288,256]{2,1,0:T(8,128)(2,1)S(1)}, u32[]{:S(2)}, u32[]{:S(2)}) collective-permute-start(bf16[8,288,256]{2,1,0:T(8,128)(2,1)S(1)} %get-tuple-element.262), channel_id=1, source_target_pairs={{0,4},{1,3},{2,6},{3,1},{4,0},{5,7},{6,2},{7,5},{8,12},{9,11},{10,... | collective-permute-start | bytes 3538952 | tf_op jit(solution)/shard_map/ppermute | solution.py:63
  223.2 9.8 %collective-permute-start.9 = (bf16[16,240,384]{2,1,0:T(8,128)(2,1)S(1)}, bf16[16,240,384]{2,1,0:T(8,128)(2,1)S(1)}, u32[]{:S(2)}, u32[]{:S(2)}) collective-permute-start(bf16[16,240,384]{2,1,0:T(8,128)(2,1)S(1)} %get-tuple-element.266), channel_id=1, source_target_pairs={{0,1},{1,0},{2,3},{3,2},{4,5},{5,4},{6,7},{7,6},{8,9},{9,8},{10,11... | collective-permute-start | bytes 8847368 | tf_op jit(solution)/shard_map/ppermute | solution.py:48
  223.3 14.9 %collective-permute-start.7 = (bf16[768,1536]{1,0:T(8,128)(2,1)}, bf16[768,1536]{1,0:T(8,128)(2,1)}, u32[]{:S(2)}, u32[]{:S(2)}) collective-permute-start(bf16[768,1536]{1,0:T(8,128)(2,1)} %get-tuple-element.256), channel_id=1, source_target_pairs={{0,1},{1,0},{2,3},{3,2},{4,5},{5,4},{6,7},{7,6},{8,9},{9,8},{10,11... | collective-permute-start | bytes 7077896 | tf_op jit(solution)/shard_map/ppermute | solution.py:48
  231.4 15.1 %collective-permute-start.11 = (bf16[16,240,384]{2,1,0:T(8,128)(2,1)S(1)}, bf16[16,240,384]{2,1,0:T(8,128)(2,1)}, u32[]{:S(2)}, u32[]{:S(2)}) collective-permute-start(bf16[16,240,384]{2,1,0:T(8,128)(2,1)S(1)} %get-tuple-element.298), channel_id=1, source_target_pairs={{0,1},{1,0},{2,3},{3,2},{4,5},{5,4},{6,7},{7,6},{8,9},{9,8},{10,11... | collective-permute-start | bytes 8847368 | tf_op jit(solution)/shard_map/ppermute | solution.py:48
  231.6 20.8 %collective-permute-start.10 = (bf16[4,288,256]{2,1,0:T(8,128)(2,1)S(1)}, bf16[4,288,256]{2,1,0:T(8,128)(2,1)}, u32[]{:S(2)}, u32[]{:S(2)}) collective-permute-start(bf16[4,288,256]{2,1,0:T(8,128)(2,1)S(1)} %get-tuple-element.296), channel_id=1, source_target_pairs={{0,2},{1,5},{2,0},{3,7},{4,6},{5,1},{6,4},{7,3},{8,10},{9,13},{10,... | collective-permute-start | bytes 1769480 | tf_op jit(solution)/shard_map/ppermute | solution.py:63
  236.6 25.5 %collective-permute-start.15 = (bf16[8,240,384]{2,1,0:T(8,128)(2,1)}, bf16[8,240,384]{2,1,0:T(8,128)(2,1)}, u32[]{:S(2)}, u32[]{:S(2)}) collective-permute-start(bf16[8,240,384]{2,1,0:T(8,128)(2,1)} %get-tuple-element.309), channel_id=1, source_target_pairs={{0,8},{1,5},{2,10},{3,7},{4,12},{5,1},{6,14},{7,3},{8,0},{9,13},{1... | collective-permute-start | bytes 4423688 | tf_op jit(solution)/shard_map/ppermute | solution.py:63
  251.7 20.8 %collective-permute-start.14 = (bf16[8,240,384]{2,1,0:T(8,128)(2,1)S(1)}, bf16[8,240,384]{2,1,0:T(8,128)(2,1)S(1)}, u32[]{:S(2)}, u32[]{:S(2)}) collective-permute-start(bf16[8,240,384]{2,1,0:T(8,128)(2,1)S(1)} %get-tuple-element.307), channel_id=1, source_target_pairs={{0,4},{1,3},{2,6},{3,1},{4,0},{5,7},{6,2},{7,5},{8,12},{9,11},{10,... | collective-permute-start | bytes 4423688 | tf_op jit(solution)/shard_map/ppermute | solution.py:63
  254.1 20.4 %collective-permute-start.13 = (bf16[2,288,256]{2,1,0:T(8,128)(2,1)S(1)}, bf16[2,288,256]{2,1,0:T(8,128)(2,1)S(1)}, u32[]{:S(2)}, u32[]{:S(2)}) collective-permute-start(bf16[2,288,256]{2,1,0:T(8,128)(2,1)S(1)} %get-tuple-element.305), channel_id=1, source_target_pairs={{0,8},{1,9},{2,10},{3,11},{4,12},{5,13},{6,14},{7,15},{8,0},{9,1},... | collective-permute-start | bytes 884744 | tf_op jit(solution)/shard_map/ppermute | solution.py:63
  262.0 12.5 %collective-permute-start.12 = (bf16[16,224,384]{2,1,0:T(8,128)(2,1)S(1)}, bf16[16,224,384]{2,1,0:T(8,128)(2,1)S(1)}, u32[]{:S(2)}, u32[]{:S(2)}) collective-permute-start(bf16[16,224,384]{2,1,0:T(8,128)(2,1)S(1)} %get-tuple-element.303), channel_id=1, source_target_pairs={{0,1},{1,0},{2,3},{3,2},{4,5},{5,4},{6,7},{7,6},{8,9},{9,8},{10,11... | collective-permute-start | bytes 8257544 | tf_op jit(solution)/shard_map/ppermute | solution.py:48
  263.9 14.6 %collective-permute-start.19 = (bf16[4,240,384]{2,1,0:T(8,128)(2,1)S(1)}, bf16[4,240,384]{2,1,0:T(8,128)(2,1)S(1)}, u32[]{:S(2)}, u32[]{:S(2)}) collective-permute-start(bf16[4,240,384]{2,1,0:T(8,128)(2,1)S(1)} %get-tuple-element.321), channel_id=1, source_target_pairs={{0,2},{1,9},{2,0},{3,11},{4,6},{5,13},{6,4},{7,15},{8,10},{9,1},{1... | collective-permute-start | bytes 2211848 | tf_op jit(solution)/shard_map/ppermute | solution.py:63
  272.9 15.8 %collective-permute-start.18 = (bf16[4,240,384]{2,1,0:T(8,128)(2,1)S(1)}, bf16[4,240,384]{2,1,0:T(8,128)(2,1)S(1)}, u32[]{:S(2)}, u32[]{:S(2)}) collective-permute-start(bf16[4,240,384]{2,1,0:T(8,128)(2,1)S(1)} %get-tuple-element.319), channel_id=1, source_target_pairs={{0,2},{1,9},{2,0},{3,11},{4,6},{5,13},{6,4},{7,15},{8,10},{9,1},{1... | collective-permute-start | bytes 2211848 | tf_op jit(solution)/shard_map/ppermute | solution.py:63
  275.3 33.2 %collective-permute-start.16 = (bf16[8,224,384]{2,1,0:T(8,128)(2,1)S(1)}, bf16[8,224,384]{2,1,0:T(8,128)(2,1)S(1)}, u32[]{:S(2)}, u32[]{:S(2)}) collective-permute-start(bf16[8,224,384]{2,1,0:T(8,128)(2,1)S(1)} %get-tuple-element.315), channel_id=1, source_target_pairs={{0,2},{1,5},{2,0},{3,7},{4,6},{5,1},{6,4},{7,3},{8,10},{9,13},{10,... | collective-permute-start | bytes 4128776 | tf_op jit(solution)/shard_map/ppermute | solution.py:63
  276.0 14.6 %collective-permute-start.17 = (bf16[1,288,256]{2,1,0:T(8,128)(2,1)S(1)}, bf16[1,288,256]{2,1,0:T(8,128)(2,1)S(1)}, u32[]{:S(2)}, u32[]{:S(2)}) collective-permute-start(bf16[1,288,256]{2,1,0:T(8,128)(2,1)S(1)} %get-tuple-element.317), channel_id=1, source_target_pairs={{0,16},{1,17},{2,18},{3,19},{4,20},{5,21},{6,22},{7,23},{8,24},{9,... | collective-permute-start | bytes 442376 | tf_op jit(solution)/shard_map/ppermute | solution.py:63
  278.7 31.4 %collective-permute-start.23 = (bf16[2,240,384]{2,1,0:T(8,128)(2,1)S(1)}, bf16[2,240,384]{2,1,0:T(8,128)(2,1)S(1)}, u32[]{:S(2)}, u32[]{:S(2)}) collective-permute-start(bf16[2,240,384]{2,1,0:T(8,128)(2,1)S(1)} %get-tuple-element.332), channel_id=1, source_target_pairs={{0,4},{1,3},{2,6},{3,1},{4,0},{5,7},{6,2},{7,5},{8,12},{9,11},{10,... | collective-permute-start | bytes 1105928 | tf_op jit(solution)/shard_map/ppermute | solution.py:63
  288.9 24.0 %collective-permute-start.22 = (bf16[2,240,384]{2,1,0:T(8,128)(2,1)S(1)}, bf16[2,240,384]{2,1,0:T(8,128)(2,1)S(1)}, u32[]{:S(2)}, u32[]{:S(2)}) collective-permute-start(bf16[2,240,384]{2,1,0:T(8,128)(2,1)S(1)} %get-tuple-element.330), channel_id=1, source_target_pairs={{0,8},{1,5},{2,10},{3,7},{4,12},{5,1},{6,14},{7,3},{8,0},{9,13},{1... | collective-permute-start | bytes 1105928 | tf_op jit(solution)/shard_map/ppermute | solution.py:63
  290.6 22.8 %collective-permute-start.21 = (bf16[1,288,256]{2,1,0:T(8,128)(2,1)S(1)}, bf16[1,288,256]{2,1,0:T(8,128)(2,1)S(1)}, u32[]{:S(2)}, u32[]{:S(2)}) collective-permute-start(bf16[1,288,256]{2,1,0:T(8,128)(2,1)S(1)} %get-tuple-element.328.refs_0_), channel_id=1, source_target_pairs={{0,16},{1,17},{2,18},{3,19},{4,20},{5,21},{6,22},{7,23},{8,24},{9,... | collective-permute-start | bytes 442376 | tf_op jit(solution)/shard_map/ppermute | solution.py:63
  308.9 13.3 %collective-permute-start.20 = (bf16[4,224,384]{2,1,0:T(8,128)(2,1)S(1)}, bf16[4,224,384]{2,1,0:T(8,128)(2,1)S(1)}, u32[]{:S(2)}, u32[]{:S(2)}) collective-permute-start(bf16[4,224,384]{2,1,0:T(8,128)(2,1)S(1)} %get-tuple-element.327), channel_id=1, source_target_pairs={{0,4},{1,3},{2,6},{3,1},{4,0},{5,7},{6,2},{7,5},{8,12},{9,11},{10,... | collective-permute-start | bytes 2064392 | tf_op jit(solution)/shard_map/ppermute | solution.py:63
  310.2 17.4 %collective-permute-start.27 = (bf16[1,240,384]{2,1,0:T(8,128)(2,1)S(1)}, bf16[1,240,384]{2,1,0:T(8,128)(2,1)S(1)}, u32[]{:S(2)}, u32[]{:S(2)}) collective-permute-start(bf16[1,240,384]{2,1,0:T(8,128)(2,1)S(1)} %get-tuple-element.343), channel_id=1, source_target_pairs={{0,16},{1,17},{2,18},{3,19},{4,20},{5,21},{6,22},{7,23},{8,24},{9,... | collective-permute-start | bytes 552968 | tf_op jit(solution)/shard_map/ppermute | solution.py:63
  313.0 17.5 %collective-permute-start.26 = (bf16[1,240,384]{2,1,0:T(8,128)(2,1)S(1)}, bf16[1,240,384]{2,1,0:T(8,128)(2,1)S(1)}, u32[]{:S(2)}, u32[]{:S(2)}) collective-permute-start(bf16[1,240,384]{2,1,0:T(8,128)(2,1)S(1)} %get-tuple-element.341), channel_id=1, source_target_pairs={{0,16},{1,17},{2,18},{3,19},{4,20},{5,21},{6,22},{7,23},{8,24},{9,... | collective-permute-start | bytes 552968 | tf_op jit(solution)/shard_map/ppermute | solution.py:63
  313.4 17.4 %collective-permute-start.25 = (bf16[2,288,256]{2,1,0:T(8,128)(2,1)S(1)}, bf16[2,288,256]{2,1,0:T(8,128)(2,1)S(1)}, u32[]{:S(2)}, u32[]{:S(2)}) collective-permute-start(bf16[2,288,256]{2,1,0:T(8,128)(2,1)S(1)} %get-tuple-element.339.refs_0_), channel_id=1, source_target_pairs={{0,8},{1,9},{2,10},{3,11},{4,12},{5,13},{6,14},{7,15},{8,0},{9,1},... | collective-permute-start | bytes 884744 | tf_op jit(solution)/shard_map/ppermute | solution.py:63
  322.4 15.4 %collective-permute-start.24 = (bf16[2,224,384]{2,1,0:T(8,128)(2,1)S(1)}, bf16[2,224,384]{2,1,0:T(8,128)(2,1)S(1)}, u32[]{:S(2)}, u32[]{:S(2)}) collective-permute-start(bf16[2,224,384]{2,1,0:T(8,128)(2,1)S(1)} %get-tuple-element.338), channel_id=1, source_target_pairs={{0,8},{1,9},{2,10},{3,11},{4,12},{5,13},{6,14},{7,15},{8,0},{9,1},... | collective-permute-start | bytes 1032200 | tf_op jit(solution)/shard_map/ppermute | solution.py:63
  327.7 11.2 %collective-permute-start.31 = (bf16[1,240,384]{2,1,0:T(8,128)(2,1)S(1)}, bf16[1,240,384]{2,1,0:T(8,128)(2,1)S(1)}, u32[]{:S(2)}, u32[]{:S(2)}) collective-permute-start(bf16[1,240,384]{2,1,0:T(8,128)(2,1)S(1)} %get-tuple-element.352.refs_0_), channel_id=1, source_target_pairs={{0,16},{1,17},{2,18},{3,19},{4,20},{5,21},{6,22},{7,23},{8,24},{9,... | collective-permute-start | bytes 552968 | tf_op jit(solution)/shard_map/ppermute | solution.py:63
  330.6 11.6 %collective-permute-start.30 = (bf16[1,240,384]{2,1,0:T(8,128)(2,1)S(1)}, bf16[1,240,384]{2,1,0:T(8,128)(2,1)S(1)}, u32[]{:S(2)}, u32[]{:S(2)}) collective-permute-start(bf16[1,240,384]{2,1,0:T(8,128)(2,1)S(1)} %get-tuple-element.351.refs_0_), channel_id=1, source_target_pairs={{0,16},{1,17},{2,18},{3,19},{4,20},{5,21},{6,22},{7,23},{8,24},{9,... | collective-permute-start | bytes 552968 | tf_op jit(solution)/shard_map/ppermute | solution.py:63
  330.9 13.9 %collective-permute-start.29 = (bf16[4,288,256]{2,1,0:T(8,128)(2,1)S(1)}, bf16[4,288,256]{2,1,0:T(8,128)(2,1)S(1)}, u32[]{:S(2)}, u32[]{:S(2)}) collective-permute-start(bf16[4,288,256]{2,1,0:T(8,128)(2,1)S(1)} %get-tuple-element.350.refs_0_), channel_id=1, source_target_pairs={{0,2},{1,5},{2,0},{3,7},{4,6},{5,1},{6,4},{7,3},{8,10},{9,13},{10,... | collective-permute-start | bytes 1769480 | tf_op jit(solution)/shard_map/ppermute | solution.py:63
  337.8 8.2 %collective-permute-start.28 = (bf16[1,224,384]{2,1,0:T(8,128)(2,1)S(1)}, bf16[1,224,384]{2,1,0:T(8,128)(2,1)S(1)}, u32[]{:S(2)}, u32[]{:S(2)}) collective-permute-start(bf16[1,224,384]{2,1,0:T(8,128)(2,1)S(1)} %get-tuple-element.349), channel_id=1, source_target_pairs={{0,16},{1,17},{2,18},{3,19},{4,20},{5,21},{6,22},{7,23},{8,24},{9,... | collective-permute-start | bytes 516104 | tf_op jit(solution)/shard_map/ppermute | solution.py:63
  339.0 10.6 %collective-permute-start.34 = (bf16[2,240,384]{2,1,0:T(8,128)(2,1)S(1)}, bf16[2,240,384]{2,1,0:T(8,128)(2,1)S(1)}, u32[]{:S(2)}, u32[]{:S(2)}) collective-permute-start(bf16[2,240,384]{2,1,0:T(8,128)(2,1)S(1)} %get-tuple-element.359.refs_0_), channel_id=1, source_target_pairs={{0,4},{1,3},{2,6},{3,1},{4,0},{5,7},{6,2},{7,5},{8,12},{9,11},{10,... | collective-permute-start | bytes 1105928 | tf_op jit(solution)/shard_map/ppermute | solution.py:63
  342.3 8.4 %collective-permute-start.33 = (bf16[2,240,384]{2,1,0:T(8,128)(2,1)S(1)}, bf16[2,240,384]{2,1,0:T(8,128)(2,1)S(1)}, u32[]{:S(2)}, u32[]{:S(2)}) collective-permute-start(bf16[2,240,384]{2,1,0:T(8,128)(2,1)S(1)} %get-tuple-element.358.refs_0_), channel_id=1, source_target_pairs={{0,8},{1,5},{2,10},{3,7},{4,12},{5,1},{6,14},{7,3},{8,0},{9,13},{1... | collective-permute-start | bytes 1105928 | tf_op jit(solution)/shard_map/ppermute | solution.py:63
  344.9 23.3 %collective-permute-start.38 = (bf16[8,288,256]{2,1,0:T(8,128)(2,1)S(1)}, bf16[8,288,256]{2,1,0:T(8,128)(2,1)S(1)}, u32[]{:S(2)}, u32[]{:S(2)}) collective-permute-start(bf16[8,288,256]{2,1,0:T(8,128)(2,1)S(1)} %get-tuple-element.366.refs_1_), channel_id=1, source_target_pairs={{0,1},{1,0},{2,3},{3,2},{4,5},{5,4},{6,7},{7,6},{8,9},{9,8},{10,11... | collective-permute-start | bytes 3538952 | tf_op jit(solution)/shard_map/ppermute | solution.py:48
  345.0 16.3 %collective-permute-start.40 = (bf16[8,288,256]{2,1,0:T(8,128)(2,1)S(1)}, bf16[8,288,256]{2,1,0:T(8,128)(2,1)S(1)}, u32[]{:S(2)}, u32[]{:S(2)}) collective-permute-start(bf16[8,288,256]{2,1,0:T(8,128)(2,1)S(1)} %get-tuple-element.366.refs_1_), channel_id=1, source_target_pairs={{0,4},{1,3},{2,6},{3,1},{4,0},{5,7},{6,2},{7,5},{8,12},{9,11},{10,... | collective-permute-start | bytes 3538952 | tf_op jit(solution)/shard_map/ppermute | solution.py:63
  346.1 11.5 %collective-permute-start.32 = (bf16[1,224,384]{2,1,0:T(8,128)(2,1)S(1)}, bf16[1,224,384]{2,1,0:T(8,128)(2,1)S(1)}, u32[]{:S(2)}, u32[]{:S(2)}) collective-permute-start(bf16[1,224,384]{2,1,0:T(8,128)(2,1)S(1)} %get-tuple-element.357.refs_0_), channel_id=1, source_target_pairs={{0,16},{1,17},{2,18},{3,19},{4,20},{5,21},{6,22},{7,23},{8,24},{9,... | collective-permute-start | bytes 516104 | tf_op jit(solution)/shard_map/ppermute | solution.py:63
  349.6 21.7 %collective-permute-start.37 = (bf16[4,240,384]{2,1,0:T(8,128)(2,1)S(1)}, bf16[4,240,384]{2,1,0:T(8,128)(2,1)S(1)}, u32[]{:S(2)}, u32[]{:S(2)}) collective-permute-start(bf16[4,240,384]{2,1,0:T(8,128)(2,1)S(1)} %get-tuple-element.365.refs_0_), channel_id=1, source_target_pairs={{0,2},{1,9},{2,0},{3,11},{4,6},{5,13},{6,4},{7,15},{8,10},{9,1},{1... | collective-permute-start | bytes 2211848 | tf_op jit(solution)/shard_map/ppermute | solution.py:63
  350.8 25.8 %collective-permute-start.36 = (bf16[4,240,384]{2,1,0:T(8,128)(2,1)S(1)}, bf16[4,240,384]{2,1,0:T(8,128)(2,1)S(1)}, u32[]{:S(2)}, u32[]{:S(2)}) collective-permute-start(bf16[4,240,384]{2,1,0:T(8,128)(2,1)S(1)} %get-tuple-element.364.refs_0_), channel_id=1, source_target_pairs={{0,2},{1,9},{2,0},{3,11},{4,6},{5,13},{6,4},{7,15},{8,10},{9,1},{1... | collective-permute-start | bytes 2211848 | tf_op jit(solution)/shard_map/ppermute | solution.py:63
  357.7 19.0 %collective-permute-start.35 = (bf16[2,224,384]{2,1,0:T(8,128)(2,1)S(1)}, bf16[2,224,384]{2,1,0:T(8,128)(2,1)S(1)}, u32[]{:S(2)}, u32[]{:S(2)}) collective-permute-start(bf16[2,224,384]{2,1,0:T(8,128)(2,1)S(1)} %get-tuple-element.363.refs_0_), channel_id=1, source_target_pairs={{0,8},{1,9},{2,10},{3,11},{4,12},{5,13},{6,14},{7,15},{8,0},{9,1},... | collective-permute-start | bytes 1032200 | tf_op jit(solution)/shard_map/ppermute | solution.py:63
  361.3 19.0 %collective-permute-start.41 = (bf16[8,288,256]{2,1,0:T(8,128)(2,1)S(1)}, bf16[8,288,256]{2,1,0:T(8,128)(2,1)S(1)}, u32[]{:S(2)}, u32[]{:S(2)}) collective-permute-start(bf16[8,288,256]{2,1,0:T(8,128)(2,1)S(1)} %collective-permute-done.40.refs_1_), channel_id=1, source_target_pairs={{0,1},{1,0},{2,3},{3,2},{4,5},{5,4},{6,7},{7,6},{8,9},{9,8},{10,11... | collective-permute-start | bytes 3538952 | tf_op jit(solution)/shard_map/ppermute | solution.py:48
  376.7 17.9 %collective-permute-start.39 = (bf16[4,224,384]{2,1,0:T(8,128)(2,1)S(1)}, bf16[4,224,384]{2,1,0:T(8,128)(2,1)S(1)}, u32[]{:S(2)}, u32[]{:S(2)}) collective-permute-start(bf16[4,224,384]{2,1,0:T(8,128)(2,1)S(1)} %get-tuple-element.371.refs_0_), channel_id=1, source_target_pairs={{0,4},{1,3},{2,6},{3,1},{4,0},{5,7},{6,2},{7,5},{8,12},{9,11},{10,... | collective-permute-start | bytes 2064392 | tf_op jit(solution)/shard_map/ppermute | solution.py:63
  377.8 17.9 %collective-permute-start.46 = (bf16[8,240,384]{2,1,0:T(8,128)(2,1)S(1)}, bf16[8,240,384]{2,1,0:T(8,128)(2,1)S(1)}, u32[]{:S(2)}, u32[]{:S(2)}) collective-permute-start(bf16[8,240,384]{2,1,0:T(8,128)(2,1)S(1)} %get-tuple-element.379.refs_1_), channel_id=1, source_target_pairs={{0,1},{1,0},{2,3},{3,2},{4,5},{5,4},{6,7},{7,6},{8,9},{9,8},{10,11... | collective-permute-start | bytes 4423688 | tf_op jit(solution)/shard_map/ppermute | solution.py:48
  378.2 19.4 %collective-permute-start.49 = (bf16[8,240,384]{2,1,0:T(8,128)(2,1)S(1)}, bf16[8,240,384]{2,1,0:T(8,128)(2,1)S(1)}, u32[]{:S(2)}, u32[]{:S(2)}) collective-permute-start(bf16[8,240,384]{2,1,0:T(8,128)(2,1)S(1)} %get-tuple-element.379.refs_1_), channel_id=1, source_target_pairs={{0,8},{1,5},{2,10},{3,7},{4,12},{5,1},{6,14},{7,3},{8,0},{9,13},{1... | collective-permute-start | bytes 4423688 | tf_op jit(solution)/shard_map/ppermute | solution.py:63
  380.2 53.7 %collective-permute-start.45 = (bf16[8,240,384]{2,1,0:T(8,128)(2,1)S(1)}, bf16[8,240,384]{2,1,0:T(8,128)(2,1)S(1)}, u32[]{:S(2)}, u32[]{:S(2)}) collective-permute-start(bf16[8,240,384]{2,1,0:T(8,128)(2,1)S(1)} %get-tuple-element.378.refs_1_), channel_id=1, source_target_pairs={{0,1},{1,0},{2,3},{3,2},{4,5},{5,4},{6,7},{7,6},{8,9},{9,8},{10,11... | collective-permute-start | bytes 4423688 | tf_op jit(solution)/shard_map/ppermute | solution.py:48
  380.2 46.0 %collective-permute-start.47 = (bf16[8,240,384]{2,1,0:T(8,128)(2,1)S(1)}, bf16[8,240,384]{2,1,0:T(8,128)(2,1)S(1)}, u32[]{:S(2)}, u32[]{:S(2)}) collective-permute-start(bf16[8,240,384]{2,1,0:T(8,128)(2,1)S(1)} %get-tuple-element.378.refs_1_), channel_id=1, source_target_pairs={{0,4},{1,3},{2,6},{3,1},{4,0},{5,7},{6,2},{7,5},{8,12},{9,11},{10,... | collective-permute-start | bytes 4423688 | tf_op jit(solution)/shard_map/ppermute | solution.py:63
  394.8 34.8 %collective-permute-start.42 = (bf16[8,224,384]{2,1,0:T(8,128)(2,1)S(1)}, bf16[8,224,384]{2,1,0:T(8,128)(2,1)S(1)}, u32[]{:S(2)}, u32[]{:S(2)}) collective-permute-start(bf16[8,224,384]{2,1,0:T(8,128)(2,1)S(1)} %get-tuple-element.377.refs_1_), channel_id=1, source_target_pairs={{0,2},{1,5},{2,0},{3,7},{4,6},{5,1},{6,4},{7,3},{8,10},{9,13},{10,... | collective-permute-start | bytes 4128776 | tf_op jit(solution)/shard_map/ppermute | solution.py:63
  395.7 41.4 %collective-permute-start.44 = (bf16[8,224,384]{2,1,0:T(8,128)(2,1)S(1)}, bf16[8,224,384]{2,1,0:T(8,128)(2,1)S(1)}, u32[]{:S(2)}, u32[]{:S(2)}) collective-permute-start(bf16[8,224,384]{2,1,0:T(8,128)(2,1)S(1)} %get-tuple-element.377.refs_1_), channel_id=1, source_target_pairs={{0,1},{1,0},{2,3},{3,2},{4,5},{5,4},{6,7},{7,6},{8,9},{9,8},{10,11... | collective-permute-start | bytes 4128776 | tf_op jit(solution)/shard_map/ppermute | solution.py:48
  397.6 42.9 %collective-permute-start.50 = (bf16[8,240,384]{2,1,0:T(8,128)(2,1)S(1)}, bf16[8,240,384]{2,1,0:T(8,128)(2,1)S(1)}, u32[]{:S(2)}, u32[]{:S(2)}) collective-permute-start(bf16[8,240,384]{2,1,0:T(8,128)(2,1)S(1)} %collective-permute-done.49.refs_1_), channel_id=1, source_target_pairs={{0,1},{1,0},{2,3},{3,2},{4,5},{5,4},{6,7},{7,6},{8,9},{9,8},{10,11... | collective-permute-start | bytes 4423688 | tf_op jit(solution)/shard_map/ppermute | solution.py:48
  426.2 17.6 %collective-permute-start.48 = (bf16[8,240,384]{2,1,0:T(8,128)(2,1)S(1)}, bf16[8,240,384]{2,1,0:T(8,128)(2,1)S(1)}, u32[]{:S(2)}, u32[]{:S(2)}) collective-permute-start(bf16[8,240,384]{2,1,0:T(8,128)(2,1)S(1)} %collective-permute-done.47.refs_1_), channel_id=1, source_target_pairs={{0,1},{1,0},{2,3},{3,2},{4,5},{5,4},{6,7},{7,6},{8,9},{9,8},{10,11... | collective-permute-start | bytes 4423688 | tf_op jit(solution)/shard_map/ppermute | solution.py:48
  429.6 17.5 %collective-permute-start.43 = (bf16[8,224,384]{2,1,0:T(8,128)(2,1)S(1)}, bf16[8,224,384]{2,1,0:T(8,128)(2,1)S(1)}, u32[]{:S(2)}, u32[]{:S(2)}) collective-permute-start(bf16[8,224,384]{2,1,0:T(8,128)(2,1)S(1)} %collective-permute-done.42.refs_1_), channel_id=1, source_target_pairs={{0,1},{1,0},{2,3},{3,2},{4,5},{5,4},{6,7},{7,6},{8,9},{9,8},{10,11... | collective-permute-start | bytes 4128776 | tf_op jit(solution)/shard_map/ppermute | solution.py:48
  (73 other events, 439.9 us)

commit v3 on v2

--- a/solution.py
+++ b/solution.py
@@ -13,7 +13,7 @@
 VMEM_LIMIT = 60 * 1024 * 1024
 DEC_BITS = ((1, 0, 2, 3), (0, 1, 2, 3))
 ENC_BITS = (((2, 0, 1, 3), (1, 2, 0, 3)), ((1, 0, 2, 3), (0, 2, 1, 3)), ((0, 1, 2, 3), (1, 0, 2, 3)))
-STEPS = "abdcabdcabdcabdcabdcabcdabcdcabcabc"
+STEPS = "abdcabdcabdcabdcabdcabcdabcdcabcabcabc"
 SHORT = 512
 WEIGHT_LIMIT = 40 * 1024 * 1024
 SMALL_LIMIT = 24 * 1024 * 1024
@@ -137,7 +137,8 @@
 
 
 class Bundle:
-    def __init__(self, order, bits, spots, tiles, entries, short=()):
+    def __init__(self, order, bits, spots, tiles, entries, short=(), late=True):
+        self.late = late
         self.order, self.run, self.entries = order, order.run, entries
         self.shards = min(16, lax.axis_size("dp"))
         self.bits = [[bit for bit in each if bit < bits_of(self.shards)] for each in bits]
@@ -351,7 +352,7 @@
 
     def step(self):
         bits = self.stages
-        for last, step in ((bits, self.halve), (bits + 1, self.own), (2 * bits, self.join), (2 * bits + 1, self.place_first)):
+        for last, step in ((bits, self.halve), (bits + 1, self.own), (2 * bits, self.join), (2 * bits + 1, self.place_first), (2 * bits + 1 + self.late, self.take)):
             if self.stage < last:
                 self.stage += 1
                 step()
@@ -410,7 +411,16 @@
 
     def place_first(self):
         self.half_placed = self.place(0, [])
-        self.other.append(across(self.held[1], "blk", 0))
+        if not self.late:
+            self.other.append(across(self.held[1], "blk", 0))
+
+    def take(self):
+        def kernel(in_ref, out_ref):
+            out_ref[...] = in_ref[...]
+
+        (late,) = self.order.run_small(kernel, "take", [self.held[1]], [self.shaped(self.held[1].shape[0])])
+        self.held = (self.held[0], late)
+        self.other.append(across(late, "blk", 0))
 
     def place(self, part, earlier):
         entries, shards, slots = self.entries, self.shards, self.shards
@@ -1203,14 +1213,15 @@
     )
     d_back = across(d_back, "blk", 0)
 
-    def bundle(bits, *entries, short=()):
-        return Bundle(order, bits, spots, meta, [Entry(*entry) for entry in entries], short)
+    def bundle(bits, *entries, short=(), late=True):
+        return Bundle(order, bits, spots, meta, [Entry(*entry) for entry in entries], short, late)
 
     dec = bundle(
         DEC_BITS,
         ("wide", d_n2, d_ub, rd, 4, dd // 2, dec_up.shape, False),
         ("tall", d_g, cotangent, rd, 4, dd // 2, dec_down.shape, False),
         ("wide", d_o, d_mb, rd, 1, dd // 2, dec_out.shape, False),
+        late=False,
     )
     dec.weigh()
     d_dqkv, lb, d_gaina, d_shifta, embed_b, token_grad = dec_head(

time: 457 us -> 454 us (level)
  waiting for transfers between devices: 90.8 us -> 82.8 us
    ppermute x32, waiting for transfers between devices: 83.2 us -> 75.3 us  [across_bits(): return lax.ppermute(value, ('dp', 'blk'), pairs)]
    pallas_call x40 -> x43, Pallas kernels: 39.8 us -> 40.1 us  [run_small(): pl.pallas_call(body, out_shape=[*out_shape, TOKEN], in_specs=in_specs, ou...]
where the time goes in v3:
time: 454 us; the launch traced here: 450 us
  Pallas kernels  236 us (52%)
  starting transfers between devices  87.3 us (19%)
  waiting for transfers between devices  82.8 us (18%)
  local copies, waits for them, and re-layouts  36.8 us (8%)
  other arithmetic  5.45 us (1%)
    pallas_call x11, Pallas kernels, run(): pl.pallas_call(body, out_shape=[*out_shape, TOKEN], grid_spec=pltpu.Prefe...  196 us
    ppermute x32, waiting for transfers between devices, across_bits(): return lax.ppermute(value, ('dp', 'blk'), pairs)  75.3 us
    ppermute x32, starting transfers between devices, across_bits(): return lax.ppermute(value, ('dp', 'blk'), pairs)  54.2 us
    pallas_call x43, Pallas kernels, run_small(): pl.pallas_call(body, out_shape=[*out_shape, TOKEN], in_specs=in_specs, ou...  40.1 us
    ppermute x19, starting transfers between devices, across(): return lax.ppermute(value, axis, [(i, i ^ 1 << bit) for i in range(count)])  33.2 us
    unnamed x140, local copies, waits for them, and re-layouts  31.7 us
  transfers between devices with their start and end apart: 51, of which 14 were waited for; matrix products, arithmetic and copies ran while one was open for 2% of the time, Pallas kernels for 21%

profile of v3, /device:TPU:0, one launch (start us, length us, event | category | flops | bytes accessed | tf_op | source)
XLA Modules:
  0.0 450.0 jit_solution(12427833348831064882)
XLA Ops:
  9.6 8.2 %enc_in.1 = (bf16[768,768]{1,0:T(8,128)(2,1)}, f32[16,768]{1,0:T(8,128)}, f32[16,768]{1,0:T(8,128)}, f32[768,16]{1,0:T(8,128)}, f32[16,768]{1,0:T(8,128)}, /*ind...) custom-call(s32[2]{0:T(128)} %fusion.meta, ...), custom_call_target="tpu_custom_call" | custom-call | flops 8049999872 | bytes 25200000 | tf_op jit(solution)/shard_map/enc_in/pallas_call | solution.py:84
  18.6 4.0 collective-permute-done.3.refs_3_.refs_6_
  24.1 20.1 %enc_main.1 = (bf16[768,768]{1,0:T(8,128)(2,1)}, f32[768,128]{1,0:T(8,128)}, f32[768,768]{1,0:T(8,128)}, bf16[768,768]{1,0:T(8,128)(2,1)}, bf16[768,3072]{1,0:T(...) custom-call(s32[2]{0:T(128)} %fusion.meta, ...), custom_call_target="tpu_custom_call" | custom-call | flops 23000000512 | bytes 72000000 | tf_op jit(solution)/shard_map/enc_main/pallas_call | solution.py:84
  44.2 7.4 %dec_in.1 = (f32[768,512]{1,0:T(8,128)}, bf16[768,512]{1,0:T(8,128)(2,1)}, bf16[768,512]{1,0:T(8,128)(2,1)}, bf16[768,1024]{1,0:T(8,128)(2,1)}, f32[8,128]{1,0:T(8,128)}) custom-call(s32[2]{0:T(128)} %fusion.meta, bf16[768,768]{1,0:T(8,128)(2,1)} %get-tuple-element.221.refs_0_, bf16[768,512]{1,0:T(8,128)(2,1)} %get-tuple-element.229.refs_1_, ...), custom_call_target="tpu_custom_call" | custom-call | flops 8049999872 | bytes 25200000 | tf_op jit(solution)/shard_map/dec_in/pallas_call | solution.py:84
  51.7 3.5 collective-permute-done.4.refs_3_
  56.3 94.6 %dec_main.1 = (bf16[768,512]{1,0:T(8,128)(2,1)}, bf16[768,512]{1,0:T(8,128)(2,1)}, bf16[768,512]{1,0:T(8,128)(2,1)}, bf16[768,2048]{1,0:T(8,128)(2,1)}, bf16[768...) custom-call(s32[2]{0:T(128)} %fusion.meta, ...), custom_call_target="tpu_custom_call" | custom-call | flops 109250002944 | bytes 342000000 | tf_op jit(solution)/shard_map/dec_main/pallas_call | solution.py:84
  159.1 8.0 %weight_grads.4 = (bf16[16,288,256]{2,1,0:T(8,128)(2,1)S(1)}, bf16[16,288,256]{2,1,0:T(8,128)(2,1)S(1)}, f32[8,128]{1,0:T(8,128)S(1)}) custom-call(s32[3]{0:T(128)S(1)} %pad_add_fusion.meta, bf16[768,512]{1,0:T(8,128)(2,1)S(1)} %copy-done.22, bf16[768,2048]{1,0:T(8,128)(2,1)S(1)} %copy-done.17, bf16[768,2048]{1,0:T(8,128)(2,1)S(1)} %copy-done.17, ...), custom_call_target="tpu_custom_call" | custom-call | flops 6899999744 | bytes 21600000 | tf_op jit(solution)/shard_map/weight_grads/pallas_call | solution.py:84
  169.5 8.1 %dec_head.1 = (bf16[768,1536]{1,0:T(8,128)(2,1)}, bf16[768,512]{1,0:T(8,128)(2,1)}, f32[1,512]{1,0:T(1,128)}, f32[1,512]{1,0:T(1,128)}, f32[1,512]{1,0:T(1,128)}, /*index=5*/f32[1,512]{1,0:T(1,128)}, f32[8,128]{1,0:T(8,128)}) custom-call(s32[2]{0:T(128)} %fusion.meta, f32[768,512]{1,0:T(8,128)} %get-tuple-element.233.refs_0_, ...), custom_call_target="tpu_custom_call" | custom-call | flops 46000001024 | bytes 144000000 | tf_op jit(solution)/shard_map/dec_head/pallas_call | solution.py:84
  179.9 2.3 halve.16
  183.8 2.6 collective-permute-start.8
  186.4 24.6 %enc_back.1 = (bf16[768,512]{1,0:T(8,128)(2,1)}, bf16[768,768]{1,0:T(8,128)(2,1)}, bf16[768,3072]{1,0:T(8,128)(2,1)}, bf16[768,768]{1,0:T(8,128)(2,1)}, f32[768,...) custom-call(s32[2]{0:T(128)} %fusion.meta, ...), custom_call_target="tpu_custom_call" | custom-call | flops 27599998976 | bytes 86400000 | tf_op jit(solution)/shard_map/enc_back/pallas_call | solution.py:84
  216.6 5.1 %weight_grads.5 = (bf16[16,240,384]{2,1,0:T(8,128)(2,1)S(1)}, bf16[16,240,384]{2,1,0:T(8,128)(2,1)S(1)}, f32[8,128]{1,0:T(8,128)S(1)}) custom-call(s32[3]{0:T(128)S(1)} %pad_add_fusion.meta, bf16[3,256,768]{2,1,0:T(8,128)(2,1)S(1)} %bitcast.48, bf16[3,256,3072]{2,1,0:T(8,128)(2,1)S(1)} %bitcast.36, bf16[3,256,3072]{2,1,0:T(8,128)(2,1)S(1)} %bitcast.37, ...), custom_call_target="tpu_custom_call" | custom-call | flops 6899999744 | bytes 21600000 | tf_op jit(solution)/shard_map/weight_grads/pallas_call | solution.py:84
  223.8 2.3 copy-done.1
  226.1 5.3 %weight_grads.6 = (bf16[16,240,384]{2,1,0:T(8,128)(2,1)S(1)}, bf16[16,240,384]{2,1,0:T(8,128)(2,1)S(1)}, f32[8,128]{1,0:T(8,128)S(1)}) custom-call(s32[3]{0:T(128)S(1)} %pad_add_fusion.meta, bf16[3,256,3072]{2,1,0:T(8,128)(2,1)S(1)} %bitcast.34, bf16[3,256,768]{2,1,0:T(8,128)(2,1)S(1)} %bitcast.50, bf16[3,256,768]{2,1,0:T(8,128)(2,1)S(1)} %bitcast.51, ...), custom_call_target="tpu_custom_call" | custom-call | flops 6899999744 | bytes 21600000 | tf_op jit(solution)/shard_map/weight_grads/pallas_call | solution.py:84
  238.2 8.3 %enc_head.1 = (bf16[768,2304]{1,0:T(8,128)(2,1)}, bf16[768,768]{1,0:T(8,128)(2,1)}, f32[1,768]{1,0:T(1,128)}, f32[1,768]{1,0:T(1,128)}, f32[8,128]{1,0:T(8,128)}) custom-call(s32[2]{0:T(128)} %fusion.meta, bf16[768,768]{1,0:T(8,128)(2,1)} %get-tuple-element.221.refs_0_, bf16[768,768]{1,0:T(8,128)(2,1)} %get-tuple-element.222.refs_0_.refs_1_, ...), custom_call_target="tpu_custom_call" | custom-call | flops 9200000000 | bytes 28800000 | tf_op jit(solution)/shard_map/enc_head/pallas_call | solution.py:84
  249.1 2.7 halve.19
  255.9 6.2 %weight_grads.7 = (bf16[16,224,384]{2,1,0:T(8,128)(2,1)S(1)}, bf16[16,224,384]{2,1,0:T(8,128)(2,1)S(1)}, f32[8,128]{1,0:T(8,128)S(1)}) custom-call(s32[3]{0:T(128)S(1)} %pad_add_fusion.meta, bf16[3,256,768]{2,1,0:T(8,128)(2,1)S(1)} %bitcast.42, bf16[3,256,2304]{2,1,0:T(8,128)(2,1)S(1)} %bitcast.39, bf16[3,256,2304]{2,1,0:T(8,128)(2,1)S(1)} %bitcast.40, ...), custom_call_target="tpu_custom_call" | custom-call | flops 6899999744 | bytes 21600000 | tf_op jit(solution)/shard_map/weight_grads/pallas_call | solution.py:84
  265.5 7.0 %collective-permute-done.14.refs_1_ = bf16[8,240,384]{2,1,0:T(8,128)(2,1)S(1)} collective-permute-done((bf16[8,240,384]{2,1,0:T(8,128)(2,1)S(1)}, bf16[8,240,384]{2,1,0:T(8,128)(2,1)S(1)}, u32[]{:S(2)}, u32[]{:S(2)}) %collective-permute-start.14) | collective-permute-done | bytes 1474592 | tf_op jit(solution)/shard_map/ppermute | solution.py:63
  276.0 2.6 collective-permute-start.17
  280.0 8.7 %collective-permute-done.18.refs_1_ = bf16[4,240,384]{2,1,0:T(8,128)(2,1)S(1)} collective-permute-done((bf16[4,240,384]{2,1,0:T(8,128)(2,1)S(1)}, bf16[4,240,384]{2,1,0:T(8,128)(2,1)S(1)}, u32[]{:S(2)}, u32[]{:S(2)}) %collective-permute-start.18) | collective-permute-done | bytes 737312 | tf_op jit(solution)/shard_map/ppermute | solution.py:63
  290.7 2.7 collective-permute-start.21
  293.3 15.2 %collective-permute-done.16.refs_1_ = bf16[8,224,384]{2,1,0:T(8,128)(2,1)S(1)} collective-permute-done((bf16[8,224,384]{2,1,0:T(8,128)(2,1)S(1)}, bf16[8,224,384]{2,1,0:T(8,128)(2,1)S(1)}, u32[]{:S(2)}, u32[]{:S(2)}) %collective-permute-start.16) | collective-permute-done | bytes 1376288 | tf_op jit(solution)/shard_map/ppermute | solution.py:63
  310.3 2.6 collective-permute-start.27
  313.5 2.9 collective-permute-start.25
  316.4 5.8 %collective-permute-done.20.refs_1_ = bf16[4,224,384]{2,1,0:T(8,128)(2,1)S(1)} collective-permute-done((bf16[4,224,384]{2,1,0:T(8,128)(2,1)S(1)}, bf16[4,224,384]{2,1,0:T(8,128)(2,1)S(1)}, u32[]{:S(2)}, u32[]{:S(2)}) %collective-permute-start.20) | collective-permute-done | bytes 688160 | tf_op jit(solution)/shard_map/ppermute | solution.py:63
  322.4 5.3 %collective-permute-start.24 = (bf16[2,224,384]{2,1,0:T(8,128)(2,1)S(1)}, bf16[2,224,384]{2,1,0:T(8,128)(2,1)S(1)}, u32[]{:S(2)}, u32[]{:S(2)}) collective-permute-start(bf16[2,224,384]{2,1,0:T(8,128)(2,1)S(1)} %get-tuple-element.344), channel_id=1, source_target_pairs={{0,8},{1,9},{2,10},{3,11},{4,12},{5,13},{6,14},{7,15},{8,0},{9,1},... | collective-permute-start | bytes 1032200 | tf_op jit(solution)/shard_map/ppermute | solution.py:63
  327.8 2.7 collective-permute-start.31
  332.0 5.8 %collective-permute-done.24.refs_1_ = bf16[2,224,384]{2,1,0:T(8,128)(2,1)S(1)} collective-permute-done((bf16[2,224,384]{2,1,0:T(8,128)(2,1)S(1)}, bf16[2,224,384]{2,1,0:T(8,128)(2,1)S(1)}, u32[]{:S(2)}, u32[]{:S(2)}) %collective-permute-start.24) | collective-permute-done | bytes 344096 | tf_op jit(solution)/shard_map/ppermute | solution.py:63
  342.4 2.6 collective-permute-start.33
  346.2 3.4 collective-permute-start.32
  351.9 5.7 %collective-permute-done.32.refs_1_ = bf16[1,224,384]{2,1,0:T(8,128)(2,1)S(1)} collective-permute-done((bf16[1,224,384]{2,1,0:T(8,128)(2,1)S(1)}, bf16[1,224,384]{2,1,0:T(8,128)(2,1)S(1)}, u32[]{:S(2)}, u32[]{:S(2)}) %collective-permute-start.32) | collective-permute-done | bytes 172064 | tf_op jit(solution)/shard_map/ppermute | solution.py:63
  359.2 2.2 collective-permute-done.40.refs_1_
  361.4 7.0 %collective-permute-start.41 = (bf16[8,288,256]{2,1,0:T(8,128)(2,1)S(1)}, bf16[8,288,256]{2,1,0:T(8,128)(2,1)S(1)}, u32[]{:S(2)}, u32[]{:S(2)}) collective-permute-start(bf16[8,288,256]{2,1,0:T(8,128)(2,1)S(1)} %collective-permute-done.40.refs_1_), channel_id=1, source_target_pairs={{0,1},{1,0},{2,3},{3,2},{4,5},{5,4},{6,7},{7,6},{8,9},{9,8},{10,11... | collective-permute-start | bytes 3538952 | tf_op jit(solution)/shard_map/ppermute | solution.py:48
  368.4 3.1 place_shards.8
  371.6 5.0 %collective-permute-done.36.refs_1_ = bf16[4,240,384]{2,1,0:T(8,128)(2,1)S(1)} collective-permute-done((bf16[4,240,384]{2,1,0:T(8,128)(2,1)S(1)}, bf16[4,240,384]{2,1,0:T(8,128)(2,1)S(1)}, u32[]{:S(2)}, u32[]{:S(2)}) %collective-permute-start.36) | collective-permute-done | bytes 737312 | tf_op jit(solution)/shard_map/ppermute | solution.py:63
  378.4 3.1 place_shards.9
  381.5 6.3 %collective-permute-done.39.refs_1_ = bf16[4,224,384]{2,1,0:T(8,128)(2,1)S(1)} collective-permute-done((bf16[4,224,384]{2,1,0:T(8,128)(2,1)S(1)}, bf16[4,224,384]{2,1,0:T(8,128)(2,1)S(1)}, u32[]{:S(2)}, u32[]{:S(2)}) %collective-permute-start.39) | collective-permute-done | bytes 688160 | tf_op jit(solution)/shard_map/ppermute | solution.py:63
  388.1 2.6 collective-permute-start.44
  392.7 3.4 place_shards.10
  396.1 3.2 place_shards.11
  399.4 3.3 place_shards.12
  402.6 5.4 %collective-permute-done.44.refs_0_ = bf16[8,240,384]{2,1,0:T(8,128)(2,1)S(1)} collective-permute-done((bf16[8,240,384]{2,1,0:T(8,128)(2,1)S(1)}, bf16[8,240,384]{2,1,0:T(8,128)(2,1)S(1)}, u32[]{:S(2)}, u32[]{:S(2)}) %collective-permute-start.44) | collective-permute-done | bytes 1474592 | tf_op jit(solution)/shard_map/ppermute | solution.py:63
  408.2 11.7 %collective-permute-start.50 = (bf16[8,240,384]{2,1,0:T(8,128)(2,1)S(1)}, bf16[8,240,384]{2,1,0:T(8,128)(2,1)S(1)}, u32[]{:S(2)}, u32[]{:S(2)}) collective-permute-start(bf16[8,240,384]{2,1,0:T(8,128)(2,1)S(1)} %get-tuple-element.399.refs_1_), channel_id=1, source_target_pairs={{0,1},{1,0},{2,3},{3,2},{4,5},{5,4},{6,7},{7,6},{8,9},{9,8},{10,11... | collective-permute-start | bytes 4423688 | tf_op jit(solution)/shard_map/ppermute | solution.py:48
  419.8 6.1 %collective-permute-done.43.refs_0_ = bf16[8,240,384]{2,1,0:T(8,128)(2,1)S(1)} collective-permute-done((bf16[8,240,384]{2,1,0:T(8,128)(2,1)S(1)}, bf16[8,240,384]{2,1,0:T(8,128)(2,1)S(1)}, u32[]{:S(2)}, u32[]{:S(2)}) %collective-permute-start.43) | collective-permute-done | bytes 1474592 | tf_op jit(solution)/shard_map/ppermute | solution.py:63
  426.3 11.2 %collective-permute-start.48 = (bf16[8,224,384]{2,1,0:T(8,128)(2,1)S(1)}, bf16[8,224,384]{2,1,0:T(8,128)(2,1)S(1)}, u32[]{:S(2)}, u32[]{:S(2)}) collective-permute-start(bf16[8,224,384]{2,1,0:T(8,128)(2,1)S(1)} %get-tuple-element.392.refs_1_), channel_id=1, source_target_pairs={{0,1},{1,0},{2,3},{3,2},{4,5},{5,4},{6,7},{7,6},{8,9},{9,8},{10,11... | collective-permute-start | bytes 4128776 | tf_op jit(solution)/shard_map/ppermute | solution.py:48
  437.5 3.4 place_shards.13
  440.9 3.2 place_shards.14
  444.1 3.3 place_shards.15
  (264 shorter events, 78.6 us)
Async XLA Ops:
  2.5 6.5 %collective-permute-start.1 = (s32[1,768]{1,0:T(1,128)S(1)}, s32[1,768]{1,0:T(1,128)S(1)}, u32[]{:S(2)}, u32[]{:S(2)}) collective-permute-start(s32[1,768]{1,0:T(1,128)S(1)} %reshape.112.refs_2_), channel_id=1, source_target_pairs={{0,1},{1,0},{2,3},{3,2},{4,5},{5,4},{6,7},{7,6},{8,9},{9,8},{10,11... | collective-permute-start | bytes 9224 | tf_op jit(solution)/shard_map/ppermute | solution.py:48
  3.3 5.7 %collective-permute-start.2 = (s32[1,768]{1,0:T(1,128)S(1)}, s32[1,768]{1,0:T(1,128)S(1)}, u32[]{:S(2)}, u32[]{:S(2)}) collective-permute-start(s32[1,768]{1,0:T(1,128)S(1)} %reshape.113.refs_3_), channel_id=1, source_target_pairs={{0,1},{1,0},{2,3},{3,2},{4,5},{5,4},{6,7},{7,6},{8,9},{9,8},{10,11... | collective-permute-start | bytes 9224 | tf_op jit(solution)/shard_map/ppermute | solution.py:48
  150.9 18.5 %collective-permute-start.5 = (bf16[768,1024]{1,0:T(8,128)(2,1)}, bf16[768,1024]{1,0:T(8,128)(2,1)}, u32[]{:S(2)}, u32[]{:S(2)}) collective-permute-start(bf16[768,1024]{1,0:T(8,128)(2,1)} %get-tuple-element.242), channel_id=1, source_target_pairs={{0,1},{1,0},{2,3},{3,2},{4,5},{5,4},{6,7},{7,6},{8,9},{9,8},{10,11... | collective-permute-start | bytes 4718600 | tf_op jit(solution)/shard_map/ppermute | solution.py:48
  169.1 8.5 %collective-permute-start.6 = (bf16[16,288,256]{2,1,0:T(8,128)(2,1)S(1)}, bf16[16,288,256]{2,1,0:T(8,128)(2,1)}, u32[]{:S(2)}, u32[]{:S(2)}) collective-permute-start(bf16[16,288,256]{2,1,0:T(8,128)(2,1)S(1)} %get-tuple-element.257), channel_id=1, source_target_pairs={{0,1},{1,0},{2,3},{3,2},{4,5},{5,4},{6,7},{7,6},{8,9},{9,8},{10,11... | collective-permute-start | bytes 7077896 | tf_op jit(solution)/shard_map/ppermute | solution.py:48
  183.8 27.2 %collective-permute-start.8 = (bf16[8,288,256]{2,1,0:T(8,128)(2,1)S(1)}, bf16[8,288,256]{2,1,0:T(8,128)(2,1)S(1)}, u32[]{:S(2)}, u32[]{:S(2)}) collective-permute-start(bf16[8,288,256]{2,1,0:T(8,128)(2,1)S(1)} %get-tuple-element.268), channel_id=1, source_target_pairs={{0,4},{1,3},{2,6},{3,1},{4,0},{5,7},{6,2},{7,5},{8,12},{9,11},{10,... | collective-permute-start | bytes 3538952 | tf_op jit(solution)/shard_map/ppermute | solution.py:63
  223.3 9.8 %collective-permute-start.9 = (bf16[16,240,384]{2,1,0:T(8,128)(2,1)S(1)}, bf16[16,240,384]{2,1,0:T(8,128)(2,1)S(1)}, u32[]{:S(2)}, u32[]{:S(2)}) collective-permute-start(bf16[16,240,384]{2,1,0:T(8,128)(2,1)S(1)} %get-tuple-element.272), channel_id=1, source_target_pairs={{0,1},{1,0},{2,3},{3,2},{4,5},{5,4},{6,7},{7,6},{8,9},{9,8},{10,11... | collective-permute-start | bytes 8847368 | tf_op jit(solution)/shard_map/ppermute | solution.py:48
  223.3 14.9 %collective-permute-start.7 = (bf16[768,1536]{1,0:T(8,128)(2,1)}, bf16[768,1536]{1,0:T(8,128)(2,1)}, u32[]{:S(2)}, u32[]{:S(2)}) collective-permute-start(bf16[768,1536]{1,0:T(8,128)(2,1)} %get-tuple-element.262), channel_id=1, source_target_pairs={{0,1},{1,0},{2,3},{3,2},{4,5},{5,4},{6,7},{7,6},{8,9},{9,8},{10,11... | collective-permute-start | bytes 7077896 | tf_op jit(solution)/shard_map/ppermute | solution.py:48
  231.5 15.1 %collective-permute-start.11 = (bf16[16,240,384]{2,1,0:T(8,128)(2,1)S(1)}, bf16[16,240,384]{2,1,0:T(8,128)(2,1)}, u32[]{:S(2)}, u32[]{:S(2)}) collective-permute-start(bf16[16,240,384]{2,1,0:T(8,128)(2,1)S(1)} %get-tuple-element.304), channel_id=1, source_target_pairs={{0,1},{1,0},{2,3},{3,2},{4,5},{5,4},{6,7},{7,6},{8,9},{9,8},{10,11... | collective-permute-start | bytes 8847368 | tf_op jit(solution)/shard_map/ppermute | solution.py:48
  231.6 20.8 %collective-permute-start.10 = (bf16[4,288,256]{2,1,0:T(8,128)(2,1)S(1)}, bf16[4,288,256]{2,1,0:T(8,128)(2,1)}, u32[]{:S(2)}, u32[]{:S(2)}) collective-permute-start(bf16[4,288,256]{2,1,0:T(8,128)(2,1)S(1)} %get-tuple-element.302), channel_id=1, source_target_pairs={{0,2},{1,5},{2,0},{3,7},{4,6},{5,1},{6,4},{7,3},{8,10},{9,13},{10,... | collective-permute-start | bytes 1769480 | tf_op jit(solution)/shard_map/ppermute | solution.py:63
  236.7 25.5 %collective-permute-start.15 = (bf16[8,240,384]{2,1,0:T(8,128)(2,1)}, bf16[8,240,384]{2,1,0:T(8,128)(2,1)}, u32[]{:S(2)}, u32[]{:S(2)}) collective-permute-start(bf16[8,240,384]{2,1,0:T(8,128)(2,1)} %get-tuple-element.315), channel_id=1, source_target_pairs={{0,8},{1,5},{2,10},{3,7},{4,12},{5,1},{6,14},{7,3},{8,0},{9,13},{1... | collective-permute-start | bytes 4423688 | tf_op jit(solution)/shard_map/ppermute | solution.py:63
  251.7 20.8 %collective-permute-start.14 = (bf16[8,240,384]{2,1,0:T(8,128)(2,1)S(1)}, bf16[8,240,384]{2,1,0:T(8,128)(2,1)S(1)}, u32[]{:S(2)}, u32[]{:S(2)}) collective-permute-start(bf16[8,240,384]{2,1,0:T(8,128)(2,1)S(1)} %get-tuple-element.313), channel_id=1, source_target_pairs={{0,4},{1,3},{2,6},{3,1},{4,0},{5,7},{6,2},{7,5},{8,12},{9,11},{10,... | collective-permute-start | bytes 4423688 | tf_op jit(solution)/shard_map/ppermute | solution.py:63
  254.1 20.4 %collective-permute-start.13 = (bf16[2,288,256]{2,1,0:T(8,128)(2,1)S(1)}, bf16[2,288,256]{2,1,0:T(8,128)(2,1)S(1)}, u32[]{:S(2)}, u32[]{:S(2)}) collective-permute-start(bf16[2,288,256]{2,1,0:T(8,128)(2,1)S(1)} %get-tuple-element.311), channel_id=1, source_target_pairs={{0,8},{1,9},{2,10},{3,11},{4,12},{5,13},{6,14},{7,15},{8,0},{9,1},... | collective-permute-start | bytes 884744 | tf_op jit(solution)/shard_map/ppermute | solution.py:63
  262.1 12.5 %collective-permute-start.12 = (bf16[16,224,384]{2,1,0:T(8,128)(2,1)S(1)}, bf16[16,224,384]{2,1,0:T(8,128)(2,1)S(1)}, u32[]{:S(2)}, u32[]{:S(2)}) collective-permute-start(bf16[16,224,384]{2,1,0:T(8,128)(2,1)S(1)} %get-tuple-element.309), channel_id=1, source_target_pairs={{0,1},{1,0},{2,3},{3,2},{4,5},{5,4},{6,7},{7,6},{8,9},{9,8},{10,11... | collective-permute-start | bytes 8257544 | tf_op jit(solution)/shard_map/ppermute | solution.py:48
  264.0 14.7 %collective-permute-start.19 = (bf16[4,240,384]{2,1,0:T(8,128)(2,1)S(1)}, bf16[4,240,384]{2,1,0:T(8,128)(2,1)S(1)}, u32[]{:S(2)}, u32[]{:S(2)}) collective-permute-start(bf16[4,240,384]{2,1,0:T(8,128)(2,1)S(1)} %get-tuple-element.327), channel_id=1, source_target_pairs={{0,2},{1,9},{2,0},{3,11},{4,6},{5,13},{6,4},{7,15},{8,10},{9,1},{1... | collective-permute-start | bytes 2211848 | tf_op jit(solution)/shard_map/ppermute | solution.py:63
  273.0 15.8 %collective-permute-start.18 = (bf16[4,240,384]{2,1,0:T(8,128)(2,1)S(1)}, bf16[4,240,384]{2,1,0:T(8,128)(2,1)S(1)}, u32[]{:S(2)}, u32[]{:S(2)}) collective-permute-start(bf16[4,240,384]{2,1,0:T(8,128)(2,1)S(1)} %get-tuple-element.325), channel_id=1, source_target_pairs={{0,2},{1,9},{2,0},{3,11},{4,6},{5,13},{6,4},{7,15},{8,10},{9,1},{1... | collective-permute-start | bytes 2211848 | tf_op jit(solution)/shard_map/ppermute | solution.py:63
  275.4 33.2 %collective-permute-start.16 = (bf16[8,224,384]{2,1,0:T(8,128)(2,1)S(1)}, bf16[8,224,384]{2,1,0:T(8,128)(2,1)S(1)}, u32[]{:S(2)}, u32[]{:S(2)}) collective-permute-start(bf16[8,224,384]{2,1,0:T(8,128)(2,1)S(1)} %get-tuple-element.321), channel_id=1, source_target_pairs={{0,2},{1,5},{2,0},{3,7},{4,6},{5,1},{6,4},{7,3},{8,10},{9,13},{10,... | collective-permute-start | bytes 4128776 | tf_op jit(solution)/shard_map/ppermute | solution.py:63
  276.0 14.6 %collective-permute-start.17 = (bf16[1,288,256]{2,1,0:T(8,128)(2,1)S(1)}, bf16[1,288,256]{2,1,0:T(8,128)(2,1)S(1)}, u32[]{:S(2)}, u32[]{:S(2)}) collective-permute-start(bf16[1,288,256]{2,1,0:T(8,128)(2,1)S(1)} %get-tuple-element.323), channel_id=1, source_target_pairs={{0,16},{1,17},{2,18},{3,19},{4,20},{5,21},{6,22},{7,23},{8,24},{9,... | collective-permute-start | bytes 442376 | tf_op jit(solution)/shard_map/ppermute | solution.py:63
  278.8 31.4 %collective-permute-start.23 = (bf16[2,240,384]{2,1,0:T(8,128)(2,1)S(1)}, bf16[2,240,384]{2,1,0:T(8,128)(2,1)S(1)}, u32[]{:S(2)}, u32[]{:S(2)}) collective-permute-start(bf16[2,240,384]{2,1,0:T(8,128)(2,1)S(1)} %get-tuple-element.338), channel_id=1, source_target_pairs={{0,4},{1,3},{2,6},{3,1},{4,0},{5,7},{6,2},{7,5},{8,12},{9,11},{10,... | collective-permute-start | bytes 1105928 | tf_op jit(solution)/shard_map/ppermute | solution.py:63
  289.0 24.0 %collective-permute-start.22 = (bf16[2,240,384]{2,1,0:T(8,128)(2,1)S(1)}, bf16[2,240,384]{2,1,0:T(8,128)(2,1)S(1)}, u32[]{:S(2)}, u32[]{:S(2)}) collective-permute-start(bf16[2,240,384]{2,1,0:T(8,128)(2,1)S(1)} %get-tuple-element.336), channel_id=1, source_target_pairs={{0,8},{1,5},{2,10},{3,7},{4,12},{5,1},{6,14},{7,3},{8,0},{9,13},{1... | collective-permute-start | bytes 1105928 | tf_op jit(solution)/shard_map/ppermute | solution.py:63
  290.7 22.8 %collective-permute-start.21 = (bf16[1,288,256]{2,1,0:T(8,128)(2,1)S(1)}, bf16[1,288,256]{2,1,0:T(8,128)(2,1)S(1)}, u32[]{:S(2)}, u32[]{:S(2)}) collective-permute-start(bf16[1,288,256]{2,1,0:T(8,128)(2,1)S(1)} %get-tuple-element.334.refs_0_), channel_id=1, source_target_pairs={{0,16},{1,17},{2,18},{3,19},{4,20},{5,21},{6,22},{7,23},{8,24},{9,... | collective-permute-start | bytes 442376 | tf_op jit(solution)/shard_map/ppermute | solution.py:63
  308.9 13.3 %collective-permute-start.20 = (bf16[4,224,384]{2,1,0:T(8,128)(2,1)S(1)}, bf16[4,224,384]{2,1,0:T(8,128)(2,1)S(1)}, u32[]{:S(2)}, u32[]{:S(2)}) collective-permute-start(bf16[4,224,384]{2,1,0:T(8,128)(2,1)S(1)} %get-tuple-element.333), channel_id=1, source_target_pairs={{0,4},{1,3},{2,6},{3,1},{4,0},{5,7},{6,2},{7,5},{8,12},{9,11},{10,... | collective-permute-start | bytes 2064392 | tf_op jit(solution)/shard_map/ppermute | solution.py:63
  310.3 17.4 %collective-permute-start.27 = (bf16[1,240,384]{2,1,0:T(8,128)(2,1)S(1)}, bf16[1,240,384]{2,1,0:T(8,128)(2,1)S(1)}, u32[]{:S(2)}, u32[]{:S(2)}) collective-permute-start(bf16[1,240,384]{2,1,0:T(8,128)(2,1)S(1)} %get-tuple-element.349), channel_id=1, source_target_pairs={{0,16},{1,17},{2,18},{3,19},{4,20},{5,21},{6,22},{7,23},{8,24},{9,... | collective-permute-start | bytes 552968 | tf_op jit(solution)/shard_map/ppermute | solution.py:63
  313.1 17.4 %collective-permute-start.26 = (bf16[1,240,384]{2,1,0:T(8,128)(2,1)S(1)}, bf16[1,240,384]{2,1,0:T(8,128)(2,1)S(1)}, u32[]{:S(2)}, u32[]{:S(2)}) collective-permute-start(bf16[1,240,384]{2,1,0:T(8,128)(2,1)S(1)} %get-tuple-element.347), channel_id=1, source_target_pairs={{0,16},{1,17},{2,18},{3,19},{4,20},{5,21},{6,22},{7,23},{8,24},{9,... | collective-permute-start | bytes 552968 | tf_op jit(solution)/shard_map/ppermute | solution.py:63
  313.5 17.4 %collective-permute-start.25 = (bf16[2,288,256]{2,1,0:T(8,128)(2,1)S(1)}, bf16[2,288,256]{2,1,0:T(8,128)(2,1)S(1)}, u32[]{:S(2)}, u32[]{:S(2)}) collective-permute-start(bf16[2,288,256]{2,1,0:T(8,128)(2,1)S(1)} %get-tuple-element.345.refs_0_), channel_id=1, source_target_pairs={{0,8},{1,9},{2,10},{3,11},{4,12},{5,13},{6,14},{7,15},{8,0},{9,1},... | collective-permute-start | bytes 884744 | tf_op jit(solution)/shard_map/ppermute | solution.py:63
  322.4 15.4 %collective-permute-start.24 = (bf16[2,224,384]{2,1,0:T(8,128)(2,1)S(1)}, bf16[2,224,384]{2,1,0:T(8,128)(2,1)S(1)}, u32[]{:S(2)}, u32[]{:S(2)}) collective-permute-start(bf16[2,224,384]{2,1,0:T(8,128)(2,1)S(1)} %get-tuple-element.344), channel_id=1, source_target_pairs={{0,8},{1,9},{2,10},{3,11},{4,12},{5,13},{6,14},{7,15},{8,0},{9,1},... | collective-permute-start | bytes 1032200 | tf_op jit(solution)/shard_map/ppermute | solution.py:63
  327.8 11.1 %collective-permute-start.31 = (bf16[1,240,384]{2,1,0:T(8,128)(2,1)S(1)}, bf16[1,240,384]{2,1,0:T(8,128)(2,1)S(1)}, u32[]{:S(2)}, u32[]{:S(2)}) collective-permute-start(bf16[1,240,384]{2,1,0:T(8,128)(2,1)S(1)} %get-tuple-element.358.refs_0_), channel_id=1, source_target_pairs={{0,16},{1,17},{2,18},{3,19},{4,20},{5,21},{6,22},{7,23},{8,24},{9,... | collective-permute-start | bytes 552968 | tf_op jit(solution)/shard_map/ppermute | solution.py:63
  330.5 11.8 %collective-permute-start.30 = (bf16[1,240,384]{2,1,0:T(8,128)(2,1)S(1)}, bf16[1,240,384]{2,1,0:T(8,128)(2,1)S(1)}, u32[]{:S(2)}, u32[]{:S(2)}) collective-permute-start(bf16[1,240,384]{2,1,0:T(8,128)(2,1)S(1)} %get-tuple-element.357.refs_0_), channel_id=1, source_target_pairs={{0,16},{1,17},{2,18},{3,19},{4,20},{5,21},{6,22},{7,23},{8,24},{9,... | collective-permute-start | bytes 552968 | tf_op jit(solution)/shard_map/ppermute | solution.py:63
  330.9 14.0 %collective-permute-start.29 = (bf16[4,288,256]{2,1,0:T(8,128)(2,1)S(1)}, bf16[4,288,256]{2,1,0:T(8,128)(2,1)S(1)}, u32[]{:S(2)}, u32[]{:S(2)}) collective-permute-start(bf16[4,288,256]{2,1,0:T(8,128)(2,1)S(1)} %get-tuple-element.356.refs_0_), channel_id=1, source_target_pairs={{0,2},{1,5},{2,0},{3,7},{4,6},{5,1},{6,4},{7,3},{8,10},{9,13},{10,... | collective-permute-start | bytes 1769480 | tf_op jit(solution)/shard_map/ppermute | solution.py:63
  337.9 8.3 %collective-permute-start.28 = (bf16[1,224,384]{2,1,0:T(8,128)(2,1)S(1)}, bf16[1,224,384]{2,1,0:T(8,128)(2,1)S(1)}, u32[]{:S(2)}, u32[]{:S(2)}) collective-permute-start(bf16[1,224,384]{2,1,0:T(8,128)(2,1)S(1)} %get-tuple-element.355), channel_id=1, source_target_pairs={{0,16},{1,17},{2,18},{3,19},{4,20},{5,21},{6,22},{7,23},{8,24},{9,... | collective-permute-start | bytes 516104 | tf_op jit(solution)/shard_map/ppermute | solution.py:63
  338.9 10.7 %collective-permute-start.34 = (bf16[2,240,384]{2,1,0:T(8,128)(2,1)S(1)}, bf16[2,240,384]{2,1,0:T(8,128)(2,1)S(1)}, u32[]{:S(2)}, u32[]{:S(2)}) collective-permute-start(bf16[2,240,384]{2,1,0:T(8,128)(2,1)S(1)} %get-tuple-element.365.refs_0_), channel_id=1, source_target_pairs={{0,4},{1,3},{2,6},{3,1},{4,0},{5,7},{6,2},{7,5},{8,12},{9,11},{10,... | collective-permute-start | bytes 1105928 | tf_op jit(solution)/shard_map/ppermute | solution.py:63
  342.4 8.4 %collective-permute-start.33 = (bf16[2,240,384]{2,1,0:T(8,128)(2,1)S(1)}, bf16[2,240,384]{2,1,0:T(8,128)(2,1)S(1)}, u32[]{:S(2)}, u32[]{:S(2)}) collective-permute-start(bf16[2,240,384]{2,1,0:T(8,128)(2,1)S(1)} %get-tuple-element.364.refs_0_), channel_id=1, source_target_pairs={{0,8},{1,5},{2,10},{3,7},{4,12},{5,1},{6,14},{7,3},{8,0},{9,13},{1... | collective-permute-start | bytes 1105928 | tf_op jit(solution)/shard_map/ppermute | solution.py:63
  345.0 23.4 %collective-permute-start.38 = (bf16[8,288,256]{2,1,0:T(8,128)(2,1)S(1)}, bf16[8,288,256]{2,1,0:T(8,128)(2,1)S(1)}, u32[]{:S(2)}, u32[]{:S(2)}) collective-permute-start(bf16[8,288,256]{2,1,0:T(8,128)(2,1)S(1)} %get-tuple-element.372.refs_1_), channel_id=1, source_target_pairs={{0,1},{1,0},{2,3},{3,2},{4,5},{5,4},{6,7},{7,6},{8,9},{9,8},{10,11... | collective-permute-start | bytes 3538952 | tf_op jit(solution)/shard_map/ppermute | solution.py:48
  345.1 16.3 %collective-permute-start.40 = (bf16[8,288,256]{2,1,0:T(8,128)(2,1)S(1)}, bf16[8,288,256]{2,1,0:T(8,128)(2,1)S(1)}, u32[]{:S(2)}, u32[]{:S(2)}) collective-permute-start(bf16[8,288,256]{2,1,0:T(8,128)(2,1)S(1)} %get-tuple-element.372.refs_1_), channel_id=1, source_target_pairs={{0,4},{1,3},{2,6},{3,1},{4,0},{5,7},{6,2},{7,5},{8,12},{9,11},{10,... | collective-permute-start | bytes 3538952 | tf_op jit(solution)/shard_map/ppermute | solution.py:63
  346.2 11.5 %collective-permute-start.32 = (bf16[1,224,384]{2,1,0:T(8,128)(2,1)S(1)}, bf16[1,224,384]{2,1,0:T(8,128)(2,1)S(1)}, u32[]{:S(2)}, u32[]{:S(2)}) collective-permute-start(bf16[1,224,384]{2,1,0:T(8,128)(2,1)S(1)} %get-tuple-element.363.refs_0_), channel_id=1, source_target_pairs={{0,16},{1,17},{2,18},{3,19},{4,20},{5,21},{6,22},{7,23},{8,24},{9,... | collective-permute-start | bytes 516104 | tf_op jit(solution)/shard_map/ppermute | solution.py:63
  349.7 21.8 %collective-permute-start.37 = (bf16[4,240,384]{2,1,0:T(8,128)(2,1)S(1)}, bf16[4,240,384]{2,1,0:T(8,128)(2,1)S(1)}, u32[]{:S(2)}, u32[]{:S(2)}) collective-permute-start(bf16[4,240,384]{2,1,0:T(8,128)(2,1)S(1)} %get-tuple-element.371.refs_0_), channel_id=1, source_target_pairs={{0,2},{1,9},{2,0},{3,11},{4,6},{5,13},{6,4},{7,15},{8,10},{9,1},{1... | collective-permute-start | bytes 2211848 | tf_op jit(solution)/shard_map/ppermute | solution.py:63
  350.8 25.8 %collective-permute-start.36 = (bf16[4,240,384]{2,1,0:T(8,128)(2,1)S(1)}, bf16[4,240,384]{2,1,0:T(8,128)(2,1)S(1)}, u32[]{:S(2)}, u32[]{:S(2)}) collective-permute-start(bf16[4,240,384]{2,1,0:T(8,128)(2,1)S(1)} %get-tuple-element.370.refs_0_), channel_id=1, source_target_pairs={{0,2},{1,9},{2,0},{3,11},{4,6},{5,13},{6,4},{7,15},{8,10},{9,1},{1... | collective-permute-start | bytes 2211848 | tf_op jit(solution)/shard_map/ppermute | solution.py:63
  357.7 19.1 %collective-permute-start.35 = (bf16[2,224,384]{2,1,0:T(8,128)(2,1)S(1)}, bf16[2,224,384]{2,1,0:T(8,128)(2,1)S(1)}, u32[]{:S(2)}, u32[]{:S(2)}) collective-permute-start(bf16[2,224,384]{2,1,0:T(8,128)(2,1)S(1)} %get-tuple-element.369.refs_0_), channel_id=1, source_target_pairs={{0,8},{1,9},{2,10},{3,11},{4,12},{5,13},{6,14},{7,15},{8,0},{9,1},... | collective-permute-start | bytes 1032200 | tf_op jit(solution)/shard_map/ppermute | solution.py:63
  361.4 17.0 %collective-permute-start.41 = (bf16[8,288,256]{2,1,0:T(8,128)(2,1)S(1)}, bf16[8,288,256]{2,1,0:T(8,128)(2,1)S(1)}, u32[]{:S(2)}, u32[]{:S(2)}) collective-permute-start(bf16[8,288,256]{2,1,0:T(8,128)(2,1)S(1)} %collective-permute-done.40.refs_1_), channel_id=1, source_target_pairs={{0,1},{1,0},{2,3},{3,2},{4,5},{5,4},{6,7},{7,6},{8,9},{9,8},{10,11... | collective-permute-start | bytes 3538952 | tf_op jit(solution)/shard_map/ppermute | solution.py:48
  376.8 11.0 %collective-permute-start.39 = (bf16[4,224,384]{2,1,0:T(8,128)(2,1)S(1)}, bf16[4,224,384]{2,1,0:T(8,128)(2,1)S(1)}, u32[]{:S(2)}, u32[]{:S(2)}) collective-permute-start(bf16[4,224,384]{2,1,0:T(8,128)(2,1)S(1)} %get-tuple-element.377.refs_0_), channel_id=1, source_target_pairs={{0,4},{1,3},{2,6},{3,1},{4,0},{5,7},{6,2},{7,5},{8,12},{9,11},{10,... | collective-permute-start | bytes 2064392 | tf_op jit(solution)/shard_map/ppermute | solution.py:63
  377.9 13.6 %collective-permute-start.47 = (bf16[8,240,384]{2,1,0:T(8,128)(2,1)S(1)}, bf16[8,240,384]{2,1,0:T(8,128)(2,1)S(1)}, u32[]{:S(2)}, u32[]{:S(2)}) collective-permute-start(bf16[8,240,384]{2,1,0:T(8,128)(2,1)S(1)} %get-tuple-element.385.refs_1_), channel_id=1, source_target_pairs={{0,1},{1,0},{2,3},{3,2},{4,5},{5,4},{6,7},{7,6},{8,9},{9,8},{10,11... | collective-permute-start | bytes 4423688 | tf_op jit(solution)/shard_map/ppermute | solution.py:48
  378.3 17.8 %collective-permute-start.46 = (bf16[8,240,384]{2,1,0:T(8,128)(2,1)S(1)}, bf16[8,240,384]{2,1,0:T(8,128)(2,1)S(1)}, u32[]{:S(2)}, u32[]{:S(2)}) collective-permute-start(bf16[8,240,384]{2,1,0:T(8,128)(2,1)S(1)} %get-tuple-element.384.refs_1_), channel_id=1, source_target_pairs={{0,1},{1,0},{2,3},{3,2},{4,5},{5,4},{6,7},{7,6},{8,9},{9,8},{10,11... | collective-permute-start | bytes 4423688 | tf_op jit(solution)/shard_map/ppermute | solution.py:48
  388.0 11.4 %collective-permute-start.45 = (bf16[8,224,384]{2,1,0:T(8,128)(2,1)S(1)}, bf16[8,224,384]{2,1,0:T(8,128)(2,1)S(1)}, u32[]{:S(2)}, u32[]{:S(2)}) collective-permute-start(bf16[8,224,384]{2,1,0:T(8,128)(2,1)S(1)} %get-tuple-element.383.refs_1_), channel_id=1, source_target_pairs={{0,1},{1,0},{2,3},{3,2},{4,5},{5,4},{6,7},{7,6},{8,9},{9,8},{10,11... | collective-permute-start | bytes 4128776 | tf_op jit(solution)/shard_map/ppermute | solution.py:48
  388.1 19.9 %collective-permute-start.44 = (bf16[8,240,384]{2,1,0:T(8,128)(2,1)S(1)}, bf16[8,240,384]{2,1,0:T(8,128)(2,1)S(1)}, u32[]{:S(2)}, u32[]{:S(2)}) collective-permute-start(bf16[8,240,384]{2,1,0:T(8,128)(2,1)S(1)} %get-tuple-element.385.refs_1_), channel_id=1, source_target_pairs={{0,8},{1,5},{2,10},{3,7},{4,12},{5,1},{6,14},{7,3},{8,0},{9,13},{1... | collective-permute-start | bytes 4423688 | tf_op jit(solution)/shard_map/ppermute | solution.py:63
  390.7 35.2 %collective-permute-start.43 = (bf16[8,240,384]{2,1,0:T(8,128)(2,1)S(1)}, bf16[8,240,384]{2,1,0:T(8,128)(2,1)S(1)}, u32[]{:S(2)}, u32[]{:S(2)}) collective-permute-start(bf16[8,240,384]{2,1,0:T(8,128)(2,1)S(1)} %get-tuple-element.384.refs_1_), channel_id=1, source_target_pairs={{0,4},{1,3},{2,6},{3,1},{4,0},{5,7},{6,2},{7,5},{8,12},{9,11},{10,... | collective-permute-start | bytes 4423688 | tf_op jit(solution)/shard_map/ppermute | solution.py:63
  391.5 34.7 %collective-permute-start.42 = (bf16[8,224,384]{2,1,0:T(8,128)(2,1)S(1)}, bf16[8,224,384]{2,1,0:T(8,128)(2,1)S(1)}, u32[]{:S(2)}, u32[]{:S(2)}) collective-permute-start(bf16[8,224,384]{2,1,0:T(8,128)(2,1)S(1)} %get-tuple-element.383.refs_1_), channel_id=1, source_target_pairs={{0,2},{1,5},{2,0},{3,7},{4,6},{5,1},{6,4},{7,3},{8,10},{9,13},{10,... | collective-permute-start | bytes 4128776 | tf_op jit(solution)/shard_map/ppermute | solution.py:63
  408.2 29.3 %collective-permute-start.50 = (bf16[8,240,384]{2,1,0:T(8,128)(2,1)S(1)}, bf16[8,240,384]{2,1,0:T(8,128)(2,1)S(1)}, u32[]{:S(2)}, u32[]{:S(2)}) collective-permute-start(bf16[8,240,384]{2,1,0:T(8,128)(2,1)S(1)} %get-tuple-element.399.refs_1_), channel_id=1, source_target_pairs={{0,1},{1,0},{2,3},{3,2},{4,5},{5,4},{6,7},{7,6},{8,9},{9,8},{10,11... | collective-permute-start | bytes 4423688 | tf_op jit(solution)/shard_map/ppermute | solution.py:48
  426.0 14.8 %collective-permute-start.49 = (bf16[8,240,384]{2,1,0:T(8,128)(2,1)S(1)}, bf16[8,240,384]{2,1,0:T(8,128)(2,1)S(1)}, u32[]{:S(2)}, u32[]{:S(2)}) collective-permute-start(bf16[8,240,384]{2,1,0:T(8,128)(2,1)S(1)} %get-tuple-element.396.refs_1_), channel_id=1, source_target_pairs={{0,1},{1,0},{2,3},{3,2},{4,5},{5,4},{6,7},{7,6},{8,9},{9,8},{10,11... | collective-permute-start | bytes 4423688 | tf_op jit(solution)/shard_map/ppermute | solution.py:48
  426.3 17.8 %collective-permute-start.48 = (bf16[8,224,384]{2,1,0:T(8,128)(2,1)S(1)}, bf16[8,224,384]{2,1,0:T(8,128)(2,1)S(1)}, u32[]{:S(2)}, u32[]{:S(2)}) collective-permute-start(bf16[8,224,384]{2,1,0:T(8,128)(2,1)S(1)} %get-tuple-element.392.refs_1_), channel_id=1, source_target_pairs={{0,1},{1,0},{2,3},{3,2},{4,5},{5,4},{6,7},{7,6},{8,9},{9,8},{10,11... | collective-permute-start | bytes 4128776 | tf_op jit(solution)/shard_map/ppermute | solution.py:48
  (73 other events, 439.8 us)
